TPU v7x, 128 devices: a whole 4x4x4 slice. The times are simulated.
128 devices in a mesh: cfg: 8 (over y_hi, z), mode: 16 (over y_lo, x, core).
Axes of the slice: x: 4, y: 4 (y_hi: 2, y_lo: 2; y = y_hi * 2 + y_lo), z: 4, core: 2. Of those that a mesh axis runs over, the one named last changes fastest.
Arguments:
- coords: bfloat16 [10368, 4096], P('mode', 'cfg'), may hold values from -6 to 6
- curvature: float32 [10368], P('mode'), may hold values from 0.2 to 5
- weight: float32 [10368], P('mode'), may hold values from 0.3 to 3
- polar: bfloat16 [10368, 10368], P('mode'), may hold values from -0.078125 to 0.078125
- forces: bfloat16 [10368, 4096], P('mode', 'cfg'), may hold values from -6 to 6
Outputs:
- gradient: float32 [10368, 10368], P('cfg', 'mode')
All inputs are finite; a program needn't handle non-finite values.
Results may differ from a plain program's by a relative error of at most 0.019.
Values may be sent and summed in bfloat16 or wider, within the bound.
No kernel may reach another device: no remote copies, remote signals or barrier semaphores. Data moves between devices by JAX's collectives and lax.ppermute only.
A program may use at most 128 MiB of HBM per device.

v0:
```python
import math

import jax
import jax.numpy as jnp
from jax import lax
from jax.sharding import PartitionSpec as P


def on_device(coords, curvature, weight, polar, forces):
    f32 = jnp.float32
    bf16 = jnp.bfloat16
    configs_dev = coords.shape[1]
    scaled = (coords.astype(f32) * curvature[:, None]).astype(bf16)
    weighted = (coords.astype(f32) * weight[:, None]).astype(bf16)
    contract = (((0,), (0,)), ((), ()))
    shares = lax.psum_scatter(
        lax.dot_general(polar, scaled, contract, preferred_element_type=f32).astype(jnp.bfloat16),
        "mode",
        scatter_dimension=0,
        tiled=True,
    ).astype(jnp.float32)
    resid_rows = (forces.astype(f32) + shares).astype(bf16)
    residual = lax.all_gather(resid_rows, "mode", axis=0, tiled=True)
    factor = 1.0 / math.sqrt(configs_dev * lax.axis_size("cfg"))
    across = (((1,), (1,)), ((), ()))
    return lax.psum_scatter(
        (lax.dot_general(residual, weighted, across, preferred_element_type=f32) * factor).astype(
            jnp.bfloat16
        ),
        "cfg",
        scatter_dimension=0,
        tiled=True,
    ).astype(jnp.float32)


def solution(mesh):
    placed = (P("mode", "cfg"), P("mode"), P("mode"), P("mode", None), P("mode", "cfg"))
    return jax.shard_map(
        on_device, mesh=mesh, in_specs=placed, out_specs=P("cfg", "mode"), check_vma=False
    )
```

profile of v0, /device:TPU:1, one launch (start us, length us, event | category | flops | bytes accessed | tf_op | source)
XLA Modules:
  0.0 412.7 jit_solution(17242804093088327751)
XLA Ops:
  6.5 0.0 reduce-scatter.5.cloned.1.call-start
  6.5 20.2 %fusion = bf16[10368,512]{1,0:T(8,128)(2,1)} fusion(bf16[648,10368]{1,0:T(8,128)(2,1)} %param.8, bf16[648,512]{1,0:T(8,128)(2,1)} %param.5, f32[648]{0:T(1024)} %param.6), kind=kOutput, calls=%fused_computation.2 | convolution fusion | flops 6886010880 | bytes 24719904 | tf_op jit(solution)/shard_map/dot_general | solution.py:17
  26.7 0.0 copy-start
  26.7 0.0 copy-start.1
  26.7 0.0 copy-start.2
  26.7 0.0 reduce-scatter.5.cloned.1.call-update
  26.8 0.0 all-gather.2.cloned.1.call-start
  26.8 79.0 %reduce-scatter.5.cloned.1.call-done = bf16[648,512]{1,0:T(8,128)(2,1)} async-done(((bf16[10368,512]{1,0:T(8,128)(2,1)}), bf16[648,512]{1,0:T(8,128)(2,1)}) %reduce-scatter.5.cloned.1.call-update) | async-done | bytes 663568 | tf_op jit(solution)/shard_map/reduce_scatter | solution.py:16
  105.8 0.0 copy-done
  105.8 2.1 add_convert_fusion
  107.9 0.0 all-gather.2.cloned.1.call-update
  107.9 0.0 reduce-scatter.7.cloned.1.call-start
  108.0 65.0 %all-gather.2.cloned.1.call-done = bf16[10368,512]{1,0:T(8,128)(2,1)} async-done(((bf16[648,512]{1,0:T(8,128)(2,1)}), bf16[10368,512]{1,0:T(8,128)(2,1)}) %all-gather.2.cloned.1.call-update) | async-done | bytes 10616848 | tf_op jit(solution)/shard_map/all_gather | solution.py:23
  173.0 0.0 copy-done.1
  173.0 0.0 copy-done.2
  173.0 16.5 %multiply_convert_fusion = bf16[10368,648]{0,1:T(8,128)(2,1)} fusion(bf16[10368,512]{1,0:T(8,128)(2,1)} %all-gather.2.cloned.1.call-done, bf16[648,512]{1,0:T(8,128)(2,1)S(1)} %copy-done.1, f32[648]{0:T(1024)S(1)} %copy-done.2), kind=kOutput, calls=%fused_computation | convolution fusion | flops 6894139392 | bytes 24719904 | tf_op jit(solution)/shard_map/dot_general | solution.py:27
  189.5 19.1 %copy.6 = bf16[10368,648]{1,0:T(8,128)(2,1)} copy(bf16[10368,648]{0,1:T(8,128)(2,1)} %multiply_convert_fusion) | data formatting | bytes 26873856
  208.5 0.0 reduce-scatter.7.cloned.1.call-update
  208.5 192.6 %reduce-scatter.7.cloned.1.call-done = bf16[1296,648]{1,0:T(8,128)(2,1)} async-done(((bf16[10368,648]{1,0:T(8,128)(2,1)}), bf16[1296,648]{1,0:T(8,128)(2,1)}) %reduce-scatter.7.cloned.1.call-update) | async-done | bytes 1679632
  401.1 3.0 copy.7
  404.1 2.1 convert_element_type.40
Async XLA Ops:
  6.5 99.2 %reduce-scatter.5.cloned.1.call-start = ((), (), s32[]{:S(2)}) async-start(), calls=%async_computation.2 | async-start | bytes 11280384 | tf_op jit(solution)/shard_map/reduce_scatter | solution.py:16
  26.7 79.0 %copy-start = (bf16[648,512]{1,0:T(8,128)(2,1)S(1)}, bf16[648,512]{1,0:T(8,128)(2,1)}, u32[]{:S(2)}) copy-start(bf16[648,512]{1,0:T(8,128)(2,1)} %param.9) | copy-start | bytes 1990660
  26.7 146.3 %copy-start.1 = (bf16[648,512]{1,0:T(8,128)(2,1)S(1)}, bf16[648,512]{1,0:T(8,128)(2,1)}, u32[]{:S(2)}) copy-start(bf16[648,512]{1,0:T(8,128)(2,1)} %param.5) | copy-start | bytes 1990660
  26.7 146.3 %copy-start.2 = (f32[648]{0:T(1024)S(1)}, f32[648]{0:T(1024)}, u32[]{:S(2)}) copy-start(f32[648]{0:T(1024)} %param.7) | copy-start | bytes 7780
  26.8 146.2 %all-gather.2.cloned.1.call-start = ((), (), s32[]{:S(2)}) async-start(), calls=%async_computation.3 | async-start | bytes 11280384 | tf_op jit(solution)/shard_map/all_gather | solution.py:23
  107.9 293.2 %reduce-scatter.7.cloned.1.call-start = ((), (), s32[]{:S(2)}) async-start(), calls=%async_computation.4 | async-start | bytes 17915904
Sparse Core Ops, SparseCore 0:
  26.9 78.8 reduce-scatter.4
  108.0 64.9 all-gather.1
  208.7 192.3 reduce-scatter.6
where the time goes:
time: 416 us; the launch traced here: 413 us
  waiting for transfers between devices  337 us (81%)
  matrix products  36.7 us (9%)
  local copies, waits for them, and re-layouts  22.1 us (5%)
  between operations  13.1 us (3%)
  other arithmetic  4.2 us (1%)
    unnamed x4, waiting for transfers between devices  193 us
    reduce_scatter x1, waiting for transfers between devices, on_device(): lax.psum_scatter(lax.dot_general(polar, scaled, contract, preferred_eleme...  79 us
    all_gather x1, waiting for transfers between devices, on_device(): residual = lax.all_gather(resid_rows, 'mode', axis=0, tiled=True)  65 us
    unnamed x8, local copies, waits for them, and re-layouts  22.1 us
    dot_general x1, matrix products, on_device(): lax.dot_general(polar, scaled, contract, preferred_element_type=f32)  20.2 us
    dot_general x1, matrix products, on_device(): lax.dot_general(residual, weighted, across, preferred_element_type=f32)  16.5 us
  transfers between devices with their start and end apart: 3, of which 3 were waited for; matrix products, arithmetic and copies ran while one was open for 0% of the time, Pallas kernels for 0%

commit v1 on v0

v1 whole, which is shorter than its diff:
```python
import math

import jax
import jax.numpy as jnp
from jax import lax
from jax.experimental import pallas as pl
from jax.experimental.pallas import tpu as pltpu
from jax.sharding import PartitionSpec as P

F32 = jnp.float32
BF16 = jnp.bfloat16
X, Z = 4, 4
Q = 128
CHUNKS = (((0, 0),), ((0, 3), (0, 1)), ((1, 0), (1, 3), (1, 1)), ((0, 2), (1, 2)))


def mode_perm(fn):
    out = []
    for j in range(16):
        yl, x, k = j // 8, (j // 2) % 4, j % 2
        a, b, c = fn(yl, x, k)
        out.append((j, (a * 4 + b) * 2 + c))
    return out


FIRST = mode_perm(lambda yl, x, k: (yl, x ^ (3 if k else 1), k))
SECOND = mode_perm(lambda yl, x, k: (yl, x ^ (1 if k else 3), k))
YSWAP = mode_perm(lambda yl, x, k: (1 - yl, x, k))
KSWAP = mode_perm(lambda yl, x, k: (yl, x, 1 - k))


def cfg_perm(dy, dz):
    return [(c, (c // 4 ^ dy) * 4 + (c % 4 + dz) % 4) for c in range(8)]


TRANSPOSE = [(i * 16 + J * 2 + k, J * 16 + i * 2 + k) for i in range(8) for J in range(8) for k in range(2)]


def reorder(v):
    return jnp.concatenate([v[:, :Q], v[:, 2 * Q : 3 * Q], v[:, Q : 2 * Q], v[:, 3 * Q :]], axis=1)


def mm1_body(n, flags, po, px, f, *refs):
    units, (keep, s2, s1) = refs[: 2 * n], refs[2 * n :]
    for u in range(n):
        co, cx = units[2 * u], units[2 * u + 1]
        h = jnp.dot(po[...], co[...], preferred_element_type=F32)
        h += jnp.dot(px[...], reorder(cx[...]), preferred_element_type=F32)
        h += f[...].astype(F32) * flags[u].astype(F32)
        h = h.astype(BF16)
        a = slice(u * Q, (u + 1) * Q)
        b = slice((n + u) * Q, (n + u + 1) * Q)
        keep[:, a] = h[:, :Q]
        s2[:, a] = h[:, Q : 2 * Q]
        s1[:, a] = h[:, 2 * Q : 3 * Q]
        s1[:, b] = h[:, 3 * Q :]


VM = pl.BlockSpec(memory_space=pltpu.VMEM)
SM = pl.BlockSpec(memory_space=pltpu.SMEM)
PARAMS = pltpu.CompilerParams(vmem_limit_bytes=48 * 1024 * 1024)


def mm1(flags, po, px, f, units):
    n = len(units)
    rows = po.shape[0]
    depth = po.shape[1] * 2
    flat = [v for u in units for v in u]
    return pl.pallas_call(
        lambda *r: mm1_body(n, *r),
        out_shape=[jax.ShapeDtypeStruct((rows, w * n * Q), BF16) for w in (1, 1, 2)],
        in_specs=[SM] + [VM] * (3 + 2 * n),
        out_specs=[VM] * 3,
        compiler_params=PARAMS,
        cost_estimate=pl.CostEstimate(
            flops=2 * rows * depth * 4 * Q * n, bytes_accessed=2 * rows * (depth + Q * 12 * n), transcendentals=0
        ),
        name="mm1",
    )(flags, po, px, f, *flat)


def mm2_body(n, first, swap, *refs):
    refs = list(refs)
    acc = None if first else refs.pop(0)
    r, units, out = refs[:4], refs[4 : 4 + n], refs[4 + n]
    total = None if first else acc[...]
    for u in range(n):
        a = slice(u * Q, (u + 1) * Q)
        order = (0, 2, 1, 3) if swap else (0, 1, 2, 3)
        ru = jnp.concatenate([r[s][:, a] for s in order], axis=1)
        t = lax.dot_general(ru, units[u][...], (((1,), (1,)), ((), ())), preferred_element_type=F32)
        total = t if total is None else total + t
    out[...] = total.astype(out.dtype)


def mm2(acc, r, units, swap, dtype=F32):
    n = len(units)
    rows, cols = r[0].shape[0], units[0].shape[0]
    first = acc is None
    args = ([] if first else [acc]) + list(r) + list(units)
    return pl.pallas_call(
        lambda *a: mm2_body(n, first, swap, *a),
        out_shape=jax.ShapeDtypeStruct((rows, cols), dtype),
        in_specs=[VM] * len(args),
        out_specs=VM,
        compiler_params=PARAMS,
        cost_estimate=pl.CostEstimate(
            flops=2 * rows * cols * 4 * Q * n, bytes_accessed=8 * rows * cols + 2 * rows * Q * 8 * n, transcendentals=0
        ),
        name="mm2",
    )(*args)


def on_device(coords, curvature, weight, polar, forces):
    i, j = lax.axis_index("cfg"), lax.axis_index("mode")
    yh, z = i // Z, i % Z
    k, x, chip = j % 2, (j // 2) % X, j // 2
    rows = coords.shape[0]

    second, first = jnp.where(k == 0, 3, 1), jnp.where(k == 0, 1, 3)
    order = [x, x ^ second, x ^ first, x ^ 2]

    def mine(v):
        return jnp.concatenate([lax.dynamic_slice_in_dim(v, o * Q, Q, axis=1) for o in order], axis=1)

    def half(which):
        part = lax.dynamic_slice_in_dim(polar, (2 * i + which) * rows, rows, axis=1)
        return (part.astype(F32) * curvature[:, None]).astype(BF16).T

    px = lax.ppermute(half(1 - k), "mode", KSWAP)
    po = half(k)

    unit = {}
    unit[0, 0] = mine(coords)
    unit[1, 0] = lax.ppermute(unit[0, 0], "cfg", cfg_perm(1, 0))
    for dz in (3, 1, 2):
        unit[0, dz] = lax.ppermute(unit[0, 0], "cfg", cfg_perm(0, -dz))
    for dz in (3, 1, 2):
        unit[1, dz] = lax.ppermute(unit[1, 0], "cfg", cfg_perm(0, -dz))
    other = {u: lax.ppermute(v, "mode", KSWAP) for u, v in unit.items()}

    f_own = mine(forces)
    f_all = mine(lax.ppermute(forces, ("cfg", "mode"), TRANSPOSE))

    acc_own = acc_oth = None
    for number, chunk in enumerate(CHUNKS):
        n = len(chunk)
        flags = jnp.stack([((yh ^ dy) * Z + (z + dz) % Z == chip).astype(jnp.int32) for dy, dz in chunk])
        keep, s2, s1 = mm1(flags, po, px, f_own if number == 0 else f_all, [(unit[u], other[u]) for u in chunk])
        g1 = lax.ppermute(s1, "mode", FIRST)
        s2 = (s2.astype(F32) + g1[:, n * Q :].astype(F32)).astype(BF16)
        g2 = lax.ppermute(s2, "mode", SECOND)
        s3 = (keep.astype(F32) + g1[:, : n * Q].astype(F32) + g2.astype(F32)).astype(BF16)
        g3 = lax.ppermute(s3, "mode", YSWAP)
        r0 = (s3.astype(F32) + g3.astype(F32)).astype(BF16)
        r1 = lax.ppermute(r0, "mode", SECOND)
        r2 = lax.ppermute(r0, "mode", FIRST)
        r3 = lax.ppermute(r1, "mode", FIRST)
        r = (r0, r1, r2, r3)
        last = number == len(CHUNKS) - 1
        acc_oth = mm2(acc_oth, r, [other[u] for u in chunk], True, BF16 if last else F32)
        if last:
            got = lax.ppermute(acc_oth, "mode", KSWAP)
        acc_own = mm2(acc_own, r, [unit[u] for u in chunk], False)

    factor = weight[None, :] * (1.0 / math.sqrt(coords.shape[1] * lax.axis_size("cfg")))
    got = got.astype(F32)
    both = jnp.where(k == 0, jnp.concatenate([acc_own, got], axis=0), jnp.concatenate([got, acc_own], axis=0))
    return both * factor


def solution(mesh):
    placed = (P("mode", "cfg"), P("mode"), P("mode"), P("mode", None), P("mode", "cfg"))
    return jax.shard_map(
        on_device, mesh=mesh, in_specs=placed, out_specs=P("cfg", "mode"), check_vma=False
    )
```

time: 416 us -> 274 us (0.66)
  waiting for transfers between devices: 337 us -> 109 us
  starting transfers between devices: 0.09 us -> 104 us
  matrix products: 36.7 us -> 0 us
  Pallas kernels: 0 us -> 34.5 us
  between operations: 13.1 us -> 0.58 us
    unnamed x4 -> x0, waiting for transfers between devices: 193 us -> none
    ppermute x0 -> x42, waiting for transfers between devices: none -> 109 us  [the longest x3 38.2 us: on_device(): unit[1, dz] = lax.ppermute(unit[1, 0], 'cfg', cfg_perm(0, -dz))]
    ppermute x0 -> x42, starting transfers between devices: none -> 104 us  [the longest x1 50.9 us: on_device(): unit[1, 0] = lax.ppermute(unit[0, 0], 'cfg', cfg_perm(1, 0))]
    reduce_scatter x1 -> x0, waiting for transfers between devices: 79 us -> none  [on_device(): lax.psum_scatter(lax.dot_general(polar, scaled, contract, preferred_eleme...]
    all_gather x1 -> x0, waiting for transfers between devices: 65 us -> none  [on_device(): residual = lax.all_gather(resid_rows, 'mode', axis=0, tiled=True)]
    dot_general x2 -> x0, matrix products: 36.7 us -> none  [the longest x1 20.2 us: on_device(): lax.dot_general(polar, scaled, contract, preferred_element_type=f32)]
    pallas_call x0 -> x12, Pallas kernels: none -> 34.5 us  [the longest x8 18.9 us: mm2(): pl.pallas_call(lambda *a: mm2_body(n, first, swap, *a), out_shape=jax.Sha...]
    unnamed x8 -> x52, local copies, waits for them, and re-layouts: 22.1 us -> 8.02 us
  transfers between devices with their start and end apart: 3 -> 42, of which waited for: 3 -> 13; matrix products, arithmetic and copies ran while one was open for 0% -> 4% of each run, Pallas kernels for 0% -> 12%
where the time goes in v1:
time: 274 us; the launch traced here: 273 us
  waiting for transfers between devices  109 us (40%)
  starting transfers between devices  104 us (38%)
  Pallas kernels  34.5 us (13%)
  local copies, waits for them, and re-layouts  19.4 us (7%)
  other arithmetic  5.69 us (2%)
    ppermute x1, starting transfers between devices, on_device(): unit[1, 0] = lax.ppermute(unit[0, 0], 'cfg', cfg_perm(1, 0))  50.9 us
    ppermute x3, waiting for transfers between devices, on_device(): unit[1, dz] = lax.ppermute(unit[1, 0], 'cfg', cfg_perm(0, -dz))  38.2 us
    ppermute x4, waiting for transfers between devices, on_device(): g1 = lax.ppermute(s1, 'mode', FIRST)  27.7 us
    pallas_call x8, Pallas kernels, mm2(): pl.pallas_call(lambda *a: mm2_body(n, first, swap, *a), out_shape=jax.Sha...  18.9 us
    pallas_call x4, Pallas kernels, mm1(): pl.pallas_call(lambda *r: mm1_body(n, *r), out_shape=[jax.ShapeDtypeStruc...  15.6 us
    ppermute x4, waiting for transfers between devices, on_device(): g3 = lax.ppermute(s3, 'mode', YSWAP)  14.8 us
    ppermute x4, waiting for transfers between devices, on_device(): r3 = lax.ppermute(r1, 'mode', FIRST)  10 us
    ppermute x1, waiting for transfers between devices, on_device(): unit[1, 0] = lax.ppermute(unit[0, 0], 'cfg', cfg_perm(1, 0))  9.28 us
  transfers between devices with their start and end apart: 42, of which 13 were waited for; matrix products, arithmetic and copies ran while one was open for 4% of the time, Pallas kernels for 12%

profile of v1, /device:TPU:1, one launch (start us, length us, event | category | flops | bytes accessed | tf_op | source)
XLA Modules:
  0.0 272.7 jit_solution(12600456355668968069)
XLA Ops:
  0.0 6.7 %collective-permute-start.8 = (bf16[648,512]{1,0:T(8,128)(2,1)}, bf16[648,512]{1,0:T(8,128)(2,1)}, u32[]{:S(2)}, u32[]{:S(2)}) collective-permute-start(bf16[648,512]{1,0:T(8,128)(2,1)} %param.9), channel_id=1, source_target_pairs={{0,0},{1,1},{2,16},{3,17},{4,32},{5,33},{6,48},{7,49},{8,64},{9,65... | collective-permute-start | bytes 1990664 | tf_op jit(solution)/shard_map/ppermute | solution.py:143
  6.7 2.5 constant_dynamic-slice_fusion.12
  10.8 1.4 fusion.2
  12.1 1.4 collective-permute-start
  13.6 2.2 constant_dynamic-slice_fusion.3
  15.9 50.9 %collective-permute-start.19 = (bf16[648,512]{1,0:T(8,128)(2,1)S(1)}, bf16[648,512]{1,0:T(8,128)(2,1)}, u32[]{:S(2)}, u32[]{:S(2)}) collective-permute-start(bf16[648,512]{1,0:T(8,128)(2,1)S(1)} %pad_maximum_fusion.1.r_4_.a_4_), channel_id=1, source_target_pairs={{0,64},{16,80},{32,96},{48,112},{64,0},{80,16},{96,32},{112,48},{1... | collective-permute-start | bytes 1990664 | tf_op jit(solution)/shard_map/ppermute | solution.py:135
  66.8 1.8 collective-permute-start.1
  68.6 2.7 collective-permute-start.11
  71.3 9.3 %collective-permute-done.19.r_4_.a_5_ = bf16[648,512]{1,0:T(8,128)(2,1)} collective-permute-done((bf16[648,512]{1,0:T(8,128)(2,1)S(1)}, bf16[648,512]{1,0:T(8,128)(2,1)}, u32[]{:S(2)}, u32[]{:S(2)}) %collective-permute-start.19) | collective-permute-done | bytes 663584 | tf_op jit(solution)/shard_map/ppermute | solution.py:135
  80.6 2.7 collective-permute-start.23
  83.3 3.2 %collective-permute-done.9.r_4_.a_5_ = bf16[648,512]{1,0:T(8,128)(2,1)} collective-permute-done((bf16[648,512]{1,0:T(8,128)(2,1)S(1)}, bf16[648,512]{1,0:T(8,128)(2,1)}, u32[]{:S(2)}, u32[]{:S(2)}) %collective-permute-start.9) | collective-permute-done | bytes 663584 | tf_op jit(solution)/shard_map/ppermute | solution.py:137
  89.0 1.7 collective-permute-start.33
  90.7 38.2 %collective-permute-done.21.r_6_.a_6_ = bf16[648,512]{1,0:T(8,128)(2,1)} collective-permute-done((bf16[648,512]{1,0:T(8,128)(2,1)}, bf16[648,512]{1,0:T(8,128)(2,1)}, u32[]{:S(2)}, u32[]{:S(2)}) %collective-permute-start.21) | collective-permute-done | bytes 663584 | tf_op jit(solution)/shard_map/ppermute | solution.py:139
  131.2 2.9 %collective-permute-start.2 = (bf16[648,256]{1,0:T(8,128)(2,1)S(1)}, bf16[648,256]{1,0:T(8,128)(2,1)S(1)}, u32[]{:S(2)}, u32[]{:S(2)}) collective-permute-start(bf16[648,256]{1,0:T(8,128)(2,1)S(1)} %get-tuple-element.18), channel_id=1, source_target_pairs={{0,2},{1,7},{2,0},{3,5},{4,6},{5,3},{6,4},{7,1},{8,10},{9,15},{10,... | collective-permute-start | bytes 995336 | tf_op jit(solution)/shard_map/ppermute | solution.py:150
  134.3 4.3 %collective-permute-done.2 = bf16[648,256]{1,0:T(8,128)(2,1)S(1)} collective-permute-done((bf16[648,256]{1,0:T(8,128)(2,1)S(1)}, bf16[648,256]{1,0:T(8,128)(2,1)S(1)}, u32[]{:S(2)}, u32[]{:S(2)}) %collective-permute-start.2) | collective-permute-done | bytes 331808 | tf_op jit(solution)/shard_map/ppermute | solution.py:150
  139.6 3.1 %collective-permute-start.34 = (bf16[648,512]{1,0:T(8,128)(2,1)S(1)}, bf16[648,512]{1,0:T(8,128)(2,1)S(1)}, u32[]{:S(2)}, u32[]{:S(2)}) collective-permute-start(bf16[648,512]{1,0:T(8,128)(2,1)S(1)} %collective-permute-done.33.r_6_.a_6_), channel_id=1, source_target_pairs={{0,1},{1,0},{2,3},{3,2},{4,5},{5,4},{6,7},{7,6},{8,9},{9,8},{10,11... | collective-permute-start | bytes 1990664 | tf_op jit(solution)/shard_map/ppermute | solution.py:140
  142.7 6.4 %mm1.6 = (bf16[648,384]{1,0:T(8,128)(2,1)S(1)}, bf16[648,384]{1,0:T(8,128)(2,1)S(1)}, bf16[648,768]{1,0:T(8,128)(2,1)}) custom-call(s32[3]{0:T(128)S(1)} %add_convert_fusion.13.r_0_, bf16[648,648]{1,0:T(8,128)(2,1)} %copy-done.5, bf16[648,648]{1,0:T(8,128)(2,1)} %copy-done.7, bf16[648,512]{1,0:T(8,128)(2,1)S(1)} %pad_maximum_fusion.2.r_3_, ...), custom_call_target="tpu_custom_call" | custom-call | flops 2579890176 | bytes 7651584 | tf_op jit(solution)/shard_map/mm1/pallas_call | solution.py:69
  149.8 4.1 %mm1.5 = (bf16[648,256]{1,0:T(8,128)(2,1)S(1)}, bf16[648,256]{1,0:T(8,128)(2,1)S(1)}, bf16[648,512]{1,0:T(8,128)(2,1)S(1)}) custom-call(s32[2]{0:T(128)S(1)} %add_convert_fusion.12.r_0_, bf16[648,648]{1,0:T(8,128)(2,1)S(1)} %copy-done.6, bf16[648,648]{1,0:T(8,128)(2,1)} %copy-done.7, bf16[648,512]{1,0:T(8,128)(2,1)S(1)} %pad_maximum_fusion.2.r_3_, ...), custom_call_target="tpu_custom_call" | custom-call | flops 1719926784 | bytes 5660928 | tf_op jit(solution)/shard_map/mm1/pallas_call | solution.py:69
  153.9 2.7 collective-permute-start.13
  156.7 3.9 %mm1.7 = (bf16[648,256]{1,0:T(8,128)(2,1)S(1)}, bf16[648,256]{1,0:T(8,128)(2,1)S(1)}, bf16[648,512]{1,0:T(8,128)(2,1)S(1)}) custom-call(s32[2]{0:T(128)S(1)} %add_convert_fusion.14.r_0_, bf16[648,648]{1,0:T(8,128)(2,1)S(1)} %copy-done.6, bf16[648,648]{1,0:T(8,128)(2,1)} %copy-done.7, bf16[648,512]{1,0:T(8,128)(2,1)S(1)} %pad_maximum_fusion.2.r_3_, ...), custom_call_target="tpu_custom_call" | custom-call | flops 1719926784 | bytes 5660928 | tf_op jit(solution)/shard_map/mm1/pallas_call | solution.py:69
  160.7 1.4 collective-permute-start.35
  162.1 1.4 collective-permute-start.6
  163.4 1.3 collective-permute-start.7
  165.7 9.7 %collective-permute-done.13 = bf16[648,512]{1,0:T(8,128)(2,1)S(1)} collective-permute-done((bf16[648,512]{1,0:T(8,128)(2,1)S(1)}, bf16[648,512]{1,0:T(8,128)(2,1)S(1)}, u32[]{:S(2)}, u32[]{:S(2)}) %collective-permute-start.13) | collective-permute-done | bytes 663584 | tf_op jit(solution)/shard_map/ppermute | solution.py:150
  175.6 13.0 %collective-permute-done.35 = bf16[648,512]{1,0:T(8,128)(2,1)S(1)} collective-permute-done((bf16[648,512]{1,0:T(8,128)(2,1)S(1)}, bf16[648,512]{1,0:T(8,128)(2,1)S(1)}, u32[]{:S(2)}, u32[]{:S(2)}) %collective-permute-start.35) | collective-permute-done | bytes 663584 | tf_op jit(solution)/shard_map/ppermute | solution.py:150
  189.3 1.5 collective-permute-start.15
  190.8 4.7 %collective-permute-done.36 = bf16[648,256]{1,0:T(8,128)(2,1)S(1)} collective-permute-done((bf16[648,256]{1,0:T(8,128)(2,1)S(1)}, bf16[648,256]{1,0:T(8,128)(2,1)S(1)}, u32[]{:S(2)}, u32[]{:S(2)}) %collective-permute-start.36) | collective-permute-done | bytes 331808 | tf_op jit(solution)/shard_map/ppermute | solution.py:152
  195.7 5.8 %collective-permute-done.27 = bf16[648,384]{1,0:T(8,128)(2,1)S(1)} collective-permute-done((bf16[648,384]{1,0:T(8,128)(2,1)S(1)}, bf16[648,384]{1,0:T(8,128)(2,1)S(1)}, u32[]{:S(2)}, u32[]{:S(2)}) %collective-permute-start.27) | collective-permute-done | bytes 497696 | tf_op jit(solution)/shard_map/ppermute | solution.py:154
  201.7 2.5 collective-permute-start.28
  204.1 4.5 %collective-permute-done.15 = bf16[648,256]{1,0:T(8,128)(2,1)S(1)} collective-permute-done((bf16[648,256]{1,0:T(8,128)(2,1)S(1)}, bf16[648,256]{1,0:T(8,128)(2,1)S(1)}, u32[]{:S(2)}, u32[]{:S(2)}) %collective-permute-start.15) | collective-permute-done | bytes 331808 | tf_op jit(solution)/shard_map/ppermute | solution.py:154
  208.7 2.5 collective-permute-start.16
  211.2 4.5 %collective-permute-done.37 = bf16[648,256]{1,0:T(8,128)(2,1)S(1)} collective-permute-done((bf16[648,256]{1,0:T(8,128)(2,1)S(1)}, bf16[648,256]{1,0:T(8,128)(2,1)S(1)}, u32[]{:S(2)}, u32[]{:S(2)}) %collective-permute-start.37) | collective-permute-done | bytes 331808 | tf_op jit(solution)/shard_map/ppermute | solution.py:154
  215.9 2.4 collective-permute-start.38
  218.2 2.0 collective-permute-start.29
  220.9 2.0 collective-permute-start.18
  223.4 3.4 %collective-permute-start.39 = (bf16[648,256]{1,0:T(8,128)(2,1)S(1)}, bf16[648,256]{1,0:T(8,128)(2,1)S(1)}, u32[]{:S(2)}, u32[]{:S(2)}) collective-permute-start(bf16[648,256]{1,0:T(8,128)(2,1)S(1)} %add_convert_fusion.3.a_1_), channel_id=1, source_target_pairs={{0,2},{1,7},{2,0},{3,5},{4,6},{5,3},{6,4},{7,1},{8,10},{9,15},{10,... | collective-permute-start | bytes 995336 | tf_op jit(solution)/shard_map/ppermute | solution.py:157
  226.8 1.8 collective-permute-start.40
  229.4 1.3 copy-done.1
  230.7 10.0 %collective-permute-done.18.a_4_ = bf16[648,256]{1,0:T(8,128)(2,1)S(1)} collective-permute-done((bf16[648,256]{1,0:T(8,128)(2,1)S(1)}, bf16[648,256]{1,0:T(8,128)(2,1)S(1)}, u32[]{:S(2)}, u32[]{:S(2)}) %collective-permute-start.18) | collective-permute-done | bytes 331808 | tf_op jit(solution)/shard_map/ppermute | solution.py:158
  240.7 2.8 %mm2.13.a_0_ = f32[648,648]{1,0:T(8,128)S(1)} custom-call(f32[648,648]{1,0:T(8,128)} %copy-done.1, bf16[648,256]{1,0:T(8,128)(2,1)S(1)} %add_convert_fusion.6.a_1_, bf16[648,256]{1,0:T(8,128)(2,1)S(1)} %collective-permute-done.16.a_2_, bf16[648,256]{1,0:T(8,128)(2,1)S(1)} %collective-permute-done.17.a_3_, bf16[648,256]{1,0:T(8,128)(2,1)S(1)} %collective-permute-done.18.a_4_, ...), custom_call_target="tpu_custom_call" | custom-call | flops 859963392 | bytes 6013440 | tf_op jit(solution)/shard_map/mm2/pallas_call | solution.py:101
  243.5 1.3 copy-done.4
  244.8 3.4 %mm2.14.a_0_ = f32[648,648]{1,0:T(8,128)S(1)} custom-call(f32[648,648]{1,0:T(8,128)} %copy-done.4, bf16[648,384]{1,0:T(8,128)(2,1)S(1)} %add_convert_fusion.a_1_, bf16[648,384]{1,0:T(8,128)(2,1)S(1)} %collective-permute-done.28.a_2_, bf16[648,384]{1,0:T(8,128)(2,1)S(1)} %collective-permute-done.29.a_3_, bf16[648,384]{1,0:T(8,128)(2,1)S(1)} %collective-permute-done.30.a_4_, ...), custom_call_target="tpu_custom_call" | custom-call | flops 1289945088 | bytes 7340544 | tf_op jit(solution)/shard_map/mm2/pallas_call | solution.py:101
  250.9 1.3 copy-done
  252.2 3.1 %mm2.9.a_0_ = f32[648,648]{1,0:T(8,128)S(1)} custom-call(f32[648,648]{1,0:T(8,128)} %copy-done, bf16[648,256]{1,0:T(8,128)(2,1)S(1)} %add_convert_fusion.6.a_1_, bf16[648,256]{1,0:T(8,128)(2,1)S(1)} %collective-permute-done.16.a_2_, bf16[648,256]{1,0:T(8,128)(2,1)S(1)} %collective-permute-done.17.a_3_, bf16[648,256]{1,0:T(8,128)(2,1)S(1)} %collective-permute-done.18.a_4_, ...), custom_call_target="tpu_custom_call" | custom-call | flops 859963392 | bytes 6013440 | tf_op jit(solution)/shard_map/mm2/pallas_call | solution.py:101
  256.6 3.9 %mm2.10.a_0_ = f32[648,648]{1,0:T(8,128)S(1)} custom-call(f32[648,648]{1,0:T(8,128)} %copy-done.2, bf16[648,384]{1,0:T(8,128)(2,1)S(1)} %add_convert_fusion.a_1_, bf16[648,384]{1,0:T(8,128)(2,1)S(1)} %collective-permute-done.28.a_2_, bf16[648,384]{1,0:T(8,128)(2,1)S(1)} %collective-permute-done.29.a_3_, bf16[648,384]{1,0:T(8,128)(2,1)S(1)} %collective-permute-done.30.a_4_, ...), custom_call_target="tpu_custom_call" | custom-call | flops 1289945088 | bytes 7340544 | tf_op jit(solution)/shard_map/mm2/pallas_call | solution.py:101
  261.8 2.9 %mm2.11 = f32[648,648]{1,0:T(8,128)S(1)} custom-call(f32[648,648]{1,0:T(8,128)} %copy-done.3, bf16[648,256]{1,0:T(8,128)(2,1)S(1)} %add_convert_fusion.3.a_1_, bf16[648,256]{1,0:T(8,128)(2,1)S(1)} %collective-permute-done.38.a_2_, bf16[648,256]{1,0:T(8,128)(2,1)S(1)} %collective-permute-done.39.a_3_, bf16[648,256]{1,0:T(8,128)(2,1)S(1)} %collective-permute-done.40.a_4_, ...), custom_call_target="tpu_custom_call" | custom-call | flops 859963392 | bytes 6013440 | tf_op jit(solution)/shard_map/mm2/pallas_call | solution.py:101
  264.9 2.4 fusion
  267.3 5.4 %copy.12 = f32[1296,648]{0,1:T(8,128)} copy(f32[1296,648]{1,0:T(8,128)} %fusion) | data formatting | bytes 6718464 | tf_op jit(solution)/shard_map/mul | solution.py:169
  (126 shorter events, 17.8 us)
Async XLA Ops:
  0.0 13.6 %collective-permute-start.8 = (bf16[648,512]{1,0:T(8,128)(2,1)}, bf16[648,512]{1,0:T(8,128)(2,1)}, u32[]{:S(2)}, u32[]{:S(2)}) collective-permute-start(bf16[648,512]{1,0:T(8,128)(2,1)} %param.9), channel_id=1, source_target_pairs={{0,0},{1,1},{2,16},{3,17},{4,32},{5,33},{6,48},{7,49},{8,64},{9,65... | collective-permute-start | bytes 1990664 | tf_op jit(solution)/shard_map/ppermute | solution.py:143
  12.1 117.8 %copy-start.5 = (bf16[648,648]{1,0:T(8,128)(2,1)}, bf16[648,648]{1,0:T(8,128)(2,1)S(1)}, u32[]{:S(2)}) copy-start(bf16[648,648]{1,0:T(8,128)(2,1)S(1)} %get-tuple-element.44.r_1_) | copy-start | bytes 2519428
  12.1 68.4 %collective-permute-start = (bf16[648,648]{1,0:T(8,128)(2,1)}, bf16[648,648]{1,0:T(8,128)(2,1)S(1)}, u32[]{:S(2)}, u32[]{:S(2)}) collective-permute-start(bf16[648,648]{1,0:T(8,128)(2,1)} %get-tuple-element.43), channel_id=1, source_target_pairs={{0,1},{1,0},{2,3},{3,2},{4,5},{5,4},{6,7},{7,6},{8,9},{9,8},{10,11... | collective-permute-start | bytes 2519432 | tf_op jit(solution)/shard_map/ppermute | solution.py:130
  15.9 64.7 %collective-permute-start.19 = (bf16[648,512]{1,0:T(8,128)(2,1)S(1)}, bf16[648,512]{1,0:T(8,128)(2,1)}, u32[]{:S(2)}, u32[]{:S(2)}) collective-permute-start(bf16[648,512]{1,0:T(8,128)(2,1)S(1)} %pad_maximum_fusion.1.r_4_.a_4_), channel_id=1, source_target_pairs={{0,64},{16,80},{32,96},{48,112},{64,0},{80,16},{96,32},{112,48},{1... | collective-permute-start | bytes 1990664 | tf_op jit(solution)/shard_map/ppermute | solution.py:135
  66.8 16.5 %collective-permute-start.1 = (bf16[648,512]{1,0:T(8,128)(2,1)S(1)}, bf16[648,512]{1,0:T(8,128)(2,1)S(1)}, u32[]{:S(2)}, u32[]{:S(2)}) collective-permute-start(bf16[648,512]{1,0:T(8,128)(2,1)S(1)} %pad_maximum_fusion.1.r_4_.a_4_), channel_id=1, source_target_pairs={{0,1},{1,0},{2,3},{3,2},{4,5},{5,4},{6,7},{7,6},{8,9},{9,8},{10,11... | collective-permute-start | bytes 1990664 | tf_op jit(solution)/shard_map/ppermute | solution.py:140
  68.6 17.9 %collective-permute-start.9 = (bf16[648,512]{1,0:T(8,128)(2,1)S(1)}, bf16[648,512]{1,0:T(8,128)(2,1)}, u32[]{:S(2)}, u32[]{:S(2)}) collective-permute-start(bf16[648,512]{1,0:T(8,128)(2,1)S(1)} %pad_maximum_fusion.1.r_4_.a_4_), channel_id=1, source_target_pairs={{0,16},{16,32},{32,48},{48,0},{64,80},{80,96},{96,112},{112,64},{1... | collective-permute-start | bytes 1990664 | tf_op jit(solution)/shard_map/ppermute | solution.py:137
  68.6 20.3 %collective-permute-start.11 = (bf16[648,512]{1,0:T(8,128)(2,1)S(1)}, bf16[648,512]{1,0:T(8,128)(2,1)}, u32[]{:S(2)}, u32[]{:S(2)}) collective-permute-start(bf16[648,512]{1,0:T(8,128)(2,1)S(1)} %pad_maximum_fusion.1.r_4_.a_4_), channel_id=1, source_target_pairs={{0,48},{16,0},{32,16},{48,32},{64,112},{80,64},{96,80},{112,96},{1... | collective-permute-start | bytes 1990664 | tf_op jit(solution)/shard_map/ppermute | solution.py:137
  80.6 48.3 %collective-permute-start.21 = (bf16[648,512]{1,0:T(8,128)(2,1)}, bf16[648,512]{1,0:T(8,128)(2,1)}, u32[]{:S(2)}, u32[]{:S(2)}) collective-permute-start(bf16[648,512]{1,0:T(8,128)(2,1)} %collective-permute-done.19.r_4_.a_5_), channel_id=1, source_target_pairs={{0,16},{16,32},{32,48},{48,0},{64,80},{80,96},{96,112},{112,64},{1... | collective-permute-start | bytes 1990664 | tf_op jit(solution)/shard_map/ppermute | solution.py:139
  80.6 50.6 %copy-start.7 = (bf16[648,648]{1,0:T(8,128)(2,1)}, bf16[648,648]{1,0:T(8,128)(2,1)S(1)}, u32[]{:S(2)}) copy-start(bf16[648,648]{1,0:T(8,128)(2,1)S(1)} %collective-permute-done.r_2_) | copy-start | bytes 2519428
  80.6 49.3 %collective-permute-start.23 = (bf16[648,512]{1,0:T(8,128)(2,1)}, bf16[648,512]{1,0:T(8,128)(2,1)}, u32[]{:S(2)}, u32[]{:S(2)}) collective-permute-start(bf16[648,512]{1,0:T(8,128)(2,1)} %collective-permute-done.19.r_4_.a_5_), channel_id=1, source_target_pairs={{0,48},{16,0},{32,16},{48,32},{64,112},{80,64},{96,80},{112,96},{1... | collective-permute-start | bytes 1990664 | tf_op jit(solution)/shard_map/ppermute | solution.py:139
  83.2 47.9 %collective-permute-start.31 = (bf16[648,512]{1,0:T(8,128)(2,1)S(1)}, bf16[648,512]{1,0:T(8,128)(2,1)}, u32[]{:S(2)}, u32[]{:S(2)}) collective-permute-start(bf16[648,512]{1,0:T(8,128)(2,1)S(1)} %pad_maximum_fusion.1.r_4_.a_4_), channel_id=1, source_target_pairs={{0,32},{16,48},{32,0},{48,16},{64,96},{80,112},{96,64},{112,80},{1... | collective-permute-start | bytes 1990664 | tf_op jit(solution)/shard_map/ppermute | solution.py:137
  86.5 52.4 %collective-permute-start.20 = (bf16[648,512]{1,0:T(8,128)(2,1)}, bf16[648,512]{1,0:T(8,128)(2,1)S(1)}, u32[]{:S(2)}, u32[]{:S(2)}) collective-permute-start(bf16[648,512]{1,0:T(8,128)(2,1)} %collective-permute-done.19.r_4_.a_5_), channel_id=1, source_target_pairs={{0,1},{1,0},{2,3},{3,2},{4,5},{5,4},{6,7},{7,6},{8,9},{9,8},{10,11... | collective-permute-start | bytes 1990664 | tf_op jit(solution)/shard_map/ppermute | solution.py:140
  89.0 50.2 %collective-permute-start.33 = (bf16[648,512]{1,0:T(8,128)(2,1)}, bf16[648,512]{1,0:T(8,128)(2,1)S(1)}, u32[]{:S(2)}, u32[]{:S(2)}) collective-permute-start(bf16[648,512]{1,0:T(8,128)(2,1)} %collective-permute-done.19.r_4_.a_5_), channel_id=1, source_target_pairs={{0,32},{16,48},{32,0},{48,16},{64,96},{80,112},{96,64},{112,80},{1... | collective-permute-start | bytes 1990664 | tf_op jit(solution)/shard_map/ppermute | solution.py:139
  128.8 10.7 %collective-permute-start.22 = (bf16[648,512]{1,0:T(8,128)(2,1)}, bf16[648,512]{1,0:T(8,128)(2,1)S(1)}, u32[]{:S(2)}, u32[]{:S(2)}) collective-permute-start(bf16[648,512]{1,0:T(8,128)(2,1)} %collective-permute-done.21.r_6_.a_6_), channel_id=1, source_target_pairs={{0,1},{1,0},{2,3},{3,2},{4,5},{5,4},{6,7},{7,6},{8,9},{9,8},{10,11... | collective-permute-start | bytes 1990664 | tf_op jit(solution)/shard_map/ppermute | solution.py:140
  129.9 9.7 %collective-permute-start.24 = (bf16[648,512]{1,0:T(8,128)(2,1)}, bf16[648,512]{1,0:T(8,128)(2,1)S(1)}, u32[]{:S(2)}, u32[]{:S(2)}) collective-permute-start(bf16[648,512]{1,0:T(8,128)(2,1)} %collective-permute-done.23.r_8_.a_7_), channel_id=1, source_target_pairs={{0,1},{1,0},{2,3},{3,2},{4,5},{5,4},{6,7},{7,6},{8,9},{9,8},{10,11... | collective-permute-start | bytes 1990664 | tf_op jit(solution)/shard_map/ppermute | solution.py:140
  131.2 7.4 %collective-permute-start.2 = (bf16[648,256]{1,0:T(8,128)(2,1)S(1)}, bf16[648,256]{1,0:T(8,128)(2,1)S(1)}, u32[]{:S(2)}, u32[]{:S(2)}) collective-permute-start(bf16[648,256]{1,0:T(8,128)(2,1)S(1)} %get-tuple-element.18), channel_id=1, source_target_pairs={{0,2},{1,7},{2,0},{3,5},{4,6},{5,3},{6,4},{7,1},{8,10},{9,15},{10,... | collective-permute-start | bytes 995336 | tf_op jit(solution)/shard_map/ppermute | solution.py:150
  138.6 10.8 %collective-permute-start.10 = (bf16[648,512]{1,0:T(8,128)(2,1)}, bf16[648,512]{1,0:T(8,128)(2,1)S(1)}, u32[]{:S(2)}, u32[]{:S(2)}) collective-permute-start(bf16[648,512]{1,0:T(8,128)(2,1)} %collective-permute-done.9.r_4_.a_5_), channel_id=1, source_target_pairs={{0,1},{1,0},{2,3},{3,2},{4,5},{5,4},{6,7},{7,6},{8,9},{9,8},{10,11... | collective-permute-start | bytes 1990664 | tf_op jit(solution)/shard_map/ppermute | solution.py:140
  138.9 10.9 %collective-permute-start.12 = (bf16[648,512]{1,0:T(8,128)(2,1)}, bf16[648,512]{1,0:T(8,128)(2,1)S(1)}, u32[]{:S(2)}, u32[]{:S(2)}) collective-permute-start(bf16[648,512]{1,0:T(8,128)(2,1)} %collective-permute-done.11.r_6_.a_6_), channel_id=1, source_target_pairs={{0,1},{1,0},{2,3},{3,2},{4,5},{5,4},{6,7},{7,6},{8,9},{9,8},{10,11... | collective-permute-start | bytes 1990664 | tf_op jit(solution)/shard_map/ppermute | solution.py:140
  139.2 17.5 %copy-start.8 = (bf16[648,512]{1,0:T(8,128)(2,1)}, bf16[648,512]{1,0:T(8,128)(2,1)S(1)}, u32[]{:S(2)}) copy-start(bf16[648,512]{1,0:T(8,128)(2,1)S(1)} %collective-permute-done.33.r_6_.a_6_) | copy-start | bytes 1990660
  139.2 17.5 %collective-permute-start.32 = (bf16[648,512]{1,0:T(8,128)(2,1)}, bf16[648,512]{1,0:T(8,128)(2,1)S(1)}, u32[]{:S(2)}, u32[]{:S(2)}) collective-permute-start(bf16[648,512]{1,0:T(8,128)(2,1)} %collective-permute-done.31.r_4_.a_5_), channel_id=1, source_target_pairs={{0,1},{1,0},{2,3},{3,2},{4,5},{5,4},{6,7},{7,6},{8,9},{9,8},{10,11... | collective-permute-start | bytes 1990664 | tf_op jit(solution)/shard_map/ppermute | solution.py:140
  139.6 9.6 %collective-permute-start.3 = (bf16[648,128]{1,0:T(8,128)(2,1)S(1)}, bf16[648,128]{1,0:T(8,128)(2,1)S(1)}, u32[]{:S(2)}, u32[]{:S(2)}) collective-permute-start(bf16[648,128]{1,0:T(8,128)(2,1)S(1)} %add_convert_fusion.11), channel_id=1, source_target_pairs={{0,6},{1,3},{2,4},{3,1},{4,2},{5,7},{6,0},{7,5},{8,14},{9,11},{10,... | collective-permute-start | bytes 497672 | tf_op jit(solution)/shard_map/ppermute | solution.py:152
  139.6 17.1 %collective-permute-start.34 = (bf16[648,512]{1,0:T(8,128)(2,1)S(1)}, bf16[648,512]{1,0:T(8,128)(2,1)S(1)}, u32[]{:S(2)}, u32[]{:S(2)}) collective-permute-start(bf16[648,512]{1,0:T(8,128)(2,1)S(1)} %collective-permute-done.33.r_6_.a_6_), channel_id=1, source_target_pairs={{0,1},{1,0},{2,3},{3,2},{4,5},{5,4},{6,7},{7,6},{8,9},{9,8},{10,11... | collective-permute-start | bytes 1990664 | tf_op jit(solution)/shard_map/ppermute | solution.py:140
  149.1 16.4 %collective-permute-start.25 = (bf16[648,768]{1,0:T(8,128)(2,1)}, bf16[648,768]{1,0:T(8,128)(2,1)S(1)}, u32[]{:S(2)}, u32[]{:S(2)}) collective-permute-start(bf16[648,768]{1,0:T(8,128)(2,1)} %get-tuple-element.24), channel_id=1, source_target_pairs={{0,2},{1,7},{2,0},{3,5},{4,6},{5,3},{6,4},{7,1},{8,10},{9,15},{10,... | collective-permute-start | bytes 2985992 | tf_op jit(solution)/shard_map/ppermute | solution.py:150
  149.4 7.1 %collective-permute-start.4 = (bf16[648,128]{1,0:T(8,128)(2,1)S(1)}, bf16[648,128]{1,0:T(8,128)(2,1)S(1)}, u32[]{:S(2)}, u32[]{:S(2)}) collective-permute-start(bf16[648,128]{1,0:T(8,128)(2,1)S(1)} %add_convert_fusion.10), channel_id=1, source_target_pairs={{0,8},{1,9},{2,10},{3,11},{4,12},{5,13},{6,14},{7,15},{8,0},{9,1},... | collective-permute-start | bytes 497672 | tf_op jit(solution)/shard_map/ppermute | solution.py:154
  153.9 21.5 %collective-permute-start.13 = (bf16[648,512]{1,0:T(8,128)(2,1)S(1)}, bf16[648,512]{1,0:T(8,128)(2,1)S(1)}, u32[]{:S(2)}, u32[]{:S(2)}) collective-permute-start(bf16[648,512]{1,0:T(8,128)(2,1)S(1)} %get-tuple-element.21), channel_id=1, source_target_pairs={{0,2},{1,7},{2,0},{3,5},{4,6},{5,3},{6,4},{7,1},{8,10},{9,15},{10,... | collective-permute-start | bytes 1990664 | tf_op jit(solution)/shard_map/ppermute | solution.py:150
  156.6 6.8 %collective-permute-start.5 = (bf16[648,128]{1,0:T(8,128)(2,1)S(1)}, bf16[648,128]{1,0:T(8,128)(2,1)S(1)}, u32[]{:S(2)}, u32[]{:S(2)}) collective-permute-start(bf16[648,128]{1,0:T(8,128)(2,1)S(1)} %add_convert_fusion.9.a_0_), channel_id=1, source_target_pairs={{0,6},{1,3},{2,4},{3,1},{4,2},{5,7},{6,0},{7,5},{8,14},{9,11},{10,... | collective-permute-start | bytes 497672 | tf_op jit(solution)/shard_map/ppermute | solution.py:156
  160.7 27.9 %collective-permute-start.35 = (bf16[648,512]{1,0:T(8,128)(2,1)S(1)}, bf16[648,512]{1,0:T(8,128)(2,1)S(1)}, u32[]{:S(2)}, u32[]{:S(2)}) collective-permute-start(bf16[648,512]{1,0:T(8,128)(2,1)S(1)} %get-tuple-element.27), channel_id=1, source_target_pairs={{0,2},{1,7},{2,0},{3,5},{4,6},{5,3},{6,4},{7,1},{8,10},{9,15},{10,... | collective-permute-start | bytes 1990664 | tf_op jit(solution)/shard_map/ppermute | solution.py:150
  162.1 53.8 %collective-permute-start.6 = (bf16[648,128]{1,0:T(8,128)(2,1)S(1)}, bf16[648,128]{1,0:T(8,128)(2,1)S(1)}, u32[]{:S(2)}, u32[]{:S(2)}) collective-permute-start(bf16[648,128]{1,0:T(8,128)(2,1)S(1)} %add_convert_fusion.9.a_0_), channel_id=1, source_target_pairs={{0,2},{1,7},{2,0},{3,5},{4,6},{5,3},{6,4},{7,1},{8,10},{9,15},{10,... | collective-permute-start | bytes 497672 | tf_op jit(solution)/shard_map/ppermute | solution.py:157
  163.4 54.8 %collective-permute-start.7 = (bf16[648,128]{1,0:T(8,128)(2,1)S(1)}, bf16[648,128]{1,0:T(8,128)(2,1)S(1)}, u32[]{:S(2)}, u32[]{:S(2)}) collective-permute-start(bf16[648,128]{1,0:T(8,128)(2,1)S(1)} %collective-permute-done.5.a_1_), channel_id=1, source_target_pairs={{0,2},{1,7},{2,0},{3,5},{4,6},{5,3},{6,4},{7,1},{8,10},{9,15},{10,... | collective-permute-start | bytes 497672 | tf_op jit(solution)/shard_map/ppermute | solution.py:158
  165.7 23.1 %collective-permute-start.26 = (bf16[648,384]{1,0:T(8,128)(2,1)S(1)}, bf16[648,384]{1,0:T(8,128)(2,1)S(1)}, u32[]{:S(2)}, u32[]{:S(2)}) collective-permute-start(bf16[648,384]{1,0:T(8,128)(2,1)S(1)} %add_convert_fusion.2), channel_id=1, source_target_pairs={{0,6},{1,3},{2,4},{3,1},{4,2},{5,7},{6,0},{7,5},{8,14},{9,11},{10,... | collective-permute-start | bytes 1493000 | tf_op jit(solution)/shard_map/ppermute | solution.py:152
  175.5 13.6 %collective-permute-start.14 = (bf16[648,256]{1,0:T(8,128)(2,1)S(1)}, bf16[648,256]{1,0:T(8,128)(2,1)S(1)}, u32[]{:S(2)}, u32[]{:S(2)}) collective-permute-start(bf16[648,256]{1,0:T(8,128)(2,1)S(1)} %add_convert_fusion.8), channel_id=1, source_target_pairs={{0,6},{1,3},{2,4},{3,1},{4,2},{5,7},{6,0},{7,5},{8,14},{9,11},{10,... | collective-permute-start | bytes 995336 | tf_op jit(solution)/shard_map/ppermute | solution.py:152
  188.7 6.8 %collective-permute-start.36 = (bf16[648,256]{1,0:T(8,128)(2,1)S(1)}, bf16[648,256]{1,0:T(8,128)(2,1)S(1)}, u32[]{:S(2)}, u32[]{:S(2)}) collective-permute-start(bf16[648,256]{1,0:T(8,128)(2,1)S(1)} %add_convert_fusion.5), channel_id=1, source_target_pairs={{0,6},{1,3},{2,4},{3,1},{4,2},{5,7},{6,0},{7,5},{8,14},{9,11},{10,... | collective-permute-start | bytes 995336 | tf_op jit(solution)/shard_map/ppermute | solution.py:152
  189.0 12.5 %collective-permute-start.27 = (bf16[648,384]{1,0:T(8,128)(2,1)S(1)}, bf16[648,384]{1,0:T(8,128)(2,1)S(1)}, u32[]{:S(2)}, u32[]{:S(2)}) collective-permute-start(bf16[648,384]{1,0:T(8,128)(2,1)S(1)} %add_convert_fusion.1), channel_id=1, source_target_pairs={{0,8},{1,9},{2,10},{3,11},{4,12},{5,13},{6,14},{7,15},{8,0},{9,1},... | collective-permute-start | bytes 1493000 | tf_op jit(solution)/shard_map/ppermute | solution.py:154
  189.3 19.4 %collective-permute-start.15 = (bf16[648,256]{1,0:T(8,128)(2,1)S(1)}, bf16[648,256]{1,0:T(8,128)(2,1)S(1)}, u32[]{:S(2)}, u32[]{:S(2)}) collective-permute-start(bf16[648,256]{1,0:T(8,128)(2,1)S(1)} %add_convert_fusion.7), channel_id=1, source_target_pairs={{0,8},{1,9},{2,10},{3,11},{4,12},{5,13},{6,14},{7,15},{8,0},{9,1},... | collective-permute-start | bytes 995336 | tf_op jit(solution)/shard_map/ppermute | solution.py:154
  195.6 20.1 %collective-permute-start.37 = (bf16[648,256]{1,0:T(8,128)(2,1)S(1)}, bf16[648,256]{1,0:T(8,128)(2,1)S(1)}, u32[]{:S(2)}, u32[]{:S(2)}) collective-permute-start(bf16[648,256]{1,0:T(8,128)(2,1)S(1)} %add_convert_fusion.4), channel_id=1, source_target_pairs={{0,8},{1,9},{2,10},{3,11},{4,12},{5,13},{6,14},{7,15},{8,0},{9,1},... | collective-permute-start | bytes 995336 | tf_op jit(solution)/shard_map/ppermute | solution.py:154
  201.7 18.6 %collective-permute-start.28 = (bf16[648,384]{1,0:T(8,128)(2,1)S(1)}, bf16[648,384]{1,0:T(8,128)(2,1)S(1)}, u32[]{:S(2)}, u32[]{:S(2)}) collective-permute-start(bf16[648,384]{1,0:T(8,128)(2,1)S(1)} %add_convert_fusion.a_1_), channel_id=1, source_target_pairs={{0,6},{1,3},{2,4},{3,1},{4,2},{5,7},{6,0},{7,5},{8,14},{9,11},{10,... | collective-permute-start | bytes 1493000 | tf_op jit(solution)/shard_map/ppermute | solution.py:156
  208.7 32.0 %copy-start.11 = (bf16[648,512]{1,0:T(8,128)(2,1)S(1)}, bf16[648,512]{1,0:T(8,128)(2,1)}, u32[]{:S(2)}) copy-start(bf16[648,512]{1,0:T(8,128)(2,1)} %copy-done.10) | copy-start | bytes 1990660
  208.7 12.2 %collective-permute-start.16 = (bf16[648,256]{1,0:T(8,128)(2,1)S(1)}, bf16[648,256]{1,0:T(8,128)(2,1)S(1)}, u32[]{:S(2)}, u32[]{:S(2)}) collective-permute-start(bf16[648,256]{1,0:T(8,128)(2,1)S(1)} %add_convert_fusion.6.a_1_), channel_id=1, source_target_pairs={{0,6},{1,3},{2,4},{3,1},{4,2},{5,7},{6,0},{7,5},{8,14},{9,11},{10,... | collective-permute-start | bytes 995336 | tf_op jit(solution)/shard_map/ppermute | solution.py:156
  215.7 7.7 %collective-permute-start.17 = (bf16[648,256]{1,0:T(8,128)(2,1)S(1)}, bf16[648,256]{1,0:T(8,128)(2,1)S(1)}, u32[]{:S(2)}, u32[]{:S(2)}) collective-permute-start(bf16[648,256]{1,0:T(8,128)(2,1)S(1)} %add_convert_fusion.6.a_1_), channel_id=1, source_target_pairs={{0,2},{1,7},{2,0},{3,5},{4,6},{5,3},{6,4},{7,1},{8,10},{9,15},{10,... | collective-permute-start | bytes 995336 | tf_op jit(solution)/shard_map/ppermute | solution.py:157
  215.9 11.0 %collective-permute-start.38 = (bf16[648,256]{1,0:T(8,128)(2,1)S(1)}, bf16[648,256]{1,0:T(8,128)(2,1)S(1)}, u32[]{:S(2)}, u32[]{:S(2)}) collective-permute-start(bf16[648,256]{1,0:T(8,128)(2,1)S(1)} %add_convert_fusion.3.a_1_), channel_id=1, source_target_pairs={{0,6},{1,3},{2,4},{3,1},{4,2},{5,7},{6,0},{7,5},{8,14},{9,11},{10,... | collective-permute-start | bytes 995336 | tf_op jit(solution)/shard_map/ppermute | solution.py:156
  218.2 26.6 %collective-permute-start.29 = (bf16[648,384]{1,0:T(8,128)(2,1)S(1)}, bf16[648,384]{1,0:T(8,128)(2,1)S(1)}, u32[]{:S(2)}, u32[]{:S(2)}) collective-permute-start(bf16[648,384]{1,0:T(8,128)(2,1)S(1)} %add_convert_fusion.a_1_), channel_id=1, source_target_pairs={{0,2},{1,7},{2,0},{3,5},{4,6},{5,3},{6,4},{7,1},{8,10},{9,15},{10,... | collective-permute-start | bytes 1493000 | tf_op jit(solution)/shard_map/ppermute | solution.py:157
  220.3 24.5 %collective-permute-start.30 = (bf16[648,384]{1,0:T(8,128)(2,1)S(1)}, bf16[648,384]{1,0:T(8,128)(2,1)S(1)}, u32[]{:S(2)}, u32[]{:S(2)}) collective-permute-start(bf16[648,384]{1,0:T(8,128)(2,1)S(1)} %collective-permute-done.28.a_2_), channel_id=1, source_target_pairs={{0,2},{1,7},{2,0},{3,5},{4,6},{5,3},{6,4},{7,1},{8,10},{9,15},{10,... | collective-permute-start | bytes 1493000 | tf_op jit(solution)/shard_map/ppermute | solution.py:158
  220.9 19.8 %collective-permute-start.18 = (bf16[648,256]{1,0:T(8,128)(2,1)S(1)}, bf16[648,256]{1,0:T(8,128)(2,1)S(1)}, u32[]{:S(2)}, u32[]{:S(2)}) collective-permute-start(bf16[648,256]{1,0:T(8,128)(2,1)S(1)} %collective-permute-done.16.a_2_), channel_id=1, source_target_pairs={{0,2},{1,7},{2,0},{3,5},{4,6},{5,3},{6,4},{7,1},{8,10},{9,15},{10,... | collective-permute-start | bytes 995336 | tf_op jit(solution)/shard_map/ppermute | solution.py:158
  223.4 24.8 %collective-permute-start.39 = (bf16[648,256]{1,0:T(8,128)(2,1)S(1)}, bf16[648,256]{1,0:T(8,128)(2,1)S(1)}, u32[]{:S(2)}, u32[]{:S(2)}) collective-permute-start(bf16[648,256]{1,0:T(8,128)(2,1)S(1)} %add_convert_fusion.3.a_1_), channel_id=1, source_target_pairs={{0,2},{1,7},{2,0},{3,5},{4,6},{5,3},{6,4},{7,1},{8,10},{9,15},{10,... | collective-permute-start | bytes 995336 | tf_op jit(solution)/shard_map/ppermute | solution.py:157
  226.8 21.4 %collective-permute-start.40 = (bf16[648,256]{1,0:T(8,128)(2,1)S(1)}, bf16[648,256]{1,0:T(8,128)(2,1)S(1)}, u32[]{:S(2)}, u32[]{:S(2)}) collective-permute-start(bf16[648,256]{1,0:T(8,128)(2,1)S(1)} %collective-permute-done.38.a_2_), channel_id=1, source_target_pairs={{0,2},{1,7},{2,0},{3,5},{4,6},{5,3},{6,4},{7,1},{8,10},{9,15},{10,... | collective-permute-start | bytes 995336 | tf_op jit(solution)/shard_map/ppermute | solution.py:158
  230.7 14.2 %copy-start.17 = (bf16[648,512]{1,0:T(8,128)(2,1)S(1)}, bf16[648,512]{1,0:T(8,128)(2,1)}, u32[]{:S(2)}) copy-start(bf16[648,512]{1,0:T(8,128)(2,1)} %copy-done.16) | copy-start | bytes 1990660
  230.7 14.2 %copy-start.19 = (bf16[648,512]{1,0:T(8,128)(2,1)S(1)}, bf16[648,512]{1,0:T(8,128)(2,1)}, u32[]{:S(2)}) copy-start(bf16[648,512]{1,0:T(8,128)(2,1)} %copy-done.18) | copy-start | bytes 1990660
  249.6 15.2 %collective-permute-start.41 = (bf16[648,648]{1,0:T(8,128)(2,1)S(1)}, bf16[648,648]{1,0:T(8,128)(2,1)S(1)}, u32[]{:S(2)}, u32[]{:S(2)}) collective-permute-start(bf16[648,648]{1,0:T(8,128)(2,1)S(1)} %mm2.15), channel_id=1, source_target_pairs={{0,1},{1,0},{2,3},{3,2},{4,5},{5,4},{6,7},{7,6},{8,9},{9,8},{10,11... | collective-permute-start | bytes 2519432 | tf_op jit(solution)/shard_map/ppermute | solution.py:163
  (19 other events, 93.7 us)

commit v2 on v0

v2 whole, which is shorter than its diff:
```python
import math

import jax
import jax.numpy as jnp
from jax import lax
from jax.experimental import pallas as pl
from jax.experimental.pallas import tpu as pltpu
from jax.sharding import PartitionSpec as P

F32 = jnp.float32
BF16 = jnp.bfloat16
X, Z = 4, 4
Q = 128
CHUNKS = (((0, 0),), ((0, 3), (0, 1), (1, 0)), ((1, 3), (1, 1)), ((0, 2), (1, 2)))
STEPS = (
    "M0 S0 Y0 G0 R0 M1 F0 S1 G1 M2 T0 Y1 S2 G2 M3 R1 Y2 S3 F1 R2 Y3 F2 R3 T1 F3 T2 T3".split()
)


def mode_perm(fn):
    out = []
    for j in range(16):
        yl, x, k = j // 8, (j // 2) % 4, j % 2
        a, b, c = fn(yl, x, k)
        out.append((j, (a * 4 + b) * 2 + c))
    return out


FIRST = mode_perm(lambda yl, x, k: (yl, x ^ (3 if k else 1), k))
SECOND = mode_perm(lambda yl, x, k: (yl, x ^ (1 if k else 3), k))
YSWAP = mode_perm(lambda yl, x, k: (1 - yl, x, k))
KSWAP = mode_perm(lambda yl, x, k: (yl, x, 1 - k))


def all_perm(fn):
    out = []
    for d in range(128):
        src = (d // 64, (d // 16) % 4, (d // 8) % 2, (d // 2) % 4, d % 2)
        a, b, c, e, k = fn(*src)
        out.append((d, (((a * 4 + b) * 2 + c) * 4 + e) * 2 + k))
    return out


def cfg_perm(dy, dz):
    return [(c, (c // 4 ^ dy) * 4 + (c % 4 + dz) % 4) for c in range(8)]


ONWARD = all_perm(lambda yh, z, yl, x, k: (yh, (z + (3 if k else 1)) % 4, yl, x, k))
FORCES = all_perm(lambda yh, z, yl, x, k: (yl, x, yh, (x + z) % 4, k))

VM = pl.BlockSpec(memory_space=pltpu.VMEM)
SM = pl.BlockSpec(memory_space=pltpu.SMEM)
ANY = pl.BlockSpec(memory_space=pl.ANY)
HBM = pl.BlockSpec(memory_space=pltpu.HBM)
TOKEN = jax.ShapeDtypeStruct((8, 128), F32)


class Chain:
    def __init__(self):
        self.token = None

    def __call__(self, name, body, outs, args, specs, out_specs=None, aliases=None, scratch=(), mib=4):
        given = self.token is not None
        n_in, n_out = len(args), len(outs)

        def kernel(*refs):
            ins = refs[:n_in]
            rest = refs[n_in + int(given) :]
            rest[n_out][...] = jnp.zeros((8, 128), F32)
            body(ins, rest[:n_out], rest[n_out + 1 :])

        res = pl.pallas_call(
            kernel,
            out_shape=list(outs) + [TOKEN],
            in_specs=list(specs) + ([ANY] if given else []),
            out_specs=(list(out_specs) if out_specs else [VM] * n_out) + [VM],
            input_output_aliases=aliases or {},
            scratch_shapes=list(scratch),
            compiler_params=pltpu.CompilerParams(vmem_limit_bytes=mib * 1024 * 1024),
            cost_estimate=pl.CostEstimate(flops=1000, bytes_accessed=1000, transcendentals=0),
            name=name,
        )(*args, *([self.token] if given else []))
        self.token = res[-1]
        return res[:-1]


def like(v):
    return jax.ShapeDtypeStruct(v.shape, v.dtype)


def wide(v):
    return v.astype(F32)


def reorder(v):
    return jnp.concatenate([v[:, :Q], v[:, 2 * Q : 3 * Q], v[:, Q : 2 * Q], v[:, 3 * Q :]], axis=1)


def on_device(coords, curvature, weight, polar, forces):
    i, j = lax.axis_index("cfg"), lax.axis_index("mode")
    yh, z = i // Z, i % Z
    k, x, chip, yl = j % 2, (j // 2) % X, j // 2, j // (2 * X)
    rows = coords.shape[0]
    run = Chain()

    second, first = jnp.where(k == 0, 3, 1), jnp.where(k == 0, 1, 3)
    order = jnp.stack([x, x ^ second, x ^ first, x ^ 2]).astype(jnp.int32)
    core = jnp.reshape(k, (1,)).astype(jnp.int32)

    def arrange(v):
        def body(ins, outs, _):
            for s in range(4):
                at = pl.multiple_of(ins[0][s] * Q, Q)
                outs[0][:, s * Q : (s + 1) * Q] = ins[1][:, pl.ds(at, Q)]

        return run("arrange", body, [like(v)], [order, v], [SM, VM])[0]

    unit, other = {}, {}
    f_far = lax.ppermute(forces, ("cfg", "mode"), FORCES)
    unit[0, 0] = arrange(coords)
    other[0, 0] = lax.ppermute(unit[0, 0], "mode", KSWAP)
    unit[0, 3] = lax.ppermute(unit[0, 0], "cfg", cfg_perm(0, 1))
    unit[0, 1] = lax.ppermute(unit[0, 0], "cfg", cfg_perm(0, -1))
    unit[1, 0] = lax.ppermute(unit[0, 0], "cfg", cfg_perm(1, 0))

    window = 6 * 128

    def slice_polar(ins, outs, scratch):
        at, scale, source = ins
        wide_t, narrow, sems = scratch
        moves = []
        for h in range(2):
            begin = pl.multiple_of(at[2 * h] * 128, 128)
            moves.append(pltpu.make_async_copy(source.at[:, pl.ds(begin, window)], narrow.at[h], sems.at[h]))
            moves[-1].start()
        for h in range(2):
            moves[h].wait()
            wide_t[...] = wide(narrow[h]).T * scale[...]
            skip = pl.multiple_of(at[2 * h + 1] * 8, 8)
            outs[h][...] = wide_t[pl.ds(skip, rows), :].astype(BF16)

    begins = [(2 * i + 1 - k) * rows, (2 * i + k) * rows]
    at = jnp.stack([v for b in begins for v in (b // 128, (b % 128) // 8)]).astype(jnp.int32)
    half = jax.ShapeDtypeStruct((rows, rows), BF16)
    px, po = run(
        "polar",
        slice_polar,
        [half, half],
        [at, curvature[None, :], polar],
        [SM, VM, HBM],
        scratch=[
            pltpu.VMEM((window, rows), F32),
            pltpu.VMEM((2, rows, window), BF16),
            pltpu.SemaphoreType.DMA((2,)),
        ],
        mib=54,
    )
    px = lax.ppermute(px, "mode", KSWAP)
    f_own = arrange(forces)

    def matmul1(chunk, f, flags):
        n = len(chunk)
        shapes = [jax.ShapeDtypeStruct((rows, w * n * Q), BF16) for w in (1, 1, 2)]

        def body(ins, outs, _):
            flag, a, b, fr = ins[:4]
            keep, s2, s1 = outs
            for u in range(n):
                h = jnp.dot(a[...], ins[4 + 2 * u][...], preferred_element_type=F32)
                h += jnp.dot(b[...], reorder(ins[5 + 2 * u][...]), preferred_element_type=F32)
                h += wide(fr[...]) * flag[u].astype(F32)
                h = h.astype(BF16)
                lo, hi = slice(u * Q, (u + 1) * Q), slice((n + u) * Q, (n + u + 1) * Q)
                keep[:, lo] = h[:, :Q]
                s2[:, lo] = h[:, Q : 2 * Q]
                s1[:, lo] = h[:, 2 * Q : 3 * Q]
                s1[:, hi] = h[:, 3 * Q :]

        args = [flags, po, px, f] + [v for u in chunk for v in (unit[u], other[u])]
        return run("product1", body, shapes, args, [SM] + [VM] * (len(args) - 1), mib=6 + 3 * n)

    def add(width, args, starts):
        def body(ins, outs, _):
            total = None
            for r, at in zip(ins, starts):
                v = wide(r[:, at : at + width])
                total = v if total is None else total + v
            outs[0][...] = total.astype(BF16)

        return run("add", body, [jax.ShapeDtypeStruct((rows, width), BF16)], args, [VM] * len(args))[0]

    def gate(args, pick=None):
        outs = [like(v) for v in args]
        scratch = []
        if pick:
            outs.append(like(args[pick[0]]))
            scratch = [pltpu.SemaphoreType.DMA]

        def body(ins, outs, sem):
            if pick:
                for c in range(2):

                    @pl.when(ins[0][0] == c)
                    def _():
                        move = pltpu.make_async_copy(ins[1 + pick[c]], outs[-1], sem[0])
                        move.start()
                        move.wait()

        aliases = {1 + a: a for a in range(len(args))}
        return run(
            "gate", body, outs, [core] + list(args), [SM] + [ANY] * len(args), [ANY] * len(outs), aliases, scratch
        )

    def join(a, b):
        w = a.shape[1]

        def body(ins, outs, _):
            outs[0][:, :w] = ins[0][...]
            outs[0][:, w:] = ins[1][...]

        return run("join", body, [jax.ShapeDtypeStruct((rows, 2 * w), BF16)], [a, b], [VM] * 2)[0]

    def matmul2(groups, acc, names, swap, dtype):
        begins = acc is None
        args = [] if begins else [acc]
        for chunk, r in groups:
            args += list(r) + [names[u] for u in chunk]

        def body(ins, outs, _):
            ins = list(ins)
            total = None if begins else ins.pop(0)[...]
            for chunk, _ in groups:
                n = len(chunk)
                pieces = [(r, h) for r in ins[:2] for h in range(2)]
                if swap:
                    pieces = [pieces[p] for p in (0, 2, 1, 3)]
                ins = ins[2:]
                for u in range(n):
                    ru = jnp.concatenate([r[:, (h * n + u) * Q : (h * n + u + 1) * Q] for r, h in pieces], axis=1)
                    t = lax.dot_general(
                        ins[u][...], ru, (((1,), (1,)), ((), ())), preferred_element_type=F32
                    )
                    total = t if total is None else total + t
                ins = ins[len(chunk) :]
            outs[0][...] = total.astype(dtype)

        return run("product2", body, [jax.ShapeDtypeStruct((rows, rows), dtype)], args, [VM] * len(args), mib=14)[0]

    last = len(CHUNKS) - 1
    keep, got1, half2, got2, part, got3, r0, r1, near_half, far_half = ({} for _ in range(10))
    own_sum = oth_sum = back = None
    f_all = None
    for step in STEPS:
        stage, c = step[0], int(step[1])
        chunk = CHUNKS[c]
        n = len(chunk)
        if stage == "M":
            if c == 0:
                flags = jnp.reshape(i == chip, (1,)).astype(jnp.int32)
                f = f_own
            else:
                if f_all is None:
                    f_all = arrange(f_far)
                f = f_all
                flags = jnp.stack(
                    [(((yh ^ dy) == yl) & ((2 * z + dz) % Z == x)).astype(jnp.int32) for dy, dz in chunk]
                )
            keep[c], half2[c], s1 = matmul1(chunk, f, flags)
            got1[c] = lax.ppermute(s1, "mode", FIRST)
        elif stage == "S":
            v = add(n * Q, [half2[c], got1[c]], [0, n * Q])
            got2[c] = lax.ppermute(v, "mode", SECOND)
        elif stage == "Y":
            part[c] = add(n * Q, [keep[c], got1[c], got2[c]], [0, 0, 0])
            got3[c] = lax.ppermute(part[c], "mode", YSWAP)
        elif stage == "R":
            r0[c] = add(n * Q, [part[c], got3[c]], [0, 0])
            r1[c] = lax.ppermute(r0[c], "mode", SECOND)
        elif stage == "F":
            near_half[c] = join(r0[c], r1[c])
            far_half[c] = lax.ppermute(near_half[c], "mode", FIRST)
        elif stage == "T":
            group = [(chunk, (near_half[c], far_half[c]))]
            oth_sum = matmul2(group, oth_sum, other, True, BF16 if c == last else F32)
            if c == last:
                back = lax.ppermute(oth_sum, "mode", KSWAP)
            own_sum = matmul2(group, own_sum, unit, False, F32)
        elif step == "G0":
            near = [(1, 0), (0, 3), (0, 1)]
            *vals, pick = gate([unit[u] for u in near], (1, 2))
            for u, v in zip(near, vals):
                unit[u] = v
                other[u] = lax.ppermute(v, "mode", KSWAP)
            unit[1, 3] = lax.ppermute(unit[1, 0], "cfg", cfg_perm(0, 1))
            unit[1, 1] = lax.ppermute(unit[1, 0], "cfg", cfg_perm(0, -1))
            unit[0, 2] = lax.ppermute(pick, ("cfg", "mode"), ONWARD)
        elif step == "G1":
            near = [(1, 3), (1, 1)]
            *vals, pick = gate([unit[u] for u in near], (0, 1))
            for u, v in zip(near, vals):
                unit[u] = v
                other[u] = lax.ppermute(v, "mode", KSWAP)
            unit[1, 2] = lax.ppermute(pick, ("cfg", "mode"), ONWARD)
        elif step == "G2":
            near = [(0, 2), (1, 2)]
            for u, v in zip(near, gate([unit[u] for u in near])):
                unit[u] = v
                other[u] = lax.ppermute(v, "mode", KSWAP)

    factor = weight[:, None] * (1.0 / math.sqrt(coords.shape[1] * lax.axis_size("cfg")))

    def finish(ins, outs, _):
        own, got = ins[2][...] * ins[1][...], wide(ins[3][...]) * ins[1][...]
        for c in range(2):

            @pl.when(ins[0][0] == c)
            def _():
                outs[0][:, :rows] = (own, got)[c]
                outs[0][:, rows:] = (got, own)[c]

    (out,) = run(
        "finish",
        finish,
        [jax.ShapeDtypeStruct((rows, 2 * rows), F32)],
        [core, factor, own_sum, back],
        [SM, VM, VM, VM],
        mib=12,
    )
    return out.T


def solution(mesh):
    placed = (P("mode", "cfg"), P("mode"), P("mode"), P("mode", None), P("mode", "cfg"))
    return jax.shard_map(
        on_device, mesh=mesh, in_specs=placed, out_specs=P("cfg", "mode"), check_vma=False
    )
```

time: 416 us -> 202 us (0.49)
  waiting for transfers between devices: 337 us -> 75.5 us
  starting transfers between devices: 0.09 us -> 60.9 us
  Pallas kernels: 0 us -> 48.4 us
  matrix products: 36.7 us -> 0 us
  between operations: 13.1 us -> 0.59 us
  local copies, waits for them, and re-layouts: 22.1 us -> 14.9 us
    unnamed x4 -> x0, waiting for transfers between devices: 193 us -> none
    reduce_scatter x1 -> x0, waiting for transfers between devices: 79 us -> none  [on_device(): lax.psum_scatter(lax.dot_general(polar, scaled, contract, preferred_eleme...]
    ppermute x0 -> x38, waiting for transfers between devices: none -> 75.5 us  [the longest x4 20.8 us: on_device(): far_half[c] = lax.ppermute(near_half[c], 'mode', FIRST)]
    all_gather x1 -> x0, waiting for transfers between devices: 65 us -> none  [on_device(): residual = lax.all_gather(resid_rows, 'mode', axis=0, tiled=True)]
    ppermute x0 -> x38, starting transfers between devices: none -> 60.9 us  [the longest x4 12.8 us: on_device(): got1[c] = lax.ppermute(s1, 'mode', FIRST)]
    pallas_call x0 -> x36, Pallas kernels: none -> 48.4 us  [__call__(): pl.pallas_call(kernel, out_shape=list(outs) + [TOKEN], in_specs=list(spec...]
    dot_general x2 -> x0, matrix products: 36.7 us -> none  [the longest x1 20.2 us: on_device(): lax.dot_general(polar, scaled, contract, preferred_element_type=f32)]
    unnamed x8 -> x68, local copies, waits for them, and re-layouts: 22.1 us -> 13.5 us
  transfers between devices with their start and end apart: 3 -> 38, of which waited for: 3 -> 18; matrix products, arithmetic and copies ran while one was open for 0% -> 0% of each run, Pallas kernels for 0% -> 14%
where the time goes in v2:
time: 202 us; the launch traced here: 201 us
  waiting for transfers between devices  75.5 us (37%)
  starting transfers between devices  60.9 us (30%)
  Pallas kernels  48.4 us (24%)
  local copies, waits for them, and re-layouts  14.9 us (7%)
    pallas_call x36, Pallas kernels, __call__(): pl.pallas_call(kernel, out_shape=list(outs) + [TOKEN], in_specs=list(spec...  48.4 us
    ppermute x4, waiting for transfers between devices, on_device(): far_half[c] = lax.ppermute(near_half[c], 'mode', FIRST)  20.8 us
    unnamed x68, local copies, waits for them, and re-layouts  13.5 us
    ppermute x4, starting transfers between devices, on_device(): got1[c] = lax.ppermute(s1, 'mode', FIRST)  12.8 us
    ppermute x4, waiting for transfers between devices, on_device(): got3[c] = lax.ppermute(part[c], 'mode', YSWAP)  12.4 us
    ppermute x4, waiting for transfers between devices, on_device(): r1[c] = lax.ppermute(r0[c], 'mode', SECOND)  11.2 us
    ppermute x4, waiting for transfers between devices, on_device(): got2[c] = lax.ppermute(v, 'mode', SECOND)  10.3 us
    ppermute x4, waiting for transfers between devices, on_device(): got1[c] = lax.ppermute(s1, 'mode', FIRST)  8.39 us
  transfers between devices with their start and end apart: 38, of which 18 were waited for; matrix products, arithmetic and copies ran while one was open for 0% of the time, Pallas kernels for 14%

profile of v2, /device:TPU:1, one launch (start us, length us, event | category | flops | bytes accessed | tf_op | source)
XLA Modules:
  0.0 201.3 jit_solution(2378434092493471333)
XLA Ops:
  4.4 3.8 %polar.1 = (bf16[648,648]{1,0:T(8,128)(2,1)}, bf16[648,648]{1,0:T(8,128)(2,1)}, f32[8,128]{1,0:T(8,128)}) custom-call(s32[4]{0:T(128)} %pad_add_fusion.refs_0_, f32[1,648]{1,0:T(1,128)} %broadcast_in_dim.4.refs_1_, bf16[648,10368]{1,0:T(8,128)(2,1)} %refs_2_.1, f32[8,128]{1,0:T(8,128)} %copy-done.23), custom_call_target="tpu_custom_call" | custom-call | flops 1000 | bytes 1000 | tf_op jit(solution)/shard_map/polar/pallas_call | solution.py:72
  8.3 1.5 collective-permute-start
  9.9 3.0 %collective-permute-start.5 = (bf16[648,512]{1,0:T(8,128)(2,1)S(1)}, bf16[648,512]{1,0:T(8,128)(2,1)S(1)}, u32[]{:S(2)}, u32[]{:S(2)}) collective-permute-start(bf16[648,512]{1,0:T(8,128)(2,1)S(1)} %get-tuple-element.96.refs_4_.refs_2_), channel_id=1, source_target_pairs={{0,64},{16,80},{32,96},{48,112},{64,0},{80,16},{96,32},{112,48},{1... | collective-permute-start | bytes 1990664 | tf_op jit(solution)/shard_map/ppermute | solution.py:124
  12.9 1.6 collective-permute-start.6
  14.5 2.1 %collective-permute-start.7 = (bf16[648,512]{1,0:T(8,128)(2,1)S(1)}, bf16[648,512]{1,0:T(8,128)(2,1)}, u32[]{:S(2)}, u32[]{:S(2)}) collective-permute-start(bf16[648,512]{1,0:T(8,128)(2,1)S(1)} %get-tuple-element.96.refs_4_.refs_2_), channel_id=1, source_target_pairs={{0,48},{16,0},{32,16},{48,32},{64,112},{80,64},{96,80},{112,96},{1... | collective-permute-start | bytes 1990664 | tf_op jit(solution)/shard_map/ppermute | solution.py:123
  19.4 1.4 copy-done
  23.2 2.6 %collective-permute-start.2 = (bf16[648,256]{1,0:T(8,128)(2,1)S(1)}, bf16[648,256]{1,0:T(8,128)(2,1)S(1)}, u32[]{:S(2)}, u32[]{:S(2)}) collective-permute-start(bf16[648,256]{1,0:T(8,128)(2,1)S(1)} %get-tuple-element.99), channel_id=1, source_target_pairs={{0,2},{1,7},{2,0},{3,5},{4,6},{5,3},{6,4},{7,1},{8,10},{9,15},{10,... | collective-permute-start | bytes 995336 | tf_op jit(solution)/shard_map/ppermute | solution.py:269
  25.7 5.1 %collective-permute-done.2.refs_1_ = bf16[648,256]{1,0:T(8,128)(2,1)S(1)} collective-permute-done((bf16[648,256]{1,0:T(8,128)(2,1)S(1)}, bf16[648,256]{1,0:T(8,128)(2,1)S(1)}, u32[]{:S(2)}, u32[]{:S(2)}) %collective-permute-start.2) | collective-permute-done | bytes 331808 | tf_op jit(solution)/shard_map/ppermute | solution.py:269
  31.0 6.8 %collective-permute-start.9 = (bf16[648,512]{1,0:T(8,128)(2,1)}, bf16[648,512]{1,0:T(8,128)(2,1)}, u32[]{:S(2)}, u32[]{:S(2)}) collective-permute-start(bf16[648,512]{1,0:T(8,128)(2,1)} %refs_1_.3), channel_id=1, source_target_pairs={{0,0},{1,1},{2,18},{3,19},{4,36},{5,37},{6,54},{7,55},{8,64},{9,65... | collective-permute-start | bytes 1990664 | tf_op jit(solution)/shard_map/ppermute | solution.py:119
  39.9 3.1 %collective-permute-start.10 = (bf16[648,512]{1,0:T(8,128)(2,1)}, bf16[648,512]{1,0:T(8,128)(2,1)}, u32[]{:S(2)}, u32[]{:S(2)}) collective-permute-start(bf16[648,512]{1,0:T(8,128)(2,1)} %get-tuple-element.110.refs_4_.refs_3_), channel_id=1, source_target_pairs={{0,1},{1,0},{2,3},{3,2},{4,5},{5,4},{6,7},{7,6},{8,9},{9,8},{10,11... | collective-permute-start | bytes 1990664 | tf_op jit(solution)/shard_map/ppermute | solution.py:293
  43.6 5.8 %collective-permute-done.4.refs_1_ = bf16[648,128]{1,0:T(8,128)(2,1)S(1)} collective-permute-done((bf16[648,128]{1,0:T(8,128)(2,1)S(1)}, bf16[648,128]{1,0:T(8,128)(2,1)S(1)}, u32[]{:S(2)}, u32[]{:S(2)}) %collective-permute-start.4) | collective-permute-done | bytes 165920 | tf_op jit(solution)/shard_map/ppermute | solution.py:275
  50.7 5.2 %product1.5 = (bf16[648,384]{1,0:T(8,128)(2,1)S(1)}, bf16[648,384]{1,0:T(8,128)(2,1)S(1)}, bf16[648,768]{1,0:T(8,128)(2,1)S(1)}, f32[8,128]{1,0:T(8,128)S(1)}) custom-call(s32[3]{0:T(128)S(1)} %add_convert_fusion.refs_0_, bf16[648,648]{1,0:T(8,128)(2,1)S(1)} %copy-done.1, bf16[648,648]{1,0:T(8,128)(2,1)S(1)} %collective-permute-done.refs_2_, ...), custom_call_target="tpu_custom_call" | custom-call | flops 1000 | bytes 1000 | tf_op jit(solution)/shard_map/product1/pallas_call | solution.py:72
  56.7 5.3 %collective-permute-start.16 = (bf16[648,768]{1,0:T(8,128)(2,1)S(1)}, bf16[648,768]{1,0:T(8,128)(2,1)S(1)}, u32[]{:S(2)}, u32[]{:S(2)}) collective-permute-start(bf16[648,768]{1,0:T(8,128)(2,1)S(1)} %get-tuple-element.117), channel_id=1, source_target_pairs={{0,2},{1,7},{2,0},{3,5},{4,6},{5,3},{6,4},{7,1},{8,10},{9,15},{10,... | collective-permute-start | bytes 2985992 | tf_op jit(solution)/shard_map/ppermute | solution.py:269
  62.0 2.7 %collective-permute-start.15 = (bf16[648,512]{1,0:T(8,128)(2,1)S(1)}, bf16[648,512]{1,0:T(8,128)(2,1)}, u32[]{:S(2)}, u32[]{:S(2)}) collective-permute-start(bf16[648,512]{1,0:T(8,128)(2,1)S(1)} %get-tuple-element.112.refs_8_.refs_5_), channel_id=1, source_target_pairs={{0,48},{16,0},{32,16},{48,32},{64,112},{80,64},{96,80},{112,96},{1... | collective-permute-start | bytes 1990664 | tf_op jit(solution)/shard_map/ppermute | solution.py:295
  64.7 2.1 %collective-permute-start.8 = (bf16[648,128]{1,0:T(8,128)(2,1)S(1)}, bf16[648,128]{1,0:T(8,128)(2,1)S(1)}, u32[]{:S(2)}, u32[]{:S(2)}) collective-permute-start(bf16[648,128]{1,0:T(8,128)(2,1)S(1)} %get-tuple-element.107.refs_0_), channel_id=1, source_target_pairs={{0,6},{1,3},{2,4},{3,1},{4,2},{5,7},{6,0},{7,5},{8,14},{9,11},{10,... | collective-permute-start | bytes 497672 | tf_op jit(solution)/shard_map/ppermute | solution.py:278
  66.7 5.0 %collective-permute-done.8.refs_1_ = bf16[648,128]{1,0:T(8,128)(2,1)S(1)} collective-permute-done((bf16[648,128]{1,0:T(8,128)(2,1)S(1)}, bf16[648,128]{1,0:T(8,128)(2,1)S(1)}, u32[]{:S(2)}, u32[]{:S(2)}) %collective-permute-start.8) | collective-permute-done | bytes 165920 | tf_op jit(solution)/shard_map/ppermute | solution.py:278
  72.5 3.3 %collective-permute-done.16.refs_1_ = bf16[648,768]{1,0:T(8,128)(2,1)S(1)} collective-permute-done((bf16[648,768]{1,0:T(8,128)(2,1)S(1)}, bf16[648,768]{1,0:T(8,128)(2,1)S(1)}, u32[]{:S(2)}, u32[]{:S(2)}) %collective-permute-start.16) | collective-permute-done | bytes 995360 | tf_op jit(solution)/shard_map/ppermute | solution.py:269
  76.8 2.0 collective-permute-done.14.refs_1_
  78.8 6.1 %collective-permute-done.15.refs_2_ = bf16[648,512]{1,0:T(8,128)(2,1)} collective-permute-done((bf16[648,512]{1,0:T(8,128)(2,1)S(1)}, bf16[648,512]{1,0:T(8,128)(2,1)}, u32[]{:S(2)}, u32[]{:S(2)}) %collective-permute-start.15) | collective-permute-done | bytes 663584 | tf_op jit(solution)/shard_map/ppermute | solution.py:295
  87.4 1.9 collective-permute-done.17.refs_5_.refs_3_
  90.3 4.1 %product1.6 = (bf16[648,256]{1,0:T(8,128)(2,1)S(1)}, bf16[648,256]{1,0:T(8,128)(2,1)S(1)}, bf16[648,512]{1,0:T(8,128)(2,1)S(1)}, f32[8,128]{1,0:T(8,128)S(1)}) custom-call(s32[2]{0:T(128)S(1)} %add_convert_fusion.1.refs_0_, bf16[648,648]{1,0:T(8,128)(2,1)S(1)} %copy-done.1, bf16[648,648]{1,0:T(8,128)(2,1)S(1)} %collective-permute-done.refs_2_, ...), custom_call_target="tpu_custom_call" | custom-call | flops 1000 | bytes 1000 | tf_op jit(solution)/shard_map/product1/pallas_call | solution.py:72
  95.2 2.4 %collective-permute-start.23 = (bf16[648,512]{1,0:T(8,128)(2,1)S(1)}, bf16[648,512]{1,0:T(8,128)(2,1)S(1)}, u32[]{:S(2)}, u32[]{:S(2)}) collective-permute-start(bf16[648,512]{1,0:T(8,128)(2,1)S(1)} %get-tuple-element.133), channel_id=1, source_target_pairs={{0,2},{1,7},{2,0},{3,5},{4,6},{5,3},{6,4},{7,1},{8,10},{9,15},{10,... | collective-permute-start | bytes 1990664 | tf_op jit(solution)/shard_map/ppermute | solution.py:269
  98.2 1.9 collective-permute-start.22
  100.3 14.5 %collective-permute-done.13.refs_1_ = bf16[648,256]{1,0:T(8,128)(2,1)S(1)} collective-permute-done((bf16[648,256]{1,0:T(8,128)(2,1)S(1)}, bf16[648,256]{1,0:T(8,128)(2,1)S(1)}, u32[]{:S(2)}, u32[]{:S(2)}) %collective-permute-start.13) | collective-permute-done | bytes 331808 | tf_op jit(solution)/shard_map/ppermute | solution.py:281
  123.9 4.1 %product1.7 = (bf16[648,256]{1,0:T(8,128)(2,1)S(1)}, bf16[648,256]{1,0:T(8,128)(2,1)S(1)}, bf16[648,512]{1,0:T(8,128)(2,1)S(1)}, f32[8,128]{1,0:T(8,128)S(1)}) custom-call(s32[2]{0:T(128)S(1)} %add_convert_fusion.2.refs_0_, bf16[648,648]{1,0:T(8,128)(2,1)S(1)} %copy-done.1, bf16[648,648]{1,0:T(8,128)(2,1)S(1)} %collective-permute-done.refs_2_, ...), custom_call_target="tpu_custom_call" | custom-call | flops 1000 | bytes 1000 | tf_op jit(solution)/shard_map/product1/pallas_call | solution.py:72
  128.0 2.5 %collective-permute-start.27 = (bf16[648,512]{1,0:T(8,128)(2,1)S(1)}, bf16[648,512]{1,0:T(8,128)(2,1)S(1)}, u32[]{:S(2)}, u32[]{:S(2)}) collective-permute-start(bf16[648,512]{1,0:T(8,128)(2,1)S(1)} %get-tuple-element.142), channel_id=1, source_target_pairs={{0,2},{1,7},{2,0},{3,5},{4,6},{5,3},{6,4},{7,1},{8,10},{9,15},{10,... | collective-permute-start | bytes 1990664 | tf_op jit(solution)/shard_map/ppermute | solution.py:269
  130.5 3.7 %collective-permute-done.20.refs_1_ = bf16[648,384]{1,0:T(8,128)(2,1)} collective-permute-done((bf16[648,384]{1,0:T(8,128)(2,1)}, bf16[648,384]{1,0:T(8,128)(2,1)}, u32[]{:S(2)}, u32[]{:S(2)}) %collective-permute-start.20) | collective-permute-done | bytes 497696 | tf_op jit(solution)/shard_map/ppermute | solution.py:275
  135.7 1.4 collective-permute-start.28
  137.1 10.3 %collective-permute-done.28.refs_2_ = bf16[648,256]{1,0:T(8,128)(2,1)S(1)} collective-permute-done((bf16[648,256]{1,0:T(8,128)(2,1)S(1)}, bf16[648,256]{1,0:T(8,128)(2,1)S(1)}, u32[]{:S(2)}, u32[]{:S(2)}) %collective-permute-start.28) | collective-permute-done | bytes 331808 | tf_op jit(solution)/shard_map/ppermute | solution.py:272
  147.5 1.4 collective-permute-start.31
  149.2 2.0 collective-permute-start.29
  151.2 2.9 %collective-permute-done.31.refs_1_ = bf16[648,256]{1,0:T(8,128)(2,1)S(1)} collective-permute-done((bf16[648,256]{1,0:T(8,128)(2,1)S(1)}, bf16[648,256]{1,0:T(8,128)(2,1)S(1)}, u32[]{:S(2)}, u32[]{:S(2)}) %collective-permute-start.31) | collective-permute-done | bytes 331808 | tf_op jit(solution)/shard_map/ppermute | solution.py:275
  154.2 1.4 collective-permute-start.33
  155.7 1.7 collective-permute-start.32
  157.5 6.2 %collective-permute-done.33.refs_1_ = bf16[648,256]{1,0:T(8,128)(2,1)S(1)} collective-permute-done((bf16[648,256]{1,0:T(8,128)(2,1)S(1)}, bf16[648,256]{1,0:T(8,128)(2,1)S(1)}, u32[]{:S(2)}, u32[]{:S(2)}) %collective-permute-start.33) | collective-permute-done | bytes 331808 | tf_op jit(solution)/shard_map/ppermute | solution.py:278
  163.8 1.8 collective-permute-start.35
  165.6 2.7 %collective-permute-start.34 = (bf16[648,512]{1,0:T(8,128)(2,1)S(1)}, bf16[648,512]{1,0:T(8,128)(2,1)S(1)}, u32[]{:S(2)}, u32[]{:S(2)}) collective-permute-start(bf16[648,512]{1,0:T(8,128)(2,1)S(1)} %get-tuple-element.162.refs_1_), channel_id=1, source_target_pairs={{0,2},{1,7},{2,0},{3,5},{4,6},{5,3},{6,4},{7,1},{8,10},{9,15},{10,... | collective-permute-start | bytes 1990664 | tf_op jit(solution)/shard_map/ppermute | solution.py:281
  168.3 2.5 %collective-permute-done.29.refs_2_ = bf16[648,768]{1,0:T(8,128)(2,1)S(1)} collective-permute-done((bf16[648,768]{1,0:T(8,128)(2,1)S(1)}, bf16[648,768]{1,0:T(8,128)(2,1)S(1)}, u32[]{:S(2)}, u32[]{:S(2)}) %collective-permute-start.29) | collective-permute-done | bytes 995360 | tf_op jit(solution)/shard_map/ppermute | solution.py:281
  170.8 3.4 %product2.10 = (f32[648,648]{1,0:T(8,128)S(1)}, f32[8,128]{1,0:T(8,128)S(1)}) custom-call(f32[648,648]{1,0:T(8,128)S(1)} %copy-done.13, bf16[648,768]{1,0:T(8,128)(2,1)S(1)} %get-tuple-element.148.refs_1_, bf16[648,768]{1,0:T(8,128)(2,1)S(1)} %collective-permute-done.29.refs_2_, bf16[648,512]{1,0:T(8,128)(2,1)} %collective-permute-done.10.refs_5_.refs_3_, ...), custom_call_target="tpu_custom_call" | custom-call | flops 1000 | bytes 1000 | tf_op jit(solution)/shard_map/product2/pallas_call | solution.py:72
  174.2 3.1 %product2.11 = (f32[648,648]{1,0:T(8,128)S(1)}, f32[8,128]{1,0:T(8,128)S(1)}) custom-call(f32[648,648]{1,0:T(8,128)S(1)} %copy-done.11, bf16[648,768]{1,0:T(8,128)(2,1)S(1)} %get-tuple-element.148.refs_1_, bf16[648,768]{1,0:T(8,128)(2,1)S(1)} %collective-permute-done.29.refs_2_, bf16[648,512]{1,0:T(8,128)(2,1)} %get-tuple-element.110.refs_4_.refs_3_, ...), custom_call_target="tpu_custom_call" | custom-call | flops 1000 | bytes 1000 | tf_op jit(solution)/shard_map/product2/pallas_call | solution.py:72
  177.4 2.1 %collective-permute-start.36 = (bf16[648,512]{1,0:T(8,128)(2,1)S(1)}, bf16[648,512]{1,0:T(8,128)(2,1)S(1)}, u32[]{:S(2)}, u32[]{:S(2)}) collective-permute-start(bf16[648,512]{1,0:T(8,128)(2,1)S(1)} %get-tuple-element.169.refs_1_), channel_id=1, source_target_pairs={{0,2},{1,7},{2,0},{3,5},{4,6},{5,3},{6,4},{7,1},{8,10},{9,15},{10,... | collective-permute-start | bytes 1990664 | tf_op jit(solution)/shard_map/ppermute | solution.py:281
  180.2 2.5 %product2.12 = (f32[648,648]{1,0:T(8,128)S(1)}, f32[8,128]{1,0:T(8,128)S(1)}) custom-call(f32[648,648]{1,0:T(8,128)S(1)} %get-tuple-element.163.refs_0_, bf16[648,512]{1,0:T(8,128)(2,1)S(1)} %get-tuple-element.162.refs_1_, bf16[648,512]{1,0:T(8,128)(2,1)S(1)} %collective-permute-done.34.refs_2_, bf16[648,512]{1,0:T(8,128)(2,1)} %collective-permute-done.17.refs_5_.refs_3_, ...), custom_call_target="tpu_custom_call" | custom-call | flops 1000 | bytes 1000 | tf_op jit(solution)/shard_map/product2/pallas_call | solution.py:72
  182.7 2.5 %product2.13 = (f32[648,648]{1,0:T(8,128)S(1)}, f32[8,128]{1,0:T(8,128)S(1)}) custom-call(f32[648,648]{1,0:T(8,128)S(1)} %get-tuple-element.161.refs_0_, bf16[648,512]{1,0:T(8,128)(2,1)S(1)} %get-tuple-element.162.refs_1_, bf16[648,512]{1,0:T(8,128)(2,1)S(1)} %collective-permute-done.34.refs_2_, bf16[648,512]{1,0:T(8,128)(2,1)} %get-tuple-element.120.refs_4_.refs_3_, ...), custom_call_target="tpu_custom_call" | custom-call | flops 1000 | bytes 1000 | tf_op jit(solution)/shard_map/product2/pallas_call | solution.py:72
  185.3 3.2 %collective-permute-done.36.refs_2_ = bf16[648,512]{1,0:T(8,128)(2,1)S(1)} collective-permute-done((bf16[648,512]{1,0:T(8,128)(2,1)S(1)}, bf16[648,512]{1,0:T(8,128)(2,1)S(1)}, u32[]{:S(2)}, u32[]{:S(2)}) %collective-permute-start.36) | collective-permute-done | bytes 663584 | tf_op jit(solution)/shard_map/ppermute | solution.py:281
  188.5 2.5 %product2.14 = (bf16[648,648]{1,0:T(8,128)(2,1)S(1)}, f32[8,128]{1,0:T(8,128)S(1)}) custom-call(f32[648,648]{1,0:T(8,128)S(1)} %get-tuple-element.170.refs_0_, bf16[648,512]{1,0:T(8,128)(2,1)S(1)} %get-tuple-element.169.refs_1_, bf16[648,512]{1,0:T(8,128)(2,1)S(1)} %collective-permute-done.36.refs_2_, ...), custom_call_target="tpu_custom_call" | custom-call | flops 1000 | bytes 1000 | tf_op jit(solution)/shard_map/product2/pallas_call | solution.py:72
  191.0 4.7 %collective-permute-start.37 = (bf16[648,648]{1,0:T(8,128)(2,1)S(1)}, bf16[648,648]{1,0:T(8,128)(2,1)S(1)}, u32[]{:S(2)}, u32[]{:S(2)}) collective-permute-start(bf16[648,648]{1,0:T(8,128)(2,1)S(1)} %get-tuple-element.174), channel_id=1, source_target_pairs={{0,1},{1,0},{2,3},{3,2},{4,5},{5,4},{6,7},{7,6},{8,9},{9,8},{10,11... | collective-permute-start | bytes 2519432 | tf_op jit(solution)/shard_map/ppermute | solution.py:286
  195.9 2.5 %product2.15 = (f32[648,648]{1,0:T(8,128)S(1)}, f32[8,128]{1,0:T(8,128)S(1)}) custom-call(f32[648,648]{1,0:T(8,128)S(1)} %get-tuple-element.168.refs_0_, bf16[648,512]{1,0:T(8,128)(2,1)S(1)} %get-tuple-element.169.refs_1_, bf16[648,512]{1,0:T(8,128)(2,1)S(1)} %collective-permute-done.36.refs_2_, bf16[648,512]{1,0:T(8,128)(2,1)} %get-tuple-element.136.refs_4_.refs_3_, ...), custom_call_target="tpu_custom_call" | custom-call | flops 1000 | bytes 1000 | tf_op jit(solution)/shard_map/product2/pallas_call | solution.py:72
  198.4 2.9 %finish.1 = (f32[648,1296]{1,0:T(8,128)}, f32[8,128]{1,0:T(8,128)}) custom-call(s32[1]{0:T(128)} %bitcast.refs_0_, f32[648,1]{1,0:T(8,128)S(1)} %mul.34.refs_1_, f32[648,648]{1,0:T(8,128)S(1)} %get-tuple-element.173.refs_2_, bf16[648,648]{1,0:T(8,128)(2,1)S(1)} %collective-permute-done.37.refs_3_, f32[8,128]{1,0:T(8,128)S(1)} %get-tuple-element.175.refs_4_), custom_call_target="tpu_custom_call" | custom-call | flops 1000 | bytes 1000 | tf_op jit(solution)/shard_map/finish/pallas_call | solution.py:72
  (140 shorter events, 33.2 us)
Async XLA Ops:
  3.7 15.7 %copy-start.4 = (bf16[648,512]{1,0:T(8,128)(2,1)}, bf16[648,512]{1,0:T(8,128)(2,1)S(1)}, u32[]{:S(2)}) copy-start(bf16[648,512]{1,0:T(8,128)(2,1)S(1)} %get-tuple-element.96.refs_4_.refs_2_) | copy-start | bytes 1990660
  8.3 11.1 %collective-permute-start = (bf16[648,648]{1,0:T(8,128)(2,1)}, bf16[648,648]{1,0:T(8,128)(2,1)S(1)}, u32[]{:S(2)}, u32[]{:S(2)}) collective-permute-start(bf16[648,648]{1,0:T(8,128)(2,1)} %get-tuple-element.93), channel_id=1, source_target_pairs={{0,1},{1,0},{2,3},{3,2},{4,5},{5,4},{6,7},{7,6},{8,9},{9,8},{10,11... | collective-permute-start | bytes 2519432 | tf_op jit(solution)/shard_map/ppermute | solution.py:158
  9.8 9.6 %collective-permute-start.1 = (bf16[648,512]{1,0:T(8,128)(2,1)S(1)}, bf16[648,512]{1,0:T(8,128)(2,1)S(1)}, u32[]{:S(2)}, u32[]{:S(2)}) collective-permute-start(bf16[648,512]{1,0:T(8,128)(2,1)S(1)} %get-tuple-element.96.refs_4_.refs_2_), channel_id=1, source_target_pairs={{0,1},{1,0},{2,3},{3,2},{4,5},{5,4},{6,7},{7,6},{8,9},{9,8},{10,11... | collective-permute-start | bytes 1990664 | tf_op jit(solution)/shard_map/ppermute | solution.py:121
  9.9 28.0 %collective-permute-start.5 = (bf16[648,512]{1,0:T(8,128)(2,1)S(1)}, bf16[648,512]{1,0:T(8,128)(2,1)S(1)}, u32[]{:S(2)}, u32[]{:S(2)}) collective-permute-start(bf16[648,512]{1,0:T(8,128)(2,1)S(1)} %get-tuple-element.96.refs_4_.refs_2_), channel_id=1, source_target_pairs={{0,64},{16,80},{32,96},{48,112},{64,0},{80,16},{96,32},{112,48},{1... | collective-permute-start | bytes 1990664 | tf_op jit(solution)/shard_map/ppermute | solution.py:124
  12.9 25.0 %collective-permute-start.6 = (bf16[648,512]{1,0:T(8,128)(2,1)S(1)}, bf16[648,512]{1,0:T(8,128)(2,1)}, u32[]{:S(2)}, u32[]{:S(2)}) collective-permute-start(bf16[648,512]{1,0:T(8,128)(2,1)S(1)} %get-tuple-element.96.refs_4_.refs_2_), channel_id=1, source_target_pairs={{0,16},{16,32},{32,48},{48,0},{64,80},{80,96},{96,112},{112,64},{1... | collective-permute-start | bytes 1990664 | tf_op jit(solution)/shard_map/ppermute | solution.py:122
  14.5 23.4 %collective-permute-start.7 = (bf16[648,512]{1,0:T(8,128)(2,1)S(1)}, bf16[648,512]{1,0:T(8,128)(2,1)}, u32[]{:S(2)}, u32[]{:S(2)}) collective-permute-start(bf16[648,512]{1,0:T(8,128)(2,1)S(1)} %get-tuple-element.96.refs_4_.refs_2_), channel_id=1, source_target_pairs={{0,48},{16,0},{32,16},{48,32},{64,112},{80,64},{96,80},{112,96},{1... | collective-permute-start | bytes 1990664 | tf_op jit(solution)/shard_map/ppermute | solution.py:123
  23.2 7.7 %collective-permute-start.2 = (bf16[648,256]{1,0:T(8,128)(2,1)S(1)}, bf16[648,256]{1,0:T(8,128)(2,1)S(1)}, u32[]{:S(2)}, u32[]{:S(2)}) collective-permute-start(bf16[648,256]{1,0:T(8,128)(2,1)S(1)} %get-tuple-element.99), channel_id=1, source_target_pairs={{0,2},{1,7},{2,0},{3,5},{4,6},{5,3},{6,4},{7,1},{8,10},{9,15},{10,... | collective-permute-start | bytes 995336 | tf_op jit(solution)/shard_map/ppermute | solution.py:269
  30.9 19.8 %copy-start.1 = (bf16[648,648]{1,0:T(8,128)(2,1)S(1)}, bf16[648,648]{1,0:T(8,128)(2,1)}, u32[]{:S(2)}) copy-start(bf16[648,648]{1,0:T(8,128)(2,1)} %get-tuple-element.92.refs_1_) | copy-start | bytes 2519428
  30.9 6.9 %collective-permute-start.3 = (bf16[648,128]{1,0:T(8,128)(2,1)S(1)}, bf16[648,128]{1,0:T(8,128)(2,1)S(1)}, u32[]{:S(2)}, u32[]{:S(2)}) collective-permute-start(bf16[648,128]{1,0:T(8,128)(2,1)S(1)} %get-tuple-element.102), channel_id=1, source_target_pairs={{0,6},{1,3},{2,4},{3,1},{4,2},{5,7},{6,0},{7,5},{8,14},{9,11},{10,... | collective-permute-start | bytes 497672 | tf_op jit(solution)/shard_map/ppermute | solution.py:272
  31.0 18.4 %collective-permute-start.9 = (bf16[648,512]{1,0:T(8,128)(2,1)}, bf16[648,512]{1,0:T(8,128)(2,1)}, u32[]{:S(2)}, u32[]{:S(2)}) collective-permute-start(bf16[648,512]{1,0:T(8,128)(2,1)} %refs_1_.3), channel_id=1, source_target_pairs={{0,0},{1,1},{2,18},{3,19},{4,36},{5,37},{6,54},{7,55},{8,64},{9,65... | collective-permute-start | bytes 1990664 | tf_op jit(solution)/shard_map/ppermute | solution.py:119
  39.9 10.8 %collective-permute-start.10 = (bf16[648,512]{1,0:T(8,128)(2,1)}, bf16[648,512]{1,0:T(8,128)(2,1)}, u32[]{:S(2)}, u32[]{:S(2)}) collective-permute-start(bf16[648,512]{1,0:T(8,128)(2,1)} %get-tuple-element.110.refs_4_.refs_3_), channel_id=1, source_target_pairs={{0,1},{1,0},{2,3},{3,2},{4,5},{5,4},{6,7},{7,6},{8,9},{9,8},{10,11... | collective-permute-start | bytes 1990664 | tf_op jit(solution)/shard_map/ppermute | solution.py:293
  43.0 7.7 %collective-permute-start.11 = (bf16[648,512]{1,0:T(8,128)(2,1)}, bf16[648,512]{1,0:T(8,128)(2,1)}, u32[]{:S(2)}, u32[]{:S(2)}) collective-permute-start(bf16[648,512]{1,0:T(8,128)(2,1)} %get-tuple-element.111.refs_6_.refs_4_), channel_id=1, source_target_pairs={{0,1},{1,0},{2,3},{3,2},{4,5},{5,4},{6,7},{7,6},{8,9},{9,8},{10,11... | collective-permute-start | bytes 1990664 | tf_op jit(solution)/shard_map/ppermute | solution.py:293
  43.0 7.7 %collective-permute-start.12 = (bf16[648,512]{1,0:T(8,128)(2,1)S(1)}, bf16[648,512]{1,0:T(8,128)(2,1)}, u32[]{:S(2)}, u32[]{:S(2)}) collective-permute-start(bf16[648,512]{1,0:T(8,128)(2,1)S(1)} %get-tuple-element.112.refs_8_.refs_5_), channel_id=1, source_target_pairs={{0,1},{1,0},{2,3},{3,2},{4,5},{5,4},{6,7},{7,6},{8,9},{9,8},{10,11... | collective-permute-start | bytes 1990664 | tf_op jit(solution)/shard_map/ppermute | solution.py:293
  43.5 5.9 %collective-permute-start.4 = (bf16[648,128]{1,0:T(8,128)(2,1)S(1)}, bf16[648,128]{1,0:T(8,128)(2,1)S(1)}, u32[]{:S(2)}, u32[]{:S(2)}) collective-permute-start(bf16[648,128]{1,0:T(8,128)(2,1)S(1)} %get-tuple-element.104.refs_0_), channel_id=1, source_target_pairs={{0,8},{1,9},{2,10},{3,11},{4,12},{5,13},{6,14},{7,15},{8,0},{9,1},... | collective-permute-start | bytes 497672 | tf_op jit(solution)/shard_map/ppermute | solution.py:275
  56.7 19.1 %collective-permute-start.16 = (bf16[648,768]{1,0:T(8,128)(2,1)S(1)}, bf16[648,768]{1,0:T(8,128)(2,1)S(1)}, u32[]{:S(2)}, u32[]{:S(2)}) collective-permute-start(bf16[648,768]{1,0:T(8,128)(2,1)S(1)} %get-tuple-element.117), channel_id=1, source_target_pairs={{0,2},{1,7},{2,0},{3,5},{4,6},{5,3},{6,4},{7,1},{8,10},{9,15},{10,... | collective-permute-start | bytes 2985992 | tf_op jit(solution)/shard_map/ppermute | solution.py:269
  62.0 16.8 %collective-permute-start.14 = (bf16[648,512]{1,0:T(8,128)(2,1)S(1)}, bf16[648,512]{1,0:T(8,128)(2,1)}, u32[]{:S(2)}, u32[]{:S(2)}) collective-permute-start(bf16[648,512]{1,0:T(8,128)(2,1)S(1)} %get-tuple-element.112.refs_8_.refs_5_), channel_id=1, source_target_pairs={{0,16},{16,32},{32,48},{48,0},{64,80},{80,96},{96,112},{112,64},{1... | collective-permute-start | bytes 1990664 | tf_op jit(solution)/shard_map/ppermute | solution.py:294
  62.0 22.9 %collective-permute-start.15 = (bf16[648,512]{1,0:T(8,128)(2,1)S(1)}, bf16[648,512]{1,0:T(8,128)(2,1)}, u32[]{:S(2)}, u32[]{:S(2)}) collective-permute-start(bf16[648,512]{1,0:T(8,128)(2,1)S(1)} %get-tuple-element.112.refs_8_.refs_5_), channel_id=1, source_target_pairs={{0,48},{16,0},{32,16},{48,32},{64,112},{80,64},{96,80},{112,96},{1... | collective-permute-start | bytes 1990664 | tf_op jit(solution)/shard_map/ppermute | solution.py:295
  64.7 7.0 %collective-permute-start.8 = (bf16[648,128]{1,0:T(8,128)(2,1)S(1)}, bf16[648,128]{1,0:T(8,128)(2,1)S(1)}, u32[]{:S(2)}, u32[]{:S(2)}) collective-permute-start(bf16[648,128]{1,0:T(8,128)(2,1)S(1)} %get-tuple-element.107.refs_0_), channel_id=1, source_target_pairs={{0,6},{1,3},{2,4},{3,1},{4,2},{5,7},{6,0},{7,5},{8,14},{9,11},{10,... | collective-permute-start | bytes 497672 | tf_op jit(solution)/shard_map/ppermute | solution.py:278
  86.9 2.5 %collective-permute-start.17 = (bf16[648,512]{1,0:T(8,128)(2,1)}, bf16[648,512]{1,0:T(8,128)(2,1)}, u32[]{:S(2)}, u32[]{:S(2)}) collective-permute-start(bf16[648,512]{1,0:T(8,128)(2,1)} %get-tuple-element.120.refs_4_.refs_3_), channel_id=1, source_target_pairs={{0,1},{1,0},{2,3},{3,2},{4,5},{5,4},{6,7},{7,6},{8,9},{9,8},{10,11... | collective-permute-start | bytes 1990664 | tf_op jit(solution)/shard_map/ppermute | solution.py:302
  86.9 3.4 %collective-permute-start.18 = (bf16[648,512]{1,0:T(8,128)(2,1)}, bf16[648,512]{1,0:T(8,128)(2,1)}, u32[]{:S(2)}, u32[]{:S(2)}) collective-permute-start(bf16[648,512]{1,0:T(8,128)(2,1)} %get-tuple-element.121.refs_6_.refs_4_), channel_id=1, source_target_pairs={{0,1},{1,0},{2,3},{3,2},{4,5},{5,4},{6,7},{7,6},{8,9},{9,8},{10,11... | collective-permute-start | bytes 1990664 | tf_op jit(solution)/shard_map/ppermute | solution.py:302
  90.3 24.5 %copy-start.7 = (bf16[648,512]{1,0:T(8,128)(2,1)S(1)}, bf16[648,512]{1,0:T(8,128)(2,1)}, u32[]{:S(2)}) copy-start(bf16[648,512]{1,0:T(8,128)(2,1)} %copy-done.6) | copy-start | bytes 1990660
  90.3 26.6 %copy-start.5 = (bf16[648,512]{1,0:T(8,128)(2,1)S(1)}, bf16[648,512]{1,0:T(8,128)(2,1)}, u32[]{:S(2)}) copy-start(bf16[648,512]{1,0:T(8,128)(2,1)} %copy-done.4) | copy-start | bytes 1990660
  95.2 22.5 %copy-start.3 = (bf16[648,768]{1,0:T(8,128)(2,1)S(1)}, bf16[648,768]{1,0:T(8,128)(2,1)}, u32[]{:S(2)}) copy-start(bf16[648,768]{1,0:T(8,128)(2,1)} %copy-done.2) | copy-start | bytes 2985988
  95.2 22.5 %copy-start.20 = (bf16[648,384]{1,0:T(8,128)(2,1)S(1)}, bf16[648,384]{1,0:T(8,128)(2,1)}, u32[]{:S(2)}) copy-start(bf16[648,384]{1,0:T(8,128)(2,1)} %copy-done.19) | copy-start | bytes 1492996
  95.2 23.7 %collective-permute-start.23 = (bf16[648,512]{1,0:T(8,128)(2,1)S(1)}, bf16[648,512]{1,0:T(8,128)(2,1)S(1)}, u32[]{:S(2)}, u32[]{:S(2)}) collective-permute-start(bf16[648,512]{1,0:T(8,128)(2,1)S(1)} %get-tuple-element.133), channel_id=1, source_target_pairs={{0,2},{1,7},{2,0},{3,5},{4,6},{5,3},{6,4},{7,1},{8,10},{9,15},{10,... | collective-permute-start | bytes 1990664 | tf_op jit(solution)/shard_map/ppermute | solution.py:269
  97.6 22.2 %collective-permute-start.21 = (bf16[648,512]{1,0:T(8,128)(2,1)S(1)}, bf16[648,512]{1,0:T(8,128)(2,1)}, u32[]{:S(2)}, u32[]{:S(2)}) collective-permute-start(bf16[648,512]{1,0:T(8,128)(2,1)S(1)} %copy-done.26), channel_id=1, source_target_pairs={{0,16},{1,49},{2,18},{3,51},{4,20},{5,53},{6,22},{7,55},{8,24},{9,... | collective-permute-start | bytes 1990664 | tf_op jit(solution)/shard_map/ppermute | solution.py:296
  98.2 21.6 %collective-permute-start.22 = (bf16[648,512]{1,0:T(8,128)(2,1)S(1)}, bf16[648,512]{1,0:T(8,128)(2,1)}, u32[]{:S(2)}, u32[]{:S(2)}) collective-permute-start(bf16[648,512]{1,0:T(8,128)(2,1)S(1)} %copy-done.28), channel_id=1, source_target_pairs={{0,16},{1,49},{2,18},{3,51},{4,20},{5,53},{6,22},{7,55},{8,24},{9,... | collective-permute-start | bytes 1990664 | tf_op jit(solution)/shard_map/ppermute | solution.py:303
  100.2 17.5 %collective-permute-start.19 = (bf16[648,384]{1,0:T(8,128)(2,1)S(1)}, bf16[648,384]{1,0:T(8,128)(2,1)S(1)}, u32[]{:S(2)}, u32[]{:S(2)}) collective-permute-start(bf16[648,384]{1,0:T(8,128)(2,1)S(1)} %copy-done.30), channel_id=1, source_target_pairs={{0,6},{1,3},{2,4},{3,1},{4,2},{5,7},{6,0},{7,5},{8,14},{9,11},{10,... | collective-permute-start | bytes 1493000 | tf_op jit(solution)/shard_map/ppermute | solution.py:272
  100.2 14.6 %collective-permute-start.13 = (bf16[648,256]{1,0:T(8,128)(2,1)S(1)}, bf16[648,256]{1,0:T(8,128)(2,1)S(1)}, u32[]{:S(2)}, u32[]{:S(2)}) collective-permute-start(bf16[648,256]{1,0:T(8,128)(2,1)S(1)} %copy-done.15), channel_id=1, source_target_pairs={{0,2},{1,7},{2,0},{3,5},{4,6},{5,3},{6,4},{7,1},{8,10},{9,15},{10,... | collective-permute-start | bytes 995336 | tf_op jit(solution)/shard_map/ppermute | solution.py:281
  120.5 2.5 %collective-permute-start.24 = (bf16[648,512]{1,0:T(8,128)(2,1)}, bf16[648,512]{1,0:T(8,128)(2,1)}, u32[]{:S(2)}, u32[]{:S(2)}) collective-permute-start(bf16[648,512]{1,0:T(8,128)(2,1)} %get-tuple-element.136.refs_4_.refs_3_), channel_id=1, source_target_pairs={{0,1},{1,0},{2,3},{3,2},{4,5},{5,4},{6,7},{7,6},{8,9},{9,8},{10,11... | collective-permute-start | bytes 1990664 | tf_op jit(solution)/shard_map/ppermute | solution.py:308
  120.6 3.3 %collective-permute-start.25 = (bf16[648,512]{1,0:T(8,128)(2,1)}, bf16[648,512]{1,0:T(8,128)(2,1)}, u32[]{:S(2)}, u32[]{:S(2)}) collective-permute-start(bf16[648,512]{1,0:T(8,128)(2,1)} %get-tuple-element.137.refs_6_.refs_4_), channel_id=1, source_target_pairs={{0,1},{1,0},{2,3},{3,2},{4,5},{5,4},{6,7},{7,6},{8,9},{9,8},{10,11... | collective-permute-start | bytes 1990664 | tf_op jit(solution)/shard_map/ppermute | solution.py:308
  121.0 13.2 %collective-permute-start.20 = (bf16[648,384]{1,0:T(8,128)(2,1)}, bf16[648,384]{1,0:T(8,128)(2,1)}, u32[]{:S(2)}, u32[]{:S(2)}) collective-permute-start(bf16[648,384]{1,0:T(8,128)(2,1)} %get-tuple-element.129.refs_0_), channel_id=1, source_target_pairs={{0,8},{1,9},{2,10},{3,11},{4,12},{5,13},{6,14},{7,15},{8,0},{9,1},... | collective-permute-start | bytes 1493000 | tf_op jit(solution)/shard_map/ppermute | solution.py:275
  123.9 11.7 %copy-start.32 = (bf16[648,256]{1,0:T(8,128)(2,1)S(1)}, bf16[648,256]{1,0:T(8,128)(2,1)}, u32[]{:S(2)}) copy-start(bf16[648,256]{1,0:T(8,128)(2,1)} %copy-done.31) | copy-start | bytes 995332
  123.9 23.5 %copy-start.9 = (bf16[648,512]{1,0:T(8,128)(2,1)S(1)}, bf16[648,512]{1,0:T(8,128)(2,1)}, u32[]{:S(2)}) copy-start(bf16[648,512]{1,0:T(8,128)(2,1)} %copy-done.8) | copy-start | bytes 1990660
  123.9 23.5 %copy-start.22 = (bf16[648,256]{1,0:T(8,128)(2,1)S(1)}, bf16[648,256]{1,0:T(8,128)(2,1)}, u32[]{:S(2)}) copy-start(bf16[648,256]{1,0:T(8,128)(2,1)} %copy-done.21) | copy-start | bytes 995332
  128.0 20.9 %collective-permute-start.27 = (bf16[648,512]{1,0:T(8,128)(2,1)S(1)}, bf16[648,512]{1,0:T(8,128)(2,1)S(1)}, u32[]{:S(2)}, u32[]{:S(2)}) collective-permute-start(bf16[648,512]{1,0:T(8,128)(2,1)S(1)} %get-tuple-element.142), channel_id=1, source_target_pairs={{0,2},{1,7},{2,0},{3,5},{4,6},{5,3},{6,4},{7,1},{8,10},{9,15},{10,... | collective-permute-start | bytes 1990664 | tf_op jit(solution)/shard_map/ppermute | solution.py:269
  135.6 13.5 %collective-permute-start.26 = (bf16[648,384]{1,0:T(8,128)(2,1)S(1)}, bf16[648,384]{1,0:T(8,128)(2,1)S(1)}, u32[]{:S(2)}, u32[]{:S(2)}) collective-permute-start(bf16[648,384]{1,0:T(8,128)(2,1)S(1)} %get-tuple-element.140.refs_0_), channel_id=1, source_target_pairs={{0,6},{1,3},{2,4},{3,1},{4,2},{5,7},{6,0},{7,5},{8,14},{9,11},{10,... | collective-permute-start | bytes 1493000 | tf_op jit(solution)/shard_map/ppermute | solution.py:278
  135.7 11.7 %collective-permute-start.28 = (bf16[648,256]{1,0:T(8,128)(2,1)S(1)}, bf16[648,256]{1,0:T(8,128)(2,1)S(1)}, u32[]{:S(2)}, u32[]{:S(2)}) collective-permute-start(bf16[648,256]{1,0:T(8,128)(2,1)S(1)} %copy-done.32), channel_id=1, source_target_pairs={{0,6},{1,3},{2,4},{3,1},{4,2},{5,7},{6,0},{7,5},{8,14},{9,11},{10,... | collective-permute-start | bytes 995336 | tf_op jit(solution)/shard_map/ppermute | solution.py:272
  147.5 6.6 %collective-permute-start.31 = (bf16[648,256]{1,0:T(8,128)(2,1)S(1)}, bf16[648,256]{1,0:T(8,128)(2,1)S(1)}, u32[]{:S(2)}, u32[]{:S(2)}) collective-permute-start(bf16[648,256]{1,0:T(8,128)(2,1)S(1)} %get-tuple-element.152.refs_0_), channel_id=1, source_target_pairs={{0,8},{1,9},{2,10},{3,11},{4,12},{5,13},{6,14},{7,15},{8,0},{9,1},... | collective-permute-start | bytes 995336 | tf_op jit(solution)/shard_map/ppermute | solution.py:275
  149.0 6.6 %collective-permute-start.30 = (bf16[648,256]{1,0:T(8,128)(2,1)S(1)}, bf16[648,256]{1,0:T(8,128)(2,1)S(1)}, u32[]{:S(2)}, u32[]{:S(2)}) collective-permute-start(bf16[648,256]{1,0:T(8,128)(2,1)S(1)} %get-tuple-element.151), channel_id=1, source_target_pairs={{0,6},{1,3},{2,4},{3,1},{4,2},{5,7},{6,0},{7,5},{8,14},{9,11},{10,... | collective-permute-start | bytes 995336 | tf_op jit(solution)/shard_map/ppermute | solution.py:272
  149.1 21.7 %copy-start.13 = (f32[648,648]{1,0:T(8,128)S(1)}, f32[648,648]{1,0:T(8,128)}, u32[]{:S(2)}) copy-start(f32[648,648]{1,0:T(8,128)} %copy-done.12) | copy-start | bytes 5038852
  149.2 21.6 %collective-permute-start.29 = (bf16[648,768]{1,0:T(8,128)(2,1)S(1)}, bf16[648,768]{1,0:T(8,128)(2,1)S(1)}, u32[]{:S(2)}, u32[]{:S(2)}) collective-permute-start(bf16[648,768]{1,0:T(8,128)(2,1)S(1)} %get-tuple-element.148.refs_1_), channel_id=1, source_target_pairs={{0,2},{1,7},{2,0},{3,5},{4,6},{5,3},{6,4},{7,1},{8,10},{9,15},{10,... | collective-permute-start | bytes 2985992 | tf_op jit(solution)/shard_map/ppermute | solution.py:281
  154.2 9.5 %collective-permute-start.33 = (bf16[648,256]{1,0:T(8,128)(2,1)S(1)}, bf16[648,256]{1,0:T(8,128)(2,1)S(1)}, u32[]{:S(2)}, u32[]{:S(2)}) collective-permute-start(bf16[648,256]{1,0:T(8,128)(2,1)S(1)} %get-tuple-element.156.refs_0_), channel_id=1, source_target_pairs={{0,6},{1,3},{2,4},{3,1},{4,2},{5,7},{6,0},{7,5},{8,14},{9,11},{10,... | collective-permute-start | bytes 995336 | tf_op jit(solution)/shard_map/ppermute | solution.py:278
  155.7 8.0 %collective-permute-start.32 = (bf16[648,256]{1,0:T(8,128)(2,1)S(1)}, bf16[648,256]{1,0:T(8,128)(2,1)S(1)}, u32[]{:S(2)}, u32[]{:S(2)}) collective-permute-start(bf16[648,256]{1,0:T(8,128)(2,1)S(1)} %get-tuple-element.155.refs_0_), channel_id=1, source_target_pairs={{0,8},{1,9},{2,10},{3,11},{4,12},{5,13},{6,14},{7,15},{8,0},{9,1},... | collective-permute-start | bytes 995336 | tf_op jit(solution)/shard_map/ppermute | solution.py:275
  163.8 13.5 %collective-permute-start.35 = (bf16[648,256]{1,0:T(8,128)(2,1)S(1)}, bf16[648,256]{1,0:T(8,128)(2,1)S(1)}, u32[]{:S(2)}, u32[]{:S(2)}) collective-permute-start(bf16[648,256]{1,0:T(8,128)(2,1)S(1)} %get-tuple-element.164.refs_0_), channel_id=1, source_target_pairs={{0,6},{1,3},{2,4},{3,1},{4,2},{5,7},{6,0},{7,5},{8,14},{9,11},{10,... | collective-permute-start | bytes 995336 | tf_op jit(solution)/shard_map/ppermute | solution.py:278
  165.6 14.5 %collective-permute-start.34 = (bf16[648,512]{1,0:T(8,128)(2,1)S(1)}, bf16[648,512]{1,0:T(8,128)(2,1)S(1)}, u32[]{:S(2)}, u32[]{:S(2)}) collective-permute-start(bf16[648,512]{1,0:T(8,128)(2,1)S(1)} %get-tuple-element.162.refs_1_), channel_id=1, source_target_pairs={{0,2},{1,7},{2,0},{3,5},{4,6},{5,3},{6,4},{7,1},{8,10},{9,15},{10,... | collective-permute-start | bytes 1990664 | tf_op jit(solution)/shard_map/ppermute | solution.py:281
  177.4 11.1 %collective-permute-start.36 = (bf16[648,512]{1,0:T(8,128)(2,1)S(1)}, bf16[648,512]{1,0:T(8,128)(2,1)S(1)}, u32[]{:S(2)}, u32[]{:S(2)}) collective-permute-start(bf16[648,512]{1,0:T(8,128)(2,1)S(1)} %get-tuple-element.169.refs_1_), channel_id=1, source_target_pairs={{0,2},{1,7},{2,0},{3,5},{4,6},{5,3},{6,4},{7,1},{8,10},{9,15},{10,... | collective-permute-start | bytes 1990664 | tf_op jit(solution)/shard_map/ppermute | solution.py:281
  191.0 7.4 %collective-permute-start.37 = (bf16[648,648]{1,0:T(8,128)(2,1)S(1)}, bf16[648,648]{1,0:T(8,128)(2,1)S(1)}, u32[]{:S(2)}, u32[]{:S(2)}) collective-permute-start(bf16[648,648]{1,0:T(8,128)(2,1)S(1)} %get-tuple-element.174), channel_id=1, source_target_pairs={{0,1},{1,0},{2,3},{3,2},{4,5},{5,4},{6,7},{7,6},{8,9},{9,8},{10,11... | collective-permute-start | bytes 2519432 | tf_op jit(solution)/shard_map/ppermute | solution.py:286
  (24 other events, 74.5 us)

commit v3 on v2

--- a/solution.py
+++ b/solution.py
@@ -11,9 +11,11 @@
 BF16 = jnp.bfloat16
 X, Z = 4, 4
 Q = 128
-CHUNKS = (((0, 0),), ((0, 3), (0, 1), (1, 0)), ((1, 3), (1, 1)), ((0, 2), (1, 2)))
+CHUNKS = (((0, 0), (0, 3), (0, 1), (1, 0)), ((1, 3), (1, 1)), ((0, 2), (1, 2)))
 STEPS = (
-    "M0 S0 Y0 G0 R0 M1 F0 S1 G1 M2 T0 Y1 S2 G2 M3 R1 Y2 S3 F1 R2 Y3 F2 R3 T1 F3 T2 T3".split()
+    "G0", "G3", "M0", "G1", "M1", "S0", "G2", "Y0", "M2",
+    "S1", "S2", "Y1", "R0", "Y2", "F0", "R1", "F1", "R2",
+    "F2", "T0", "T1", "T2",
 )
 
 
@@ -58,6 +60,7 @@
 class Chain:
     def __init__(self):
         self.token = None
+        self.step = ""
 
     def __call__(self, name, body, outs, args, specs, out_specs=None, aliases=None, scratch=(), mib=4):
         given = self.token is not None
@@ -78,7 +81,7 @@
             scratch_shapes=list(scratch),
             compiler_params=pltpu.CompilerParams(vmem_limit_bytes=mib * 1024 * 1024),
             cost_estimate=pl.CostEstimate(flops=1000, bytes_accessed=1000, transcendentals=0),
-            name=name,
+            name=self.step + name,
         )(*args, *([self.token] if given else []))
         self.token = res[-1]
         return res[:-1]
@@ -97,23 +100,27 @@
 
 
 def on_device(coords, curvature, weight, polar, forces):
-    i, j = lax.axis_index("cfg"), lax.axis_index("mode")
-    yh, z = i // Z, i % Z
-    k, x, chip, yl = j % 2, (j // 2) % X, j // 2, j // (2 * X)
     rows = coords.shape[0]
     run = Chain()
 
-    second, first = jnp.where(k == 0, 3, 1), jnp.where(k == 0, 1, 3)
-    order = jnp.stack([x, x ^ second, x ^ first, x ^ 2]).astype(jnp.int32)
-    core = jnp.reshape(k, (1,)).astype(jnp.int32)
+    def place():
+        i, j = lax.axis_index("cfg"), lax.axis_index("mode")
+        return i, j // 2, j % 2
+
+    def pieces():
+        _, chip, k = place()
+        x = chip % X
+        return x, x ^ (3 - 2 * k), x ^ (1 + 2 * k), x ^ 2
+
+    def columns(piece):
+        return pl.ds(pl.multiple_of(piece * Q, Q), Q)
 
     def arrange(v):
         def body(ins, outs, _):
-            for s in range(4):
-                at = pl.multiple_of(ins[0][s] * Q, Q)
-                outs[0][:, s * Q : (s + 1) * Q] = ins[1][:, pl.ds(at, Q)]
-
-        return run("arrange", body, [like(v)], [order, v], [SM, VM])[0]
+            for s, p in enumerate(pieces()):
+                outs[0][:, s * Q : (s + 1) * Q] = ins[0][:, columns(p)]
+
+        return run("arrange", body, [like(v)], [v], [VM])[0]
 
     unit, other = {}, {}
     f_far = lax.ppermute(forces, ("cfg", "mode"), FORCES)
@@ -126,58 +133,63 @@
     window = 6 * 128
 
     def slice_polar(ins, outs, scratch):
-        at, scale, source = ins
+        scale, source = ins
+        i, _, k = place()
         wide_t, narrow, sems = scratch
         moves = []
+        begins = [(2 * i + 1 - k) * rows, (2 * i + k) * rows]
         for h in range(2):
-            begin = pl.multiple_of(at[2 * h] * 128, 128)
+            begin = pl.multiple_of(begins[h] // 128 * 128, 128)
             moves.append(pltpu.make_async_copy(source.at[:, pl.ds(begin, window)], narrow.at[h], sems.at[h]))
             moves[-1].start()
         for h in range(2):
             moves[h].wait()
-            wide_t[...] = wide(narrow[h]).T * scale[...]
-            skip = pl.multiple_of(at[2 * h + 1] * 8, 8)
+            wide_t[...] = wide(narrow[h]).T * scale[...][None, :]
+            skip = pl.multiple_of(begins[h] % 128, 8)
             outs[h][...] = wide_t[pl.ds(skip, rows), :].astype(BF16)
 
-    begins = [(2 * i + 1 - k) * rows, (2 * i + k) * rows]
-    at = jnp.stack([v for b in begins for v in (b // 128, (b % 128) // 8)]).astype(jnp.int32)
     half = jax.ShapeDtypeStruct((rows, rows), BF16)
     px, po = run(
         "polar",
         slice_polar,
         [half, half],
-        [at, curvature[None, :], polar],
-        [SM, VM, HBM],
+        [curvature, polar],
+        [VM, HBM],
         scratch=[
             pltpu.VMEM((window, rows), F32),
             pltpu.VMEM((2, rows, window), BF16),
             pltpu.SemaphoreType.DMA((2,)),
         ],
-        mib=54,
+        mib=52,
     )
     px = lax.ppermute(px, "mode", KSWAP)
-    f_own = arrange(forces)
-
-    def matmul1(chunk, f, flags):
+
+    def matmul1(chunk, f):
         n = len(chunk)
         shapes = [jax.ShapeDtypeStruct((rows, w * n * Q), BF16) for w in (1, 1, 2)]
 
         def body(ins, outs, _):
-            flag, a, b, fr = ins[:4]
+            a, b, fr = ins[:3]
             keep, s2, s1 = outs
-            for u in range(n):
-                h = jnp.dot(a[...], ins[4 + 2 * u][...], preferred_element_type=F32)
-                h += jnp.dot(b[...], reorder(ins[5 + 2 * u][...]), preferred_element_type=F32)
-                h += wide(fr[...]) * flag[u].astype(F32)
-                h = h.astype(BF16)
+            i, chip, _ = place()
+            for u, (dy, dz) in enumerate(chunk):
+                yh, z, yl, x = i // Z ^ dy, i % Z, chip // X, chip % X
+                here = (yh == yl) & ((2 * z + dz) % Z == x)
+                flag = jnp.where(here, 1.0, 0.0)
+                h = jnp.dot(a[...], ins[3 + 2 * u][...], preferred_element_type=F32)
+                h += jnp.dot(b[...], reorder(ins[4 + 2 * u][...]), preferred_element_type=F32)
+                part = [
+                    (h[:, s * Q : (s + 1) * Q] + wide(fr[:, columns(p)]) * flag).astype(BF16)
+                    for s, p in enumerate(pieces())
+                ]
                 lo, hi = slice(u * Q, (u + 1) * Q), slice((n + u) * Q, (n + u + 1) * Q)
-                keep[:, lo] = h[:, :Q]
-                s2[:, lo] = h[:, Q : 2 * Q]
-                s1[:, lo] = h[:, 2 * Q : 3 * Q]
-                s1[:, hi] = h[:, 3 * Q :]
-
-        args = [flags, po, px, f] + [v for u in chunk for v in (unit[u], other[u])]
-        return run("product1", body, shapes, args, [SM] + [VM] * (len(args) - 1), mib=6 + 3 * n)
+                keep[:, lo] = part[0]
+                s2[:, lo] = part[1]
+                s1[:, lo] = part[2]
+                s1[:, hi] = part[3]
+
+        args = [po, px, f] + [v for u in chunk for v in (unit[u], other[u])]
+        return run("product1", body, shapes, args, [VM] * len(args), mib=6 + 3 * n)
 
     def add(width, args, starts):
         def body(ins, outs, _):
@@ -200,16 +212,14 @@
             if pick:
                 for c in range(2):
 
-                    @pl.when(ins[0][0] == c)
+                    @pl.when(place()[2] == c)
                     def _():
-                        move = pltpu.make_async_copy(ins[1 + pick[c]], outs[-1], sem[0])
+                        move = pltpu.make_async_copy(ins[pick[c]], outs[-1], sem[0])
                         move.start()
                         move.wait()
 
-        aliases = {1 + a: a for a in range(len(args))}
-        return run(
-            "gate", body, outs, [core] + list(args), [SM] + [ANY] * len(args), [ANY] * len(outs), aliases, scratch
-        )
+        aliases = {a: a for a in range(len(args))}
+        return run("gate", body, outs, list(args), [ANY] * len(args), [ANY] * len(outs), aliases, scratch)
 
     def join(a, b):
         w = a.shape[1]
@@ -249,23 +259,14 @@
     last = len(CHUNKS) - 1
     keep, got1, half2, got2, part, got3, r0, r1, near_half, far_half = ({} for _ in range(10))
     own_sum = oth_sum = back = None
-    f_all = None
+    done = 0
     for step in STEPS:
+        run.step = step.lower() + "_"
         stage, c = step[0], int(step[1])
-        chunk = CHUNKS[c]
+        chunk = CHUNKS[c] if stage != "G" else ()
         n = len(chunk)
         if stage == "M":
-            if c == 0:
-                flags = jnp.reshape(i == chip, (1,)).astype(jnp.int32)
-                f = f_own
-            else:
-                if f_all is None:
-                    f_all = arrange(f_far)
-                f = f_all
-                flags = jnp.stack(
-                    [(((yh ^ dy) == yl) & ((2 * z + dz) % Z == x)).astype(jnp.int32) for dy, dz in chunk]
-                )
-            keep[c], half2[c], s1 = matmul1(chunk, f, flags)
+            keep[c], half2[c], s1 = matmul1(chunk, f_far)
             got1[c] = lax.ppermute(s1, "mode", FIRST)
         elif stage == "S":
             v = add(n * Q, [half2[c], got1[c]], [0, n * Q])
@@ -280,7 +281,8 @@
             near_half[c] = join(r0[c], r1[c])
             far_half[c] = lax.ppermute(near_half[c], "mode", FIRST)
         elif stage == "T":
-            group = [(chunk, (near_half[c], far_half[c]))]
+            group = [(CHUNKS[d], (near_half[d], far_half[d])) for d in range(done, c + 1)]
+            done = c + 1
             oth_sum = matmul2(group, oth_sum, other, True, BF16 if c == last else F32)
             if c == last:
                 back = lax.ppermute(oth_sum, "mode", KSWAP)
@@ -301,6 +303,8 @@
                 unit[u] = v
                 other[u] = lax.ppermute(v, "mode", KSWAP)
             unit[1, 2] = lax.ppermute(pick, ("cfg", "mode"), ONWARD)
+        elif step == "G3":
+            (f_far,) = gate([f_far])
         elif step == "G2":
             near = [(0, 2), (1, 2)]
             for u, v in zip(near, gate([unit[u] for u in near])):
@@ -310,22 +314,17 @@
     factor = weight[:, None] * (1.0 / math.sqrt(coords.shape[1] * lax.axis_size("cfg")))
 
     def finish(ins, outs, _):
-        own, got = ins[2][...] * ins[1][...], wide(ins[3][...]) * ins[1][...]
+        own, got = ins[1][...] * ins[0][...], wide(ins[2][...]) * ins[0][...]
         for c in range(2):
 
-            @pl.when(ins[0][0] == c)
+            @pl.when(place()[2] == c)
             def _():
                 outs[0][:, :rows] = (own, got)[c]
                 outs[0][:, rows:] = (got, own)[c]
 
-    (out,) = run(
-        "finish",
-        finish,
-        [jax.ShapeDtypeStruct((rows, 2 * rows), F32)],
-        [core, factor, own_sum, back],
-        [SM, VM, VM, VM],
-        mib=12,
-    )
+
+    shape = jax.ShapeDtypeStruct((rows, 2 * rows), F32)
+    (out,) = run("finish", finish, [shape], [factor, own_sum, back], [VM, VM, VM], mib=12)
     return out.T
 
 

time: 202 us -> 162 us (0.80)
  Pallas kernels: 48.4 us -> 25.4 us
  starting transfers between devices: 60.9 us -> 43.7 us
  waiting for transfers between devices: 75.5 us -> 90.3 us
  local copies, waits for them, and re-layouts: 14.9 us -> 1.92 us
    pallas_call x36 -> x28, Pallas kernels: 48.4 us -> 25.4 us  [__call__(): pl.pallas_call(kernel, out_shape=list(outs) + [TOKEN], in_specs=list(spec...]
    ppermute x1, waiting for transfers between devices: 0.01 us -> 13.3 us  [on_device(): unit[0, 1] = lax.ppermute(unit[0, 0], 'cfg', cfg_perm(0, -1))]
    unnamed x68 -> x6, local copies, waits for them, and re-layouts: 13.5 us -> 1.78 us
    ppermute x4 -> x3, waiting for transfers between devices: 20.8 us -> 10.3 us  [on_device(): far_half[c] = lax.ppermute(near_half[c], 'mode', FIRST)]
    ppermute x4 -> x3, waiting for transfers between devices: 12.4 us -> 2.76 us  [on_device(): got3[c] = lax.ppermute(part[c], 'mode', YSWAP)]
    ppermute x1, waiting for transfers between devices: 0.01 us -> 7.11 us  [on_device(): unit[1, 2] = lax.ppermute(pick, ('cfg', 'mode'), ONWARD)]
    ppermute x1, waiting for transfers between devices: 6.09 us -> 0.01 us  [on_device(): unit[1, 1] = lax.ppermute(unit[1, 0], 'cfg', cfg_perm(0, -1))]
    ppermute x1, waiting for transfers between devices: 2 us -> 7.82 us  [on_device(): unit[1, 3] = lax.ppermute(unit[1, 0], 'cfg', cfg_perm(0, 1))]
  transfers between devices with their start and end apart: 38 -> 33, of which waited for: 18 -> 18; matrix products, arithmetic and copies ran while one was open for 0% -> 0% of each run, Pallas kernels for 14% -> 13%
where the time goes in v3:
time: 162 us
  waiting for transfers between devices  90.3 us (56%)
  starting transfers between devices  43.7 us (27%)
  Pallas kernels  25.4 us (16%)
  local copies, waits for them, and re-layouts  1.92 us (1%)
    pallas_call x28, Pallas kernels, __call__(): pl.pallas_call(kernel, out_shape=list(outs) + [TOKEN], in_specs=list(spec...  25.4 us
    ppermute x3, waiting for transfers between devices, on_device(): got1[c] = lax.ppermute(s1, 'mode', FIRST)  13.7 us
    ppermute x1, waiting for transfers between devices, on_device(): unit[0, 1] = lax.ppermute(unit[0, 0], 'cfg', cfg_perm(0, -1))  13.3 us
    ppermute x3, waiting for transfers between devices, on_device(): r1[c] = lax.ppermute(r0[c], 'mode', SECOND)  12 us
    ppermute x3, waiting for transfers between devices, on_device(): got2[c] = lax.ppermute(v, 'mode', SECOND)  11.7 us
    ppermute x3, waiting for transfers between devices, on_device(): far_half[c] = lax.ppermute(near_half[c], 'mode', FIRST)  10.3 us
    ppermute x3, starting transfers between devices, on_device(): got1[c] = lax.ppermute(s1, 'mode', FIRST)  7.87 us
    ppermute x1, waiting for transfers between devices, on_device(): unit[1, 3] = lax.ppermute(unit[1, 0], 'cfg', cfg_perm(0, 1))  7.82 us
  transfers between devices with their start and end apart: 33, of which 18 were waited for; matrix products, arithmetic and copies ran while one was open for 0% of the time, Pallas kernels for 13%

profile of v3, /device:TPU:1, one launch (start us, length us, event | category | flops | bytes accessed | tf_op | source)
XLA Modules:
  0.0 161.6 jit_solution(3557396504845883546)
XLA Ops:
  0.0 1.1 copy-done
  1.2 3.8 %collective-permute-start.2 = (bf16[648,512]{1,0:T(8,128)(2,1)S(1)}, bf16[648,512]{1,0:T(8,128)(2,1)S(1)}, u32[]{:S(2)}, u32[]{:S(2)}) collective-permute-start(bf16[648,512]{1,0:T(8,128)(2,1)S(1)} %get-tuple-element.76.refs_3_.refs_2_), channel_id=1, source_target_pairs={{0,64},{16,80},{32,96},{48,112},{64,0},{80,16},{96,32},{112,48},{1... | collective-permute-start | bytes 1990664 | tf_op jit(solution)/shard_map/ppermute | solution.py:131
  5.0 1.6 %collective-permute-start.3 = (bf16[648,512]{1,0:T(8,128)(2,1)S(1)}, bf16[648,512]{1,0:T(8,128)(2,1)S(1)}, u32[]{:S(2)}, u32[]{:S(2)}) collective-permute-start(bf16[648,512]{1,0:T(8,128)(2,1)S(1)} %get-tuple-element.76.refs_3_.refs_2_), channel_id=1, source_target_pairs={{0,16},{16,32},{32,48},{48,0},{64,80},{80,96},{96,112},{112,64},{1... | collective-permute-start | bytes 1990664 | tf_op jit(solution)/shard_map/ppermute | solution.py:129
  6.7 2.1 %collective-permute-start.4 = (bf16[648,512]{1,0:T(8,128)(2,1)S(1)}, bf16[648,512]{1,0:T(8,128)(2,1)S(1)}, u32[]{:S(2)}, u32[]{:S(2)}) collective-permute-start(bf16[648,512]{1,0:T(8,128)(2,1)S(1)} %get-tuple-element.76.refs_3_.refs_2_), channel_id=1, source_target_pairs={{0,48},{16,0},{32,16},{48,32},{64,112},{80,64},{96,80},{112,96},{1... | collective-permute-start | bytes 1990664 | tf_op jit(solution)/shard_map/ppermute | solution.py:130
  8.8 1.7 %collective-permute-start.1 = (bf16[648,512]{1,0:T(8,128)(2,1)}, bf16[648,512]{1,0:T(8,128)(2,1)S(1)}, u32[]{:S(2)}, u32[]{:S(2)}) collective-permute-start(bf16[648,512]{1,0:T(8,128)(2,1)} %param.9), channel_id=1, source_target_pairs={{0,0},{1,1},{2,18},{3,19},{4,36},{5,37},{6,54},{7,55},{8,64},{9,65... | collective-permute-start | bytes 1990664 | tf_op jit(solution)/shard_map/ppermute | solution.py:126
  11.2 2.2 %polar.1 = (bf16[648,648]{1,0:T(8,128)(2,1)S(1)}, bf16[648,648]{1,0:T(8,128)(2,1)S(1)}, f32[8,128]{1,0:T(8,128)S(1)}) custom-call(f32[648]{0:T(1024)S(1)} %copy-done.1, bf16[648,10368]{1,0:T(8,128)(2,1)} %refs_1_.1, f32[8,128]{1,0:T(8,128)S(1)} %get-tuple-element.73.refs_2_), custom_call_target="tpu_custom_call" | custom-call | flops 1000 | bytes 1000 | tf_op jit(solution)/shard_map/polar/pallas_call | solution.py:75
  13.4 1.3 collective-permute-start
  14.7 4.7 %collective-permute-done.2.refs_0_ = bf16[648,512]{1,0:T(8,128)(2,1)S(1)} collective-permute-done((bf16[648,512]{1,0:T(8,128)(2,1)S(1)}, bf16[648,512]{1,0:T(8,128)(2,1)S(1)}, u32[]{:S(2)}, u32[]{:S(2)}) %collective-permute-start.2) | collective-permute-done | bytes 663584 | tf_op jit(solution)/shard_map/ppermute | solution.py:131
  19.4 1.5 collective-permute-start.5
  20.9 2.2 %collective-permute-done.3.refs_1_ = bf16[648,512]{1,0:T(8,128)(2,1)S(1)} collective-permute-done((bf16[648,512]{1,0:T(8,128)(2,1)S(1)}, bf16[648,512]{1,0:T(8,128)(2,1)S(1)}, u32[]{:S(2)}, u32[]{:S(2)}) %collective-permute-start.3) | collective-permute-done | bytes 663584 | tf_op jit(solution)/shard_map/ppermute | solution.py:129
  23.1 13.3 %collective-permute-done.4.refs_2_ = bf16[648,512]{1,0:T(8,128)(2,1)S(1)} collective-permute-done((bf16[648,512]{1,0:T(8,128)(2,1)S(1)}, bf16[648,512]{1,0:T(8,128)(2,1)S(1)}, u32[]{:S(2)}, u32[]{:S(2)}) %collective-permute-start.4) | collective-permute-done | bytes 663584 | tf_op jit(solution)/shard_map/ppermute | solution.py:130
  36.6 2.1 %collective-permute-start.6 = (bf16[648,512]{1,0:T(8,128)(2,1)S(1)}, bf16[648,512]{1,0:T(8,128)(2,1)S(1)}, u32[]{:S(2)}, u32[]{:S(2)}) collective-permute-start(bf16[648,512]{1,0:T(8,128)(2,1)S(1)} %get-tuple-element.80.refs_5_.refs_3_), channel_id=1, source_target_pairs={{0,1},{1,0},{2,3},{3,2},{4,5},{5,4},{6,7},{7,6},{8,9},{9,8},{10,11... | collective-permute-start | bytes 1990664 | tf_op jit(solution)/shard_map/ppermute | solution.py:295
  39.2 1.5 collective-permute-start.10
  40.7 1.8 %collective-permute-start.11 = (bf16[648,512]{1,0:T(8,128)(2,1)S(1)}, bf16[648,512]{1,0:T(8,128)(2,1)S(1)}, u32[]{:S(2)}, u32[]{:S(2)}) collective-permute-start(bf16[648,512]{1,0:T(8,128)(2,1)S(1)} %get-tuple-element.82.refs_9_.refs_5_), channel_id=1, source_target_pairs={{0,48},{16,0},{32,16},{48,32},{64,112},{80,64},{96,80},{112,96},{1... | collective-permute-start | bytes 1990664 | tf_op jit(solution)/shard_map/ppermute | solution.py:297
  42.5 4.4 %m0_product1.1 = (bf16[648,512]{1,0:T(8,128)(2,1)S(1)}, bf16[648,512]{1,0:T(8,128)(2,1)S(1)}, bf16[648,1024]{1,0:T(8,128)(2,1)S(1)}, f32[8,128]{1,0:T(8,128)S(1)}) custom-call(bf16[648,648]{1,0:T(8,128)(2,1)S(1)} %get-tuple-element.74.refs_0_, bf16[648,648]{1,0:T(8,128)(2,1)S(1)} %collective-permute-done.refs_1_, ...), custom_call_target="tpu_custom_call" | custom-call | flops 1000 | bytes 1000 | tf_op jit(solution)/shard_map/m0_product1/pallas_call | solution.py:75
  46.9 2.9 %collective-permute-start.9 = (bf16[648,1024]{1,0:T(8,128)(2,1)S(1)}, bf16[648,1024]{1,0:T(8,128)(2,1)S(1)}, u32[]{:S(2)}, u32[]{:S(2)}) collective-permute-start(bf16[648,1024]{1,0:T(8,128)(2,1)S(1)} %get-tuple-element.85), channel_id=1, source_target_pairs={{0,2},{1,7},{2,0},{3,5},{4,6},{5,3},{6,4},{7,1},{8,10},{9,15},{10,... | collective-permute-start | bytes 3981320 | tf_op jit(solution)/shard_map/ppermute | solution.py:270
  49.8 7.8 %collective-permute-done.10.refs_0_ = bf16[648,512]{1,0:T(8,128)(2,1)S(1)} collective-permute-done((bf16[648,512]{1,0:T(8,128)(2,1)S(1)}, bf16[648,512]{1,0:T(8,128)(2,1)S(1)}, u32[]{:S(2)}, u32[]{:S(2)}) %collective-permute-start.10) | collective-permute-done | bytes 663584 | tf_op jit(solution)/shard_map/ppermute | solution.py:296
  57.8 0.8 collective-permute-start.12
  58.7 2.8 %collective-permute-start.15 = (bf16[648,512]{1,0:T(8,128)(2,1)S(1)}, bf16[648,512]{1,0:T(8,128)(2,1)S(1)}, u32[]{:S(2)}, u32[]{:S(2)}) collective-permute-start(bf16[648,512]{1,0:T(8,128)(2,1)S(1)} %get-tuple-element.93), channel_id=1, source_target_pairs={{0,16},{1,49},{2,18},{3,51},{4,20},{5,53},{6,22},{7,55},{8,24},{9,... | collective-permute-start | bytes 1990664 | tf_op jit(solution)/shard_map/ppermute | solution.py:298
  61.6 2.3 %m1_product1.1 = (bf16[648,256]{1,0:T(8,128)(2,1)S(1)}, bf16[648,256]{1,0:T(8,128)(2,1)S(1)}, bf16[648,512]{1,0:T(8,128)(2,1)S(1)}, f32[8,128]{1,0:T(8,128)S(1)}) custom-call(bf16[648,648]{1,0:T(8,128)(2,1)S(1)} %get-tuple-element.74.refs_0_, bf16[648,648]{1,0:T(8,128)(2,1)S(1)} %collective-permute-done.refs_1_, ...), custom_call_target="tpu_custom_call" | custom-call | flops 1000 | bytes 1000 | tf_op jit(solution)/shard_map/m1_product1/pallas_call | solution.py:75
  63.9 1.3 collective-permute-done.9.refs_1_
  65.5 3.6 %collective-permute-done.15.refs_0_ = bf16[648,512]{1,0:T(8,128)(2,1)S(1)} collective-permute-done((bf16[648,512]{1,0:T(8,128)(2,1)S(1)}, bf16[648,512]{1,0:T(8,128)(2,1)S(1)}, u32[]{:S(2)}, u32[]{:S(2)}) %collective-permute-start.15) | collective-permute-done | bytes 663584 | tf_op jit(solution)/shard_map/ppermute | solution.py:298
  69.0 7.1 %collective-permute-done.16.refs_1_ = bf16[648,512]{1,0:T(8,128)(2,1)S(1)} collective-permute-done((bf16[648,512]{1,0:T(8,128)(2,1)S(1)}, bf16[648,512]{1,0:T(8,128)(2,1)S(1)}, u32[]{:S(2)}, u32[]{:S(2)}) %collective-permute-start.16) | collective-permute-done | bytes 663584 | tf_op jit(solution)/shard_map/ppermute | solution.py:305
  76.2 1.9 %collective-permute-start.19 = (bf16[648,512]{1,0:T(8,128)(2,1)S(1)}, bf16[648,512]{1,0:T(8,128)(2,1)S(1)}, u32[]{:S(2)}, u32[]{:S(2)}) collective-permute-start(bf16[648,512]{1,0:T(8,128)(2,1)S(1)} %get-tuple-element.101.refs_3_), channel_id=1, source_target_pairs={{0,1},{1,0},{2,3},{3,2},{4,5},{5,4},{6,7},{7,6},{8,9},{9,8},{10,11... | collective-permute-start | bytes 1990664 | tf_op jit(solution)/shard_map/ppermute | solution.py:312
  78.1 2.5 %collective-permute-start.18 = (bf16[648,512]{1,0:T(8,128)(2,1)S(1)}, bf16[648,512]{1,0:T(8,128)(2,1)S(1)}, u32[]{:S(2)}, u32[]{:S(2)}) collective-permute-start(bf16[648,512]{1,0:T(8,128)(2,1)S(1)} %get-tuple-element.99), channel_id=1, source_target_pairs={{0,2},{1,7},{2,0},{3,5},{4,6},{5,3},{6,4},{7,1},{8,10},{9,15},{10,... | collective-permute-start | bytes 1990664 | tf_op jit(solution)/shard_map/ppermute | solution.py:270
  80.8 2.3 %m2_product1.1 = (bf16[648,256]{1,0:T(8,128)(2,1)S(1)}, bf16[648,256]{1,0:T(8,128)(2,1)S(1)}, bf16[648,512]{1,0:T(8,128)(2,1)S(1)}, f32[8,128]{1,0:T(8,128)S(1)}) custom-call(bf16[648,648]{1,0:T(8,128)(2,1)S(1)} %get-tuple-element.74.refs_0_, bf16[648,648]{1,0:T(8,128)(2,1)S(1)} %collective-permute-done.refs_1_, ...), custom_call_target="tpu_custom_call" | custom-call | flops 1000 | bytes 1000 | tf_op jit(solution)/shard_map/m2_product1/pallas_call | solution.py:75
  83.1 2.5 %collective-permute-start.22 = (bf16[648,512]{1,0:T(8,128)(2,1)S(1)}, bf16[648,512]{1,0:T(8,128)(2,1)S(1)}, u32[]{:S(2)}, u32[]{:S(2)}) collective-permute-start(bf16[648,512]{1,0:T(8,128)(2,1)S(1)} %get-tuple-element.107), channel_id=1, source_target_pairs={{0,2},{1,7},{2,0},{3,5},{4,6},{5,3},{6,4},{7,1},{8,10},{9,15},{10,... | collective-permute-start | bytes 1990664 | tf_op jit(solution)/shard_map/ppermute | solution.py:270
  86.0 2.8 %collective-permute-done.18.refs_1_ = bf16[648,512]{1,0:T(8,128)(2,1)S(1)} collective-permute-done((bf16[648,512]{1,0:T(8,128)(2,1)S(1)}, bf16[648,512]{1,0:T(8,128)(2,1)S(1)}, u32[]{:S(2)}, u32[]{:S(2)}) %collective-permute-start.18) | collective-permute-done | bytes 663584 | tf_op jit(solution)/shard_map/ppermute | solution.py:270
  89.0 9.5 %collective-permute-done.22.refs_1_ = bf16[648,512]{1,0:T(8,128)(2,1)S(1)} collective-permute-done((bf16[648,512]{1,0:T(8,128)(2,1)S(1)}, bf16[648,512]{1,0:T(8,128)(2,1)S(1)}, u32[]{:S(2)}, u32[]{:S(2)}) %collective-permute-start.22) | collective-permute-done | bytes 663584 | tf_op jit(solution)/shard_map/ppermute | solution.py:270
  99.0 2.8 %collective-permute-done.17.refs_1_ = bf16[648,512]{1,0:T(8,128)(2,1)S(1)} collective-permute-done((bf16[648,512]{1,0:T(8,128)(2,1)S(1)}, bf16[648,512]{1,0:T(8,128)(2,1)S(1)}, u32[]{:S(2)}, u32[]{:S(2)}) %collective-permute-start.17) | collective-permute-done | bytes 663584 | tf_op jit(solution)/shard_map/ppermute | solution.py:276
  102.6 0.9 collective-permute-start.24
  103.8 11.5 %collective-permute-done.24.refs_2_ = bf16[648,256]{1,0:T(8,128)(2,1)S(1)} collective-permute-done((bf16[648,256]{1,0:T(8,128)(2,1)S(1)}, bf16[648,256]{1,0:T(8,128)(2,1)S(1)}, u32[]{:S(2)}, u32[]{:S(2)}) %collective-permute-start.24) | collective-permute-done | bytes 331808 | tf_op jit(solution)/shard_map/ppermute | solution.py:273
  116.5 6.6 %collective-permute-done.28.refs_1_ = bf16[648,256]{1,0:T(8,128)(2,1)S(1)} collective-permute-done((bf16[648,256]{1,0:T(8,128)(2,1)S(1)}, bf16[648,256]{1,0:T(8,128)(2,1)S(1)}, u32[]{:S(2)}, u32[]{:S(2)}) %collective-permute-start.28) | collective-permute-done | bytes 331808 | tf_op jit(solution)/shard_map/ppermute | solution.py:279
  123.2 1.6 collective-permute-start.29
  124.7 3.0 %collective-permute-start.30 = (bf16[648,512]{1,0:T(8,128)(2,1)S(1)}, bf16[648,512]{1,0:T(8,128)(2,1)S(1)}, u32[]{:S(2)}, u32[]{:S(2)}) collective-permute-start(bf16[648,512]{1,0:T(8,128)(2,1)S(1)} %get-tuple-element.128.refs_1_), channel_id=1, source_target_pairs={{0,2},{1,7},{2,0},{3,5},{4,6},{5,3},{6,4},{7,1},{8,10},{9,15},{10,... | collective-permute-start | bytes 1990664 | tf_op jit(solution)/shard_map/ppermute | solution.py:282
  127.7 5.4 %collective-permute-done.29.refs_1_ = bf16[648,256]{1,0:T(8,128)(2,1)S(1)} collective-permute-done((bf16[648,256]{1,0:T(8,128)(2,1)S(1)}, bf16[648,256]{1,0:T(8,128)(2,1)S(1)}, u32[]{:S(2)}, u32[]{:S(2)}) %collective-permute-start.29) | collective-permute-done | bytes 331808 | tf_op jit(solution)/shard_map/ppermute | solution.py:279
  133.2 4.2 %collective-permute-start.31 = (bf16[648,512]{1,0:T(8,128)(2,1)S(1)}, bf16[648,512]{1,0:T(8,128)(2,1)S(1)}, u32[]{:S(2)}, u32[]{:S(2)}) collective-permute-start(bf16[648,512]{1,0:T(8,128)(2,1)S(1)} %get-tuple-element.133.refs_1_), channel_id=1, source_target_pairs={{0,2},{1,7},{2,0},{3,5},{4,6},{5,3},{6,4},{7,1},{8,10},{9,15},{10,... | collective-permute-start | bytes 1990664 | tf_op jit(solution)/shard_map/ppermute | solution.py:282
  137.4 2.5 %collective-permute-done.25.refs_1_ = bf16[648,1024]{1,0:T(8,128)(2,1)S(1)} collective-permute-done((bf16[648,1024]{1,0:T(8,128)(2,1)S(1)}, bf16[648,1024]{1,0:T(8,128)(2,1)S(1)}, u32[]{:S(2)}, u32[]{:S(2)}) %collective-permute-start.25) | collective-permute-done | bytes 1327136 | tf_op jit(solution)/shard_map/ppermute | solution.py:282
  139.9 2.3 %t0_product2.2 = (f32[648,648]{1,0:T(8,128)S(1)}, f32[8,128]{1,0:T(8,128)S(1)}) custom-call(bf16[648,1024]{1,0:T(8,128)(2,1)S(1)} %get-tuple-element.116.refs_0_, bf16[648,1024]{1,0:T(8,128)(2,1)S(1)} %collective-permute-done.25.refs_1_, bf16[648,512]{1,0:T(8,128)(2,1)S(1)} %collective-permute-done.5.refs_4_.refs_2_, ...), custom_call_target="tpu_custom_call" | custom-call | flops 1000 | bytes 1000 | tf_op jit(solution)/shard_map/t0_product2/pallas_call | solution.py:75
  142.2 2.3 %t0_product2.3 = (f32[648,648]{1,0:T(8,128)S(1)}, f32[8,128]{1,0:T(8,128)S(1)}) custom-call(bf16[648,1024]{1,0:T(8,128)(2,1)S(1)} %get-tuple-element.116.refs_0_, bf16[648,1024]{1,0:T(8,128)(2,1)S(1)} %collective-permute-done.25.refs_1_, bf16[648,512]{1,0:T(8,128)(2,1)S(1)} %get-tuple-element.76.refs_3_.refs_2_, ...), custom_call_target="tpu_custom_call" | custom-call | flops 1000 | bytes 1000 | tf_op jit(solution)/shard_map/t0_product2/pallas_call | solution.py:75
  144.5 3.2 %collective-permute-done.30.refs_2_ = bf16[648,512]{1,0:T(8,128)(2,1)S(1)} collective-permute-done((bf16[648,512]{1,0:T(8,128)(2,1)S(1)}, bf16[648,512]{1,0:T(8,128)(2,1)S(1)}, u32[]{:S(2)}, u32[]{:S(2)}) %collective-permute-start.30) | collective-permute-done | bytes 663584 | tf_op jit(solution)/shard_map/ppermute | solution.py:282
  147.7 1.2 t1_product2.2
  149.0 1.2 t1_product2.3
  150.2 4.6 %collective-permute-done.31.refs_2_ = bf16[648,512]{1,0:T(8,128)(2,1)S(1)} collective-permute-done((bf16[648,512]{1,0:T(8,128)(2,1)S(1)}, bf16[648,512]{1,0:T(8,128)(2,1)S(1)}, u32[]{:S(2)}, u32[]{:S(2)}) %collective-permute-start.31) | collective-permute-done | bytes 663584 | tf_op jit(solution)/shard_map/ppermute | solution.py:282
  154.8 1.2 t2_product2.2
  156.4 1.3 t2_product2.3
  157.6 1.1 collective-permute-done.32.refs_2_
  158.8 2.9 %t2_finish.1 = (f32[648,1296]{1,0:T(8,128)}, f32[8,128]{1,0:T(8,128)}) custom-call(f32[648,1]{1,0:T(8,128)S(1)} %mul.11.refs_0_, f32[648,648]{1,0:T(8,128)S(1)} %get-tuple-element.137.refs_1_, bf16[648,648]{1,0:T(8,128)(2,1)S(1)} %collective-permute-done.32.refs_2_, f32[8,128]{1,0:T(8,128)S(1)} %get-tuple-element.139.refs_3_), custom_call_target="tpu_custom_call" | custom-call | flops 1000 | bytes 1000 | tf_op jit(solution)/shard_map/t2_finish/pallas_call | solution.py:75
  (54 shorter events, 6.3 us)
Async XLA Ops:
  0.0 1.1 copy-start
  1.2 18.2 %collective-permute-start.2 = (bf16[648,512]{1,0:T(8,128)(2,1)S(1)}, bf16[648,512]{1,0:T(8,128)(2,1)S(1)}, u32[]{:S(2)}, u32[]{:S(2)}) collective-permute-start(bf16[648,512]{1,0:T(8,128)(2,1)S(1)} %get-tuple-element.76.refs_3_.refs_2_), channel_id=1, source_target_pairs={{0,64},{16,80},{32,96},{48,112},{64,0},{80,16},{96,32},{112,48},{1... | collective-permute-start | bytes 1990664 | tf_op jit(solution)/shard_map/ppermute | solution.py:131
  5.0 18.1 %collective-permute-start.3 = (bf16[648,512]{1,0:T(8,128)(2,1)S(1)}, bf16[648,512]{1,0:T(8,128)(2,1)S(1)}, u32[]{:S(2)}, u32[]{:S(2)}) collective-permute-start(bf16[648,512]{1,0:T(8,128)(2,1)S(1)} %get-tuple-element.76.refs_3_.refs_2_), channel_id=1, source_target_pairs={{0,16},{16,32},{32,48},{48,0},{64,80},{80,96},{96,112},{112,64},{1... | collective-permute-start | bytes 1990664 | tf_op jit(solution)/shard_map/ppermute | solution.py:129
  6.7 29.7 %collective-permute-start.4 = (bf16[648,512]{1,0:T(8,128)(2,1)S(1)}, bf16[648,512]{1,0:T(8,128)(2,1)S(1)}, u32[]{:S(2)}, u32[]{:S(2)}) collective-permute-start(bf16[648,512]{1,0:T(8,128)(2,1)S(1)} %get-tuple-element.76.refs_3_.refs_2_), channel_id=1, source_target_pairs={{0,48},{16,0},{32,16},{48,32},{64,112},{80,64},{96,80},{112,96},{1... | collective-permute-start | bytes 1990664 | tf_op jit(solution)/shard_map/ppermute | solution.py:130
  8.8 30.0 %collective-permute-start.1 = (bf16[648,512]{1,0:T(8,128)(2,1)}, bf16[648,512]{1,0:T(8,128)(2,1)S(1)}, u32[]{:S(2)}, u32[]{:S(2)}) collective-permute-start(bf16[648,512]{1,0:T(8,128)(2,1)} %param.9), channel_id=1, source_target_pairs={{0,0},{1,1},{2,18},{3,19},{4,36},{5,37},{6,54},{7,55},{8,64},{9,65... | collective-permute-start | bytes 1990664 | tf_op jit(solution)/shard_map/ppermute | solution.py:126
  10.5 0.7 copy-start.1
  13.4 27.3 %collective-permute-start = (bf16[648,648]{1,0:T(8,128)(2,1)S(1)}, bf16[648,648]{1,0:T(8,128)(2,1)S(1)}, u32[]{:S(2)}, u32[]{:S(2)}) collective-permute-start(bf16[648,648]{1,0:T(8,128)(2,1)S(1)} %get-tuple-element.75), channel_id=1, source_target_pairs={{0,1},{1,0},{2,3},{3,2},{4,5},{5,4},{6,7},{7,6},{8,9},{9,8},{10,11... | collective-permute-start | bytes 2519432 | tf_op jit(solution)/shard_map/ppermute | solution.py:165
  19.4 19.8 %collective-permute-start.5 = (bf16[648,512]{1,0:T(8,128)(2,1)S(1)}, bf16[648,512]{1,0:T(8,128)(2,1)S(1)}, u32[]{:S(2)}, u32[]{:S(2)}) collective-permute-start(bf16[648,512]{1,0:T(8,128)(2,1)S(1)} %get-tuple-element.76.refs_3_.refs_2_), channel_id=1, source_target_pairs={{0,1},{1,0},{2,3},{3,2},{4,5},{5,4},{6,7},{7,6},{8,9},{9,8},{10,11... | collective-permute-start | bytes 1990664 | tf_op jit(solution)/shard_map/ppermute | solution.py:128
  36.6 5.9 %collective-permute-start.6 = (bf16[648,512]{1,0:T(8,128)(2,1)S(1)}, bf16[648,512]{1,0:T(8,128)(2,1)S(1)}, u32[]{:S(2)}, u32[]{:S(2)}) collective-permute-start(bf16[648,512]{1,0:T(8,128)(2,1)S(1)} %get-tuple-element.80.refs_5_.refs_3_), channel_id=1, source_target_pairs={{0,1},{1,0},{2,3},{3,2},{4,5},{5,4},{6,7},{7,6},{8,9},{9,8},{10,11... | collective-permute-start | bytes 1990664 | tf_op jit(solution)/shard_map/ppermute | solution.py:295
  38.7 3.8 %collective-permute-start.7 = (bf16[648,512]{1,0:T(8,128)(2,1)S(1)}, bf16[648,512]{1,0:T(8,128)(2,1)S(1)}, u32[]{:S(2)}, u32[]{:S(2)}) collective-permute-start(bf16[648,512]{1,0:T(8,128)(2,1)S(1)} %get-tuple-element.81.refs_7_.refs_4_), channel_id=1, source_target_pairs={{0,1},{1,0},{2,3},{3,2},{4,5},{5,4},{6,7},{7,6},{8,9},{9,8},{10,11... | collective-permute-start | bytes 1990664 | tf_op jit(solution)/shard_map/ppermute | solution.py:295
  38.8 3.7 %collective-permute-start.8 = (bf16[648,512]{1,0:T(8,128)(2,1)S(1)}, bf16[648,512]{1,0:T(8,128)(2,1)S(1)}, u32[]{:S(2)}, u32[]{:S(2)}) collective-permute-start(bf16[648,512]{1,0:T(8,128)(2,1)S(1)} %get-tuple-element.82.refs_9_.refs_5_), channel_id=1, source_target_pairs={{0,1},{1,0},{2,3},{3,2},{4,5},{5,4},{6,7},{7,6},{8,9},{9,8},{10,11... | collective-permute-start | bytes 1990664 | tf_op jit(solution)/shard_map/ppermute | solution.py:295
  39.2 18.4 %collective-permute-start.10 = (bf16[648,512]{1,0:T(8,128)(2,1)S(1)}, bf16[648,512]{1,0:T(8,128)(2,1)S(1)}, u32[]{:S(2)}, u32[]{:S(2)}) collective-permute-start(bf16[648,512]{1,0:T(8,128)(2,1)S(1)} %get-tuple-element.82.refs_9_.refs_5_), channel_id=1, source_target_pairs={{0,16},{16,32},{32,48},{48,0},{64,80},{80,96},{96,112},{112,64},{1... | collective-permute-start | bytes 1990664 | tf_op jit(solution)/shard_map/ppermute | solution.py:296
  40.7 16.9 %collective-permute-start.11 = (bf16[648,512]{1,0:T(8,128)(2,1)S(1)}, bf16[648,512]{1,0:T(8,128)(2,1)S(1)}, u32[]{:S(2)}, u32[]{:S(2)}) collective-permute-start(bf16[648,512]{1,0:T(8,128)(2,1)S(1)} %get-tuple-element.82.refs_9_.refs_5_), channel_id=1, source_target_pairs={{0,48},{16,0},{32,16},{48,32},{64,112},{80,64},{96,80},{112,96},{1... | collective-permute-start | bytes 1990664 | tf_op jit(solution)/shard_map/ppermute | solution.py:297
  46.9 18.4 %collective-permute-start.9 = (bf16[648,1024]{1,0:T(8,128)(2,1)S(1)}, bf16[648,1024]{1,0:T(8,128)(2,1)S(1)}, u32[]{:S(2)}, u32[]{:S(2)}) collective-permute-start(bf16[648,1024]{1,0:T(8,128)(2,1)S(1)} %get-tuple-element.85), channel_id=1, source_target_pairs={{0,2},{1,7},{2,0},{3,5},{4,6},{5,3},{6,4},{7,1},{8,10},{9,15},{10,... | collective-permute-start | bytes 3981320 | tf_op jit(solution)/shard_map/ppermute | solution.py:270
  57.8 3.8 %collective-permute-start.12 = (bf16[648,512]{1,0:T(8,128)(2,1)S(1)}, bf16[648,512]{1,0:T(8,128)(2,1)S(1)}, u32[]{:S(2)}, u32[]{:S(2)}) collective-permute-start(bf16[648,512]{1,0:T(8,128)(2,1)S(1)} %get-tuple-element.88.refs_3_), channel_id=1, source_target_pairs={{0,1},{1,0},{2,3},{3,2},{4,5},{5,4},{6,7},{7,6},{8,9},{9,8},{10,11... | collective-permute-start | bytes 1990664 | tf_op jit(solution)/shard_map/ppermute | solution.py:304
  58.6 3.0 %collective-permute-start.13 = (bf16[648,512]{1,0:T(8,128)(2,1)S(1)}, bf16[648,512]{1,0:T(8,128)(2,1)S(1)}, u32[]{:S(2)}, u32[]{:S(2)}) collective-permute-start(bf16[648,512]{1,0:T(8,128)(2,1)S(1)} %get-tuple-element.89.refs_5_.refs_4_), channel_id=1, source_target_pairs={{0,1},{1,0},{2,3},{3,2},{4,5},{5,4},{6,7},{7,6},{8,9},{9,8},{10,11... | collective-permute-start | bytes 1990664 | tf_op jit(solution)/shard_map/ppermute | solution.py:304
  58.7 10.4 %collective-permute-start.15 = (bf16[648,512]{1,0:T(8,128)(2,1)S(1)}, bf16[648,512]{1,0:T(8,128)(2,1)S(1)}, u32[]{:S(2)}, u32[]{:S(2)}) collective-permute-start(bf16[648,512]{1,0:T(8,128)(2,1)S(1)} %get-tuple-element.93), channel_id=1, source_target_pairs={{0,16},{1,49},{2,18},{3,51},{4,20},{5,53},{6,22},{7,55},{8,24},{9,... | collective-permute-start | bytes 1990664 | tf_op jit(solution)/shard_map/ppermute | solution.py:298
  61.4 14.7 %collective-permute-start.16 = (bf16[648,512]{1,0:T(8,128)(2,1)S(1)}, bf16[648,512]{1,0:T(8,128)(2,1)S(1)}, u32[]{:S(2)}, u32[]{:S(2)}) collective-permute-start(bf16[648,512]{1,0:T(8,128)(2,1)S(1)} %get-tuple-element.94), channel_id=1, source_target_pairs={{0,16},{1,49},{2,18},{3,51},{4,20},{5,53},{6,22},{7,55},{8,24},{9,... | collective-permute-start | bytes 1990664 | tf_op jit(solution)/shard_map/ppermute | solution.py:305
  65.4 15.2 %collective-permute-start.14 = (bf16[648,512]{1,0:T(8,128)(2,1)S(1)}, bf16[648,512]{1,0:T(8,128)(2,1)S(1)}, u32[]{:S(2)}, u32[]{:S(2)}) collective-permute-start(bf16[648,512]{1,0:T(8,128)(2,1)S(1)} %get-tuple-element.92), channel_id=1, source_target_pairs={{0,6},{1,3},{2,4},{3,1},{4,2},{5,7},{6,0},{7,5},{8,14},{9,11},{10,... | collective-permute-start | bytes 1990664 | tf_op jit(solution)/shard_map/ppermute | solution.py:273
  76.2 4.7 %collective-permute-start.19 = (bf16[648,512]{1,0:T(8,128)(2,1)S(1)}, bf16[648,512]{1,0:T(8,128)(2,1)S(1)}, u32[]{:S(2)}, u32[]{:S(2)}) collective-permute-start(bf16[648,512]{1,0:T(8,128)(2,1)S(1)} %get-tuple-element.101.refs_3_), channel_id=1, source_target_pairs={{0,1},{1,0},{2,3},{3,2},{4,5},{5,4},{6,7},{7,6},{8,9},{9,8},{10,11... | collective-permute-start | bytes 1990664 | tf_op jit(solution)/shard_map/ppermute | solution.py:312
  78.1 2.8 %collective-permute-start.20 = (bf16[648,512]{1,0:T(8,128)(2,1)S(1)}, bf16[648,512]{1,0:T(8,128)(2,1)S(1)}, u32[]{:S(2)}, u32[]{:S(2)}) collective-permute-start(bf16[648,512]{1,0:T(8,128)(2,1)S(1)} %get-tuple-element.102.refs_5_.refs_4_), channel_id=1, source_target_pairs={{0,1},{1,0},{2,3},{3,2},{4,5},{5,4},{6,7},{7,6},{8,9},{9,8},{10,11... | collective-permute-start | bytes 1990664 | tf_op jit(solution)/shard_map/ppermute | solution.py:312
  78.1 10.7 %collective-permute-start.18 = (bf16[648,512]{1,0:T(8,128)(2,1)S(1)}, bf16[648,512]{1,0:T(8,128)(2,1)S(1)}, u32[]{:S(2)}, u32[]{:S(2)}) collective-permute-start(bf16[648,512]{1,0:T(8,128)(2,1)S(1)} %get-tuple-element.99), channel_id=1, source_target_pairs={{0,2},{1,7},{2,0},{3,5},{4,6},{5,3},{6,4},{7,1},{8,10},{9,15},{10,... | collective-permute-start | bytes 1990664 | tf_op jit(solution)/shard_map/ppermute | solution.py:270
  83.1 15.5 %collective-permute-start.22 = (bf16[648,512]{1,0:T(8,128)(2,1)S(1)}, bf16[648,512]{1,0:T(8,128)(2,1)S(1)}, u32[]{:S(2)}, u32[]{:S(2)}) collective-permute-start(bf16[648,512]{1,0:T(8,128)(2,1)S(1)} %get-tuple-element.107), channel_id=1, source_target_pairs={{0,2},{1,7},{2,0},{3,5},{4,6},{5,3},{6,4},{7,1},{8,10},{9,15},{10,... | collective-permute-start | bytes 1990664 | tf_op jit(solution)/shard_map/ppermute | solution.py:270
  85.6 16.1 %collective-permute-start.17 = (bf16[648,512]{1,0:T(8,128)(2,1)S(1)}, bf16[648,512]{1,0:T(8,128)(2,1)S(1)}, u32[]{:S(2)}, u32[]{:S(2)}) collective-permute-start(bf16[648,512]{1,0:T(8,128)(2,1)S(1)} %get-tuple-element.97.refs_0_), channel_id=1, source_target_pairs={{0,8},{1,9},{2,10},{3,11},{4,12},{5,13},{6,14},{7,15},{8,0},{9,1},... | collective-permute-start | bytes 1990664 | tf_op jit(solution)/shard_map/ppermute | solution.py:276
  88.9 10.0 %collective-permute-start.21 = (bf16[648,256]{1,0:T(8,128)(2,1)S(1)}, bf16[648,256]{1,0:T(8,128)(2,1)S(1)}, u32[]{:S(2)}, u32[]{:S(2)}) collective-permute-start(bf16[648,256]{1,0:T(8,128)(2,1)S(1)} %get-tuple-element.105), channel_id=1, source_target_pairs={{0,6},{1,3},{2,4},{3,1},{4,2},{5,7},{6,0},{7,5},{8,14},{9,11},{10,... | collective-permute-start | bytes 995336 | tf_op jit(solution)/shard_map/ppermute | solution.py:273
  101.9 13.6 %collective-permute-start.23 = (bf16[648,512]{1,0:T(8,128)(2,1)S(1)}, bf16[648,512]{1,0:T(8,128)(2,1)S(1)}, u32[]{:S(2)}, u32[]{:S(2)}) collective-permute-start(bf16[648,512]{1,0:T(8,128)(2,1)S(1)} %get-tuple-element.111.refs_0_), channel_id=1, source_target_pairs={{0,6},{1,3},{2,4},{3,1},{4,2},{5,7},{6,0},{7,5},{8,14},{9,11},{10,... | collective-permute-start | bytes 1990664 | tf_op jit(solution)/shard_map/ppermute | solution.py:279
  102.6 12.8 %collective-permute-start.24 = (bf16[648,256]{1,0:T(8,128)(2,1)S(1)}, bf16[648,256]{1,0:T(8,128)(2,1)S(1)}, u32[]{:S(2)}, u32[]{:S(2)}) collective-permute-start(bf16[648,256]{1,0:T(8,128)(2,1)S(1)} %get-tuple-element.113), channel_id=1, source_target_pairs={{0,6},{1,3},{2,4},{3,1},{4,2},{5,7},{6,0},{7,5},{8,14},{9,11},{10,... | collective-permute-start | bytes 995336 | tf_op jit(solution)/shard_map/ppermute | solution.py:273
  103.4 12.2 %collective-permute-start.27 = (bf16[648,256]{1,0:T(8,128)(2,1)S(1)}, bf16[648,256]{1,0:T(8,128)(2,1)S(1)}, u32[]{:S(2)}, u32[]{:S(2)}) collective-permute-start(bf16[648,256]{1,0:T(8,128)(2,1)S(1)} %get-tuple-element.118.refs_0_), channel_id=1, source_target_pairs={{0,8},{1,9},{2,10},{3,11},{4,12},{5,13},{6,14},{7,15},{8,0},{9,1},... | collective-permute-start | bytes 995336 | tf_op jit(solution)/shard_map/ppermute | solution.py:276
  115.6 24.3 %collective-permute-start.25 = (bf16[648,1024]{1,0:T(8,128)(2,1)S(1)}, bf16[648,1024]{1,0:T(8,128)(2,1)S(1)}, u32[]{:S(2)}, u32[]{:S(2)}) collective-permute-start(bf16[648,1024]{1,0:T(8,128)(2,1)S(1)} %get-tuple-element.116.refs_0_), channel_id=1, source_target_pairs={{0,2},{1,7},{2,0},{3,5},{4,6},{5,3},{6,4},{7,1},{8,10},{9,15},{10,... | collective-permute-start | bytes 3981320 | tf_op jit(solution)/shard_map/ppermute | solution.py:282
  115.8 7.2 %collective-permute-start.28 = (bf16[648,256]{1,0:T(8,128)(2,1)S(1)}, bf16[648,256]{1,0:T(8,128)(2,1)S(1)}, u32[]{:S(2)}, u32[]{:S(2)}) collective-permute-start(bf16[648,256]{1,0:T(8,128)(2,1)S(1)} %get-tuple-element.120.refs_0_), channel_id=1, source_target_pairs={{0,6},{1,3},{2,4},{3,1},{4,2},{5,7},{6,0},{7,5},{8,14},{9,11},{10,... | collective-permute-start | bytes 995336 | tf_op jit(solution)/shard_map/ppermute | solution.py:279
  116.5 6.6 %collective-permute-start.26 = (bf16[648,256]{1,0:T(8,128)(2,1)S(1)}, bf16[648,256]{1,0:T(8,128)(2,1)S(1)}, u32[]{:S(2)}, u32[]{:S(2)}) collective-permute-start(bf16[648,256]{1,0:T(8,128)(2,1)S(1)} %get-tuple-element.117.refs_0_), channel_id=1, source_target_pairs={{0,8},{1,9},{2,10},{3,11},{4,12},{5,13},{6,14},{7,15},{8,0},{9,1},... | collective-permute-start | bytes 995336 | tf_op jit(solution)/shard_map/ppermute | solution.py:276
  123.2 10.0 %collective-permute-start.29 = (bf16[648,256]{1,0:T(8,128)(2,1)S(1)}, bf16[648,256]{1,0:T(8,128)(2,1)S(1)}, u32[]{:S(2)}, u32[]{:S(2)}) collective-permute-start(bf16[648,256]{1,0:T(8,128)(2,1)S(1)} %get-tuple-element.123.refs_0_), channel_id=1, source_target_pairs={{0,6},{1,3},{2,4},{3,1},{4,2},{5,7},{6,0},{7,5},{8,14},{9,11},{10,... | collective-permute-start | bytes 995336 | tf_op jit(solution)/shard_map/ppermute | solution.py:279
  124.7 23.0 %collective-permute-start.30 = (bf16[648,512]{1,0:T(8,128)(2,1)S(1)}, bf16[648,512]{1,0:T(8,128)(2,1)S(1)}, u32[]{:S(2)}, u32[]{:S(2)}) collective-permute-start(bf16[648,512]{1,0:T(8,128)(2,1)S(1)} %get-tuple-element.128.refs_1_), channel_id=1, source_target_pairs={{0,2},{1,7},{2,0},{3,5},{4,6},{5,3},{6,4},{7,1},{8,10},{9,15},{10,... | collective-permute-start | bytes 1990664 | tf_op jit(solution)/shard_map/ppermute | solution.py:282
  133.2 21.6 %collective-permute-start.31 = (bf16[648,512]{1,0:T(8,128)(2,1)S(1)}, bf16[648,512]{1,0:T(8,128)(2,1)S(1)}, u32[]{:S(2)}, u32[]{:S(2)}) collective-permute-start(bf16[648,512]{1,0:T(8,128)(2,1)S(1)} %get-tuple-element.133.refs_1_), channel_id=1, source_target_pairs={{0,2},{1,7},{2,0},{3,5},{4,6},{5,3},{6,4},{7,1},{8,10},{9,15},{10,... | collective-permute-start | bytes 1990664 | tf_op jit(solution)/shard_map/ppermute | solution.py:282
  154.8 1.3 copy-start.2
  156.1 2.7 %collective-permute-start.32 = (bf16[648,648]{1,0:T(8,128)(2,1)S(1)}, bf16[648,648]{1,0:T(8,128)(2,1)S(1)}, u32[]{:S(2)}, u32[]{:S(2)}) collective-permute-start(bf16[648,648]{1,0:T(8,128)(2,1)S(1)} %get-tuple-element.138), channel_id=1, source_target_pairs={{0,1},{1,0},{2,3},{3,2},{4,5},{5,4},{6,7},{7,6},{8,9},{9,8},{10,11... | collective-permute-start | bytes 2519432 | tf_op jit(solution)/shard_map/ppermute | solution.py:288

commit v4 on v3

--- a/solution.py
+++ b/solution.py
@@ -12,10 +12,11 @@
 X, Z = 4, 4
 Q = 128
 CHUNKS = (((0, 0), (0, 3), (0, 1), (1, 0)), ((1, 3), (1, 1)), ((0, 2), (1, 2)))
+FINISH = 3
 STEPS = (
     "G0", "G3", "M0", "G1", "M1", "S0", "G2", "Y0", "M2",
-    "S1", "S2", "Y1", "R0", "Y2", "F0", "R1", "F1", "R2",
-    "F2", "T0", "T1", "T2",
+    "S1", "Y1", "R0", "S2", "R1", "F0", "Y2", "R2", "F1",
+    "F2", "N2", "T0", "T1", "T2",
 )
 
 
@@ -164,7 +165,7 @@
     )
     px = lax.ppermute(px, "mode", KSWAP)
 
-    def matmul1(chunk, f):
+    def matmul1(chunk, f, early):
         n = len(chunk)
         shapes = [jax.ShapeDtypeStruct((rows, w * n * Q), BF16) for w in (1, 1, 2)]
 
@@ -174,7 +175,7 @@
             i, chip, _ = place()
             for u, (dy, dz) in enumerate(chunk):
                 yh, z, yl, x = i // Z ^ dy, i % Z, chip // X, chip % X
-                here = (yh == yl) & ((2 * z + dz) % Z == x)
+                here = (i == chip) if early else (yh == yl) & ((2 * z + dz) % Z == x)
                 flag = jnp.where(here, 1.0, 0.0)
                 h = jnp.dot(a[...], ins[3 + 2 * u][...], preferred_element_type=F32)
                 h += jnp.dot(b[...], reorder(ins[4 + 2 * u][...]), preferred_element_type=F32)
@@ -191,15 +192,27 @@
         args = [po, px, f] + [v for u in chunk for v in (unit[u], other[u])]
         return run("product1", body, shapes, args, [VM] * len(args), mib=6 + 3 * n)
 
-    def add(width, args, starts):
-        def body(ins, outs, _):
-            total = None
-            for r, at in zip(ins, starts):
-                v = wide(r[:, at : at + width])
-                total = v if total is None else total + v
-            outs[0][...] = total.astype(BF16)
-
-        return run("add", body, [jax.ShapeDtypeStruct((rows, width), BF16)], args, [VM] * len(args))[0]
+    def add(products, which, far, more=()):
+        args = [v for p in products for v in (p[which], p[3])] + list(more)
+        sizes = [p[which].shape[1] for p in products]
+
+        def body(ins, outs, _):
+            at = 0
+            for q, w in enumerate(sizes):
+                got = ins[2 * q + 1]
+                total = wide(ins[2 * q][...]) + wide(got[:, w:] if far else got[:, :w])
+                for r in ins[2 * len(sizes) :]:
+                    total += wide(r[:, at : at + w])
+                outs[0][:, at : at + w] = total.astype(BF16)
+                at += w
+
+        return run("add", body, [jax.ShapeDtypeStruct((rows, sum(sizes)), BF16)], args, [VM] * len(args), mib=6)[0]
+
+    def add2(a, b):
+        def body(ins, outs, _):
+            outs[0][...] = (wide(ins[0][...]) + wide(ins[1][...])).astype(BF16)
+
+        return run("add", body, [like(a)], [a, b], [VM] * 2)[0]
 
     def gate(args, pick=None):
         outs = [like(v) for v in args]
@@ -230,63 +243,67 @@
 
         return run("join", body, [jax.ShapeDtypeStruct((rows, 2 * w), BF16)], [a, b], [VM] * 2)[0]
 
-    def matmul2(groups, acc, names, swap, dtype):
+    def matmul2(groups, acc, names, swap, dtype, far):
         begins = acc is None
         args = [] if begins else [acc]
         for chunk, r in groups:
-            args += list(r) + [names[u] for u in chunk]
+            args += [r] + [names[u] for u in chunk]
+        places = [(0, 2, 1, 3)[s] if swap else s for s in ((2, 3) if far else (0, 1))]
 
         def body(ins, outs, _):
             ins = list(ins)
             total = None if begins else ins.pop(0)[...]
             for chunk, _ in groups:
-                n = len(chunk)
-                pieces = [(r, h) for r in ins[:2] for h in range(2)]
-                if swap:
-                    pieces = [pieces[p] for p in (0, 2, 1, 3)]
-                ins = ins[2:]
+                n, r, ins = len(chunk), ins[0], ins[1:]
                 for u in range(n):
-                    ru = jnp.concatenate([r[:, (h * n + u) * Q : (h * n + u + 1) * Q] for r, h in pieces], axis=1)
-                    t = lax.dot_general(
-                        ins[u][...], ru, (((1,), (1,)), ((), ())), preferred_element_type=F32
-                    )
+                    ru = jnp.concatenate([r[:, (h * n + u) * Q : (h * n + u + 1) * Q] for h in range(2)], axis=1)
+                    cu = jnp.concatenate([ins[u][:, p * Q : (p + 1) * Q] for p in places], axis=1)
+                    t = lax.dot_general(cu, ru, (((1,), (1,)), ((), ())), preferred_element_type=F32)
                     total = t if total is None else total + t
-                ins = ins[len(chunk) :]
+                ins = ins[n:]
             outs[0][...] = total.astype(dtype)
 
-        return run("product2", body, [jax.ShapeDtypeStruct((rows, rows), dtype)], args, [VM] * len(args), mib=14)[0]
+        shape = jax.ShapeDtypeStruct((rows, rows), dtype)
+        return run("product2", body, [shape], args, [VM] * len(args), mib=6 + 2 * sum(len(g[0]) for g in groups))[0]
 
     last = len(CHUNKS) - 1
-    keep, got1, half2, got2, part, got3, r0, r1, near_half, far_half = ({} for _ in range(10))
+    products = [[] for _ in CHUNKS]
+    got2, part3, got3, r0, r1, near_half, far_half = ({} for _ in range(7))
     own_sum = oth_sum = back = None
-    done = 0
+    begun = done = 0
     for step in STEPS:
         run.step = step.lower() + "_"
         stage, c = step[0], int(step[1])
         chunk = CHUNKS[c] if stage != "G" else ()
-        n = len(chunk)
-        if stage == "M":
-            keep[c], half2[c], s1 = matmul1(chunk, f_far)
-            got1[c] = lax.ppermute(s1, "mode", FIRST)
+        if stage in "AM":
+            early = stage == "A"
+            part = chunk[:1] if early else chunk[len(products[c]) :]
+            got = matmul1(part, forces if early else f_far, early)
+            products[c].append((*got, lax.ppermute(got[2], "mode", FIRST)))
         elif stage == "S":
-            v = add(n * Q, [half2[c], got1[c]], [0, n * Q])
+            v = add(products[c], 1, True)
             got2[c] = lax.ppermute(v, "mode", SECOND)
         elif stage == "Y":
-            part[c] = add(n * Q, [keep[c], got1[c], got2[c]], [0, 0, 0])
-            got3[c] = lax.ppermute(part[c], "mode", YSWAP)
+            part3[c] = add(products[c], 0, False, [got2[c]])
+            got3[c] = lax.ppermute(part3[c], "mode", YSWAP)
         elif stage == "R":
-            r0[c] = add(n * Q, [part[c], got3[c]], [0, 0])
+            r0[c] = add2(part3[c], got3[c])
             r1[c] = lax.ppermute(r0[c], "mode", SECOND)
         elif stage == "F":
             near_half[c] = join(r0[c], r1[c])
             far_half[c] = lax.ppermute(near_half[c], "mode", FIRST)
+        elif stage == "N":
+            group = [(CHUNKS[d], near_half[d]) for d in range(begun, c + 1)]
+            begun = c + 1
+            oth_sum = matmul2(group, oth_sum, other, True, F32, False)
+            own_sum = matmul2(group, own_sum, unit, False, F32, False)
         elif stage == "T":
-            group = [(CHUNKS[d], (near_half[d], far_half[d])) for d in range(done, c + 1)]
+            group = [(CHUNKS[d], far_half[d]) for d in range(done, c + 1)]
             done = c + 1
-            oth_sum = matmul2(group, oth_sum, other, True, BF16 if c == last else F32)
+            oth_sum = matmul2(group, oth_sum, other, True, BF16 if c == last else F32, True)
             if c == last:
                 back = lax.ppermute(oth_sum, "mode", KSWAP)
-            own_sum = matmul2(group, own_sum, unit, False, F32)
+            own_sum = matmul2(group, own_sum, unit, False, F32, True)
         elif step == "G0":
             near = [(1, 0), (0, 3), (0, 1)]
             *vals, pick = gate([unit[u] for u in near], (1, 2))
@@ -322,9 +339,17 @@
                 outs[0][:, :rows] = (own, got)[c]
                 outs[0][:, rows:] = (got, own)[c]
 
-
+    cut = FINISH if rows % (8 * FINISH) == 0 else 1
     shape = jax.ShapeDtypeStruct((rows, 2 * rows), F32)
-    (out,) = run("finish", finish, [shape], [factor, own_sum, back], [VM, VM, VM], mib=12)
+    out = pl.pallas_call(
+        lambda *refs: finish(refs[:3], refs[3:], ()),
+        out_shape=shape,
+        grid=(cut,),
+        in_specs=[pl.BlockSpec((rows // cut, w), lambda t: (t, 0)) for w in (1, rows, rows)],
+        out_specs=pl.BlockSpec((rows // cut, 2 * rows), lambda t: (t, 0)),
+        compiler_params=pltpu.CompilerParams(vmem_limit_bytes=16 * 1024 * 1024),
+        name="finish",
+    )(factor, own_sum, back)
     return out.T
 
 

time: 162 us -> 159 us (0.981)
  waiting for transfers between devices: 90.3 us -> 87.7 us
    ppermute x3, waiting for transfers between devices: 11.7 us -> 4.68 us  [on_device(): got2[c] = lax.ppermute(v, 'mode', SECOND)]
    ppermute x6, waiting for transfers between devices: 16.5 us -> 19.6 us  [the longest x3 11.4 us: on_device(): products[c].append((*got, lax.ppermute(got[2], 'mode', FIRST)))]
    pallas_call x0 -> x1, Pallas kernels: none -> 2.89 us  [on_device(): pl.pallas_call(lambda *refs: finish(refs[:3], refs[3:], ()), out_shape=sh...]
    ppermute x3, starting transfers between devices: 2.92 us -> 0.2 us  [on_device(): r1[c] = lax.ppermute(r0[c], 'mode', SECOND)]
    pallas_call x28 -> x29, Pallas kernels: 25.4 us -> 23.5 us  [__call__(): pl.pallas_call(kernel, out_shape=list(outs) + [TOKEN], in_specs=list(spec...]
  transfers between devices with their start and end apart: 33 -> 33, of which waited for: 18 -> 19; matrix products, arithmetic and copies ran while one was open for 0% -> 0% of each run, Pallas kernels for 13% -> 14%
where the time goes in v4:
time: 159 us; the launch traced here: 158 us
  waiting for transfers between devices  87.7 us (55%)
  starting transfers between devices  42.1 us (26%)
  Pallas kernels  26.4 us (17%)
  local copies, waits for them, and re-layouts  1.92 us (1%)
    pallas_call x29, Pallas kernels, __call__(): pl.pallas_call(kernel, out_shape=list(outs) + [TOKEN], in_specs=list(spec...  23.5 us
    ppermute x1, waiting for transfers between devices, on_device(): unit[0, 1] = lax.ppermute(unit[0, 0], 'cfg', cfg_perm(0, -1))  13.3 us
    ppermute x3, waiting for transfers between devices, on_device(): r1[c] = lax.ppermute(r0[c], 'mode', SECOND)  13.3 us
    ppermute x3, waiting for transfers between devices, on_device(): products[c].append((*got, lax.ppermute(got[2], 'mode', FIRST)))  11.4 us
    ppermute x3, waiting for transfers between devices, on_device(): far_half[c] = lax.ppermute(near_half[c], 'mode', FIRST)  10.6 us
    ppermute x3, waiting for transfers between devices, on_device(): got3[c] = lax.ppermute(part3[c], 'mode', YSWAP)  8.15 us
    ppermute x3, starting transfers between devices, on_device(): products[c].append((*got, lax.ppermute(got[2], 'mode', FIRST)))  7.91 us
    ppermute x1, waiting for transfers between devices, on_device(): unit[1, 3] = lax.ppermute(unit[1, 0], 'cfg', cfg_perm(0, 1))  7.81 us
  transfers between devices with their start and end apart: 33, of which 19 were waited for; matrix products, arithmetic and copies ran while one was open for 0% of the time, Pallas kernels for 14%

profile of v4, /device:TPU:1, one launch (start us, length us, event | category | flops | bytes accessed | tf_op | source)
XLA Modules:
  0.0 158.3 jit_solution(15697077984870239568)
XLA Ops:
  0.0 1.1 copy-done
  1.2 3.8 %collective-permute-start.2 = (bf16[648,512]{1,0:T(8,128)(2,1)S(1)}, bf16[648,512]{1,0:T(8,128)(2,1)S(1)}, u32[]{:S(2)}, u32[]{:S(2)}) collective-permute-start(bf16[648,512]{1,0:T(8,128)(2,1)S(1)} %get-tuple-element.78.refs_3_.refs_1_.refs_2_), channel_id=1, source_target_pairs={{0,64},{16,80},{32,96},{48,112},{64,0},{80,16},{96,32},{112,48},{1... | collective-permute-start | bytes 1990664 | tf_op jit(solution)/shard_map/ppermute | solution.py:132
  5.0 1.6 %collective-permute-start.3 = (bf16[648,512]{1,0:T(8,128)(2,1)S(1)}, bf16[648,512]{1,0:T(8,128)(2,1)S(1)}, u32[]{:S(2)}, u32[]{:S(2)}) collective-permute-start(bf16[648,512]{1,0:T(8,128)(2,1)S(1)} %get-tuple-element.78.refs_3_.refs_1_.refs_2_), channel_id=1, source_target_pairs={{0,16},{16,32},{32,48},{48,0},{64,80},{80,96},{96,112},{112,64},{1... | collective-permute-start | bytes 1990664 | tf_op jit(solution)/shard_map/ppermute | solution.py:130
  6.7 2.1 %collective-permute-start.4 = (bf16[648,512]{1,0:T(8,128)(2,1)S(1)}, bf16[648,512]{1,0:T(8,128)(2,1)S(1)}, u32[]{:S(2)}, u32[]{:S(2)}) collective-permute-start(bf16[648,512]{1,0:T(8,128)(2,1)S(1)} %get-tuple-element.78.refs_3_.refs_1_.refs_2_), channel_id=1, source_target_pairs={{0,48},{16,0},{32,16},{48,32},{64,112},{80,64},{96,80},{112,96},{1... | collective-permute-start | bytes 1990664 | tf_op jit(solution)/shard_map/ppermute | solution.py:131
  8.8 1.7 %collective-permute-start.1 = (bf16[648,512]{1,0:T(8,128)(2,1)}, bf16[648,512]{1,0:T(8,128)(2,1)S(1)}, u32[]{:S(2)}, u32[]{:S(2)}) collective-permute-start(bf16[648,512]{1,0:T(8,128)(2,1)} %param.9), channel_id=1, source_target_pairs={{0,0},{1,1},{2,18},{3,19},{4,36},{5,37},{6,54},{7,55},{8,64},{9,65... | collective-permute-start | bytes 1990664 | tf_op jit(solution)/shard_map/ppermute | solution.py:127
  11.2 2.2 %polar.1 = (bf16[648,648]{1,0:T(8,128)(2,1)S(1)}, bf16[648,648]{1,0:T(8,128)(2,1)S(1)}, f32[8,128]{1,0:T(8,128)S(1)}) custom-call(f32[648]{0:T(1024)S(1)} %copy-done.1, bf16[648,10368]{1,0:T(8,128)(2,1)} %refs_1_.1, f32[8,128]{1,0:T(8,128)S(1)} %get-tuple-element.75.refs_2_), custom_call_target="tpu_custom_call" | custom-call | flops 1000 | bytes 1000 | tf_op jit(solution)/shard_map/polar/pallas_call | solution.py:76
  13.4 1.3 collective-permute-start
  14.7 4.7 %collective-permute-done.2.refs_0_ = bf16[648,512]{1,0:T(8,128)(2,1)S(1)} collective-permute-done((bf16[648,512]{1,0:T(8,128)(2,1)S(1)}, bf16[648,512]{1,0:T(8,128)(2,1)S(1)}, u32[]{:S(2)}, u32[]{:S(2)}) %collective-permute-start.2) | collective-permute-done | bytes 663584 | tf_op jit(solution)/shard_map/ppermute | solution.py:132
  19.4 1.5 collective-permute-start.5
  20.9 2.2 %collective-permute-done.3.refs_1_ = bf16[648,512]{1,0:T(8,128)(2,1)S(1)} collective-permute-done((bf16[648,512]{1,0:T(8,128)(2,1)S(1)}, bf16[648,512]{1,0:T(8,128)(2,1)S(1)}, u32[]{:S(2)}, u32[]{:S(2)}) %collective-permute-start.3) | collective-permute-done | bytes 663584 | tf_op jit(solution)/shard_map/ppermute | solution.py:130
  23.1 13.3 %collective-permute-done.4.refs_2_ = bf16[648,512]{1,0:T(8,128)(2,1)S(1)} collective-permute-done((bf16[648,512]{1,0:T(8,128)(2,1)S(1)}, bf16[648,512]{1,0:T(8,128)(2,1)S(1)}, u32[]{:S(2)}, u32[]{:S(2)}) %collective-permute-start.4) | collective-permute-done | bytes 663584 | tf_op jit(solution)/shard_map/ppermute | solution.py:131
  36.6 2.1 %collective-permute-start.8 = (bf16[648,512]{1,0:T(8,128)(2,1)S(1)}, bf16[648,512]{1,0:T(8,128)(2,1)S(1)}, u32[]{:S(2)}, u32[]{:S(2)}) collective-permute-start(bf16[648,512]{1,0:T(8,128)(2,1)S(1)} %get-tuple-element.84.refs_9_.refs_4_.refs_5_), channel_id=1, source_target_pairs={{0,1},{1,0},{2,3},{3,2},{4,5},{5,4},{6,7},{7,6},{8,9},{9,8},{10,11... | collective-permute-start | bytes 1990664 | tf_op jit(solution)/shard_map/ppermute | solution.py:312
  39.2 1.5 collective-permute-start.10
  40.7 1.8 %collective-permute-start.11 = (bf16[648,512]{1,0:T(8,128)(2,1)S(1)}, bf16[648,512]{1,0:T(8,128)(2,1)S(1)}, u32[]{:S(2)}, u32[]{:S(2)}) collective-permute-start(bf16[648,512]{1,0:T(8,128)(2,1)S(1)} %get-tuple-element.84.refs_9_.refs_4_.refs_5_), channel_id=1, source_target_pairs={{0,48},{16,0},{32,16},{48,32},{64,112},{80,64},{96,80},{112,96},{1... | collective-permute-start | bytes 1990664 | tf_op jit(solution)/shard_map/ppermute | solution.py:314
  42.5 4.4 %m0_product1.1 = (bf16[648,512]{1,0:T(8,128)(2,1)S(1)}, bf16[648,512]{1,0:T(8,128)(2,1)S(1)}, bf16[648,1024]{1,0:T(8,128)(2,1)S(1)}, f32[8,128]{1,0:T(8,128)S(1)}) custom-call(bf16[648,648]{1,0:T(8,128)(2,1)S(1)} %get-tuple-element.76.refs_0_, bf16[648,648]{1,0:T(8,128)(2,1)S(1)} %collective-permute-done.refs_1_, ...), custom_call_target="tpu_custom_call" | custom-call | flops 1000 | bytes 1000 | tf_op jit(solution)/shard_map/m0_product1/pallas_call | solution.py:76
  46.9 2.9 %collective-permute-start.9 = (bf16[648,1024]{1,0:T(8,128)(2,1)S(1)}, bf16[648,1024]{1,0:T(8,128)(2,1)S(1)}, u32[]{:S(2)}, u32[]{:S(2)}) collective-permute-start(bf16[648,1024]{1,0:T(8,128)(2,1)S(1)} %get-tuple-element.87), channel_id=1, source_target_pairs={{0,2},{1,7},{2,0},{3,5},{4,6},{5,3},{6,4},{7,1},{8,10},{9,15},{10,... | collective-permute-start | bytes 3981320 | tf_op jit(solution)/shard_map/ppermute | solution.py:282
  49.8 7.8 %collective-permute-done.10.refs_0_ = bf16[648,512]{1,0:T(8,128)(2,1)S(1)} collective-permute-done((bf16[648,512]{1,0:T(8,128)(2,1)S(1)}, bf16[648,512]{1,0:T(8,128)(2,1)S(1)}, u32[]{:S(2)}, u32[]{:S(2)}) %collective-permute-start.10) | collective-permute-done | bytes 663584 | tf_op jit(solution)/shard_map/ppermute | solution.py:313
  58.7 2.8 %collective-permute-start.15 = (bf16[648,512]{1,0:T(8,128)(2,1)S(1)}, bf16[648,512]{1,0:T(8,128)(2,1)S(1)}, u32[]{:S(2)}, u32[]{:S(2)}) collective-permute-start(bf16[648,512]{1,0:T(8,128)(2,1)S(1)} %get-tuple-element.95), channel_id=1, source_target_pairs={{0,16},{1,49},{2,18},{3,51},{4,20},{5,53},{6,22},{7,55},{8,24},{9,... | collective-permute-start | bytes 1990664 | tf_op jit(solution)/shard_map/ppermute | solution.py:315
  61.6 2.3 %m1_product1.1 = (bf16[648,256]{1,0:T(8,128)(2,1)S(1)}, bf16[648,256]{1,0:T(8,128)(2,1)S(1)}, bf16[648,512]{1,0:T(8,128)(2,1)S(1)}, f32[8,128]{1,0:T(8,128)S(1)}) custom-call(bf16[648,648]{1,0:T(8,128)(2,1)S(1)} %get-tuple-element.76.refs_0_, bf16[648,648]{1,0:T(8,128)(2,1)S(1)} %collective-permute-done.refs_1_, ...), custom_call_target="tpu_custom_call" | custom-call | flops 1000 | bytes 1000 | tf_op jit(solution)/shard_map/m1_product1/pallas_call | solution.py:76
  63.9 1.3 collective-permute-done.9.refs_1_
  65.5 3.6 %collective-permute-done.15.refs_0_ = bf16[648,512]{1,0:T(8,128)(2,1)S(1)} collective-permute-done((bf16[648,512]{1,0:T(8,128)(2,1)S(1)}, bf16[648,512]{1,0:T(8,128)(2,1)S(1)}, u32[]{:S(2)}, u32[]{:S(2)}) %collective-permute-start.15) | collective-permute-done | bytes 663584 | tf_op jit(solution)/shard_map/ppermute | solution.py:315
  69.0 7.1 %collective-permute-done.16.refs_1_ = bf16[648,512]{1,0:T(8,128)(2,1)S(1)} collective-permute-done((bf16[648,512]{1,0:T(8,128)(2,1)S(1)}, bf16[648,512]{1,0:T(8,128)(2,1)S(1)}, u32[]{:S(2)}, u32[]{:S(2)}) %collective-permute-start.16) | collective-permute-done | bytes 663584 | tf_op jit(solution)/shard_map/ppermute | solution.py:322
  76.2 1.9 %collective-permute-start.19 = (bf16[648,512]{1,0:T(8,128)(2,1)S(1)}, bf16[648,512]{1,0:T(8,128)(2,1)S(1)}, u32[]{:S(2)}, u32[]{:S(2)}) collective-permute-start(bf16[648,512]{1,0:T(8,128)(2,1)S(1)} %get-tuple-element.103.refs_3_.refs_9_.refs_2_), channel_id=1, source_target_pairs={{0,1},{1,0},{2,3},{3,2},{4,5},{5,4},{6,7},{7,6},{8,9},{9,8},{10,11... | collective-permute-start | bytes 1990664 | tf_op jit(solution)/shard_map/ppermute | solution.py:329
  78.1 2.5 %collective-permute-start.18 = (bf16[648,512]{1,0:T(8,128)(2,1)S(1)}, bf16[648,512]{1,0:T(8,128)(2,1)S(1)}, u32[]{:S(2)}, u32[]{:S(2)}) collective-permute-start(bf16[648,512]{1,0:T(8,128)(2,1)S(1)} %get-tuple-element.101), channel_id=1, source_target_pairs={{0,2},{1,7},{2,0},{3,5},{4,6},{5,3},{6,4},{7,1},{8,10},{9,15},{10,... | collective-permute-start | bytes 1990664 | tf_op jit(solution)/shard_map/ppermute | solution.py:282
  81.5 2.3 %m2_product1.1 = (bf16[648,256]{1,0:T(8,128)(2,1)S(1)}, bf16[648,256]{1,0:T(8,128)(2,1)S(1)}, bf16[648,512]{1,0:T(8,128)(2,1)S(1)}, f32[8,128]{1,0:T(8,128)S(1)}) custom-call(bf16[648,648]{1,0:T(8,128)(2,1)S(1)} %get-tuple-element.76.refs_0_, bf16[648,648]{1,0:T(8,128)(2,1)S(1)} %collective-permute-done.refs_1_, ...), custom_call_target="tpu_custom_call" | custom-call | flops 1000 | bytes 1000 | tf_op jit(solution)/shard_map/m2_product1/pallas_call | solution.py:76
  83.7 5.1 %collective-permute-done.18.refs_1_ = bf16[648,512]{1,0:T(8,128)(2,1)S(1)} collective-permute-done((bf16[648,512]{1,0:T(8,128)(2,1)S(1)}, bf16[648,512]{1,0:T(8,128)(2,1)S(1)}, u32[]{:S(2)}, u32[]{:S(2)}) %collective-permute-start.18) | collective-permute-done | bytes 663584 | tf_op jit(solution)/shard_map/ppermute | solution.py:282
  89.0 2.5 %collective-permute-start.24 = (bf16[648,512]{1,0:T(8,128)(2,1)S(1)}, bf16[648,512]{1,0:T(8,128)(2,1)S(1)}, u32[]{:S(2)}, u32[]{:S(2)}) collective-permute-start(bf16[648,512]{1,0:T(8,128)(2,1)S(1)} %get-tuple-element.113), channel_id=1, source_target_pairs={{0,2},{1,7},{2,0},{3,5},{4,6},{5,3},{6,4},{7,1},{8,10},{9,15},{10,... | collective-permute-start | bytes 1990664 | tf_op jit(solution)/shard_map/ppermute | solution.py:282
  91.6 3.7 %collective-permute-done.21.refs_2_ = bf16[648,256]{1,0:T(8,128)(2,1)S(1)} collective-permute-done((bf16[648,256]{1,0:T(8,128)(2,1)S(1)}, bf16[648,256]{1,0:T(8,128)(2,1)S(1)}, u32[]{:S(2)}, u32[]{:S(2)}) %collective-permute-start.21) | collective-permute-done | bytes 331808 | tf_op jit(solution)/shard_map/ppermute | solution.py:285
  95.4 2.3 %collective-permute-done.17.refs_1_ = bf16[648,512]{1,0:T(8,128)(2,1)S(1)} collective-permute-done((bf16[648,512]{1,0:T(8,128)(2,1)S(1)}, bf16[648,512]{1,0:T(8,128)(2,1)S(1)}, u32[]{:S(2)}, u32[]{:S(2)}) %collective-permute-start.17) | collective-permute-done | bytes 663584 | tf_op jit(solution)/shard_map/ppermute | solution.py:288
  98.4 5.0 %collective-permute-done.24.refs_1_ = bf16[648,512]{1,0:T(8,128)(2,1)S(1)} collective-permute-done((bf16[648,512]{1,0:T(8,128)(2,1)S(1)}, bf16[648,512]{1,0:T(8,128)(2,1)S(1)}, u32[]{:S(2)}, u32[]{:S(2)}) %collective-permute-start.24) | collective-permute-done | bytes 663584 | tf_op jit(solution)/shard_map/ppermute | solution.py:282
  103.4 0.8 collective-permute-start.26
  104.4 5.2 %collective-permute-done.22.refs_1_ = bf16[648,512]{1,0:T(8,128)(2,1)S(1)} collective-permute-done((bf16[648,512]{1,0:T(8,128)(2,1)S(1)}, bf16[648,512]{1,0:T(8,128)(2,1)S(1)}, u32[]{:S(2)}, u32[]{:S(2)}) %collective-permute-start.22) | collective-permute-done | bytes 663584 | tf_op jit(solution)/shard_map/ppermute | solution.py:291
  109.7 2.4 %collective-permute-start.29 = (bf16[648,1024]{1,0:T(8,128)(2,1)S(1)}, bf16[648,1024]{1,0:T(8,128)(2,1)S(1)}, u32[]{:S(2)}, u32[]{:S(2)}) collective-permute-start(bf16[648,1024]{1,0:T(8,128)(2,1)S(1)} %get-tuple-element.117.refs_0_), channel_id=1, source_target_pairs={{0,2},{1,7},{2,0},{3,5},{4,6},{5,3},{6,4},{7,1},{8,10},{9,15},{10,... | collective-permute-start | bytes 3981320 | tf_op jit(solution)/shard_map/ppermute | solution.py:294
  112.1 1.0 collective-permute-done.26.refs_2_
  113.7 5.9 %collective-permute-done.27.refs_1_ = bf16[648,256]{1,0:T(8,128)(2,1)S(1)} collective-permute-done((bf16[648,256]{1,0:T(8,128)(2,1)S(1)}, bf16[648,256]{1,0:T(8,128)(2,1)S(1)}, u32[]{:S(2)}, u32[]{:S(2)}) %collective-permute-start.27) | collective-permute-done | bytes 331808 | tf_op jit(solution)/shard_map/ppermute | solution.py:288
  119.8 3.4 %collective-permute-done.25.refs_1_ = bf16[648,256]{1,0:T(8,128)(2,1)S(1)} collective-permute-done((bf16[648,256]{1,0:T(8,128)(2,1)S(1)}, bf16[648,256]{1,0:T(8,128)(2,1)S(1)}, u32[]{:S(2)}, u32[]{:S(2)}) %collective-permute-start.25) | collective-permute-done | bytes 331808 | tf_op jit(solution)/shard_map/ppermute | solution.py:291
  123.2 2.4 %collective-permute-start.30 = (bf16[648,512]{1,0:T(8,128)(2,1)S(1)}, bf16[648,512]{1,0:T(8,128)(2,1)S(1)}, u32[]{:S(2)}, u32[]{:S(2)}) collective-permute-start(bf16[648,512]{1,0:T(8,128)(2,1)S(1)} %get-tuple-element.125.refs_5_), channel_id=1, source_target_pairs={{0,2},{1,7},{2,0},{3,5},{4,6},{5,3},{6,4},{7,1},{8,10},{9,15},{10,... | collective-permute-start | bytes 1990664 | tf_op jit(solution)/shard_map/ppermute | solution.py:294
  125.6 4.7 %collective-permute-done.28.refs_1_ = bf16[648,256]{1,0:T(8,128)(2,1)S(1)} collective-permute-done((bf16[648,256]{1,0:T(8,128)(2,1)S(1)}, bf16[648,256]{1,0:T(8,128)(2,1)S(1)}, u32[]{:S(2)}, u32[]{:S(2)}) %collective-permute-start.28) | collective-permute-done | bytes 331808 | tf_op jit(solution)/shard_map/ppermute | solution.py:291
  130.3 2.4 %collective-permute-start.31 = (bf16[648,512]{1,0:T(8,128)(2,1)S(1)}, bf16[648,512]{1,0:T(8,128)(2,1)S(1)}, u32[]{:S(2)}, u32[]{:S(2)}) collective-permute-start(bf16[648,512]{1,0:T(8,128)(2,1)S(1)} %get-tuple-element.128.refs_8_), channel_id=1, source_target_pairs={{0,2},{1,7},{2,0},{3,5},{4,6},{5,3},{6,4},{7,1},{8,10},{9,15},{10,... | collective-permute-start | bytes 1990664 | tf_op jit(solution)/shard_map/ppermute | solution.py:294
  132.7 2.3 %n2_product2.2 = (f32[648,648]{1,0:T(8,128)S(1)}, f32[8,128]{1,0:T(8,128)S(1)}) custom-call(bf16[648,1024]{1,0:T(8,128)(2,1)S(1)} %get-tuple-element.117.refs_0_, bf16[648,512]{1,0:T(8,128)(2,1)S(1)} %collective-permute-done.5.refs_4_.refs_1_.refs_2_, bf16[648,512]{1,0:T(8,128)(2,1)S(1)} %collective-permute-done.6.refs_6_.refs_2_.refs_3_, ...), custom_call_target="tpu_custom_call" | custom-call | flops 1000 | bytes 1000 | tf_op jit(solution)/shard_map/n2_product2/pallas_call | solution.py:76
  135.0 2.3 %n2_product2.3 = (f32[648,648]{1,0:T(8,128)S(1)}, f32[8,128]{1,0:T(8,128)S(1)}) custom-call(bf16[648,1024]{1,0:T(8,128)(2,1)S(1)} %get-tuple-element.117.refs_0_, bf16[648,512]{1,0:T(8,128)(2,1)S(1)} %get-tuple-element.78.refs_3_.refs_1_.refs_2_, bf16[648,512]{1,0:T(8,128)(2,1)S(1)} %get-tuple-element.82.refs_5_.refs_2_.refs_3_, ...), custom_call_target="tpu_custom_call" | custom-call | flops 1000 | bytes 1000 | tf_op jit(solution)/shard_map/n2_product2/pallas_call | solution.py:76
  137.3 1.2 t0_product2.2
  138.6 1.3 t0_product2.3
  139.9 5.0 %collective-permute-done.30.refs_1_ = bf16[648,512]{1,0:T(8,128)(2,1)S(1)} collective-permute-done((bf16[648,512]{1,0:T(8,128)(2,1)S(1)}, bf16[648,512]{1,0:T(8,128)(2,1)S(1)}, u32[]{:S(2)}, u32[]{:S(2)}) %collective-permute-start.30) | collective-permute-done | bytes 663584 | tf_op jit(solution)/shard_map/ppermute | solution.py:294
  146.3 5.7 %collective-permute-done.31.refs_1_ = bf16[648,512]{1,0:T(8,128)(2,1)S(1)} collective-permute-done((bf16[648,512]{1,0:T(8,128)(2,1)S(1)}, bf16[648,512]{1,0:T(8,128)(2,1)S(1)}, u32[]{:S(2)}, u32[]{:S(2)}) %collective-permute-start.31) | collective-permute-done | bytes 663584 | tf_op jit(solution)/shard_map/ppermute | solution.py:294
  153.3 1.2 t2_product2.3
  154.6 0.8 collective-permute-done.32.refs_2_
  155.4 2.9 %finish.1 = f32[648,1296]{1,0:T(8,128)} custom-call(f32[648,1]{1,0:T(8,128)S(1)} %mul.11.refs_0_, f32[648,648]{1,0:T(8,128)S(1)} %get-tuple-element.143.refs_1_, bf16[648,648]{1,0:T(8,128)(2,1)S(1)} %collective-permute-done.32.refs_2_), custom_call_target="tpu_custom_call" | custom-call | tf_op jit(solution)/shard_map/finish/pallas_call | solution.py:344
  (56 shorter events, 8.9 us)
Async XLA Ops:
  0.0 1.1 copy-start
  1.2 18.2 %collective-permute-start.2 = (bf16[648,512]{1,0:T(8,128)(2,1)S(1)}, bf16[648,512]{1,0:T(8,128)(2,1)S(1)}, u32[]{:S(2)}, u32[]{:S(2)}) collective-permute-start(bf16[648,512]{1,0:T(8,128)(2,1)S(1)} %get-tuple-element.78.refs_3_.refs_1_.refs_2_), channel_id=1, source_target_pairs={{0,64},{16,80},{32,96},{48,112},{64,0},{80,16},{96,32},{112,48},{1... | collective-permute-start | bytes 1990664 | tf_op jit(solution)/shard_map/ppermute | solution.py:132
  5.0 18.1 %collective-permute-start.3 = (bf16[648,512]{1,0:T(8,128)(2,1)S(1)}, bf16[648,512]{1,0:T(8,128)(2,1)S(1)}, u32[]{:S(2)}, u32[]{:S(2)}) collective-permute-start(bf16[648,512]{1,0:T(8,128)(2,1)S(1)} %get-tuple-element.78.refs_3_.refs_1_.refs_2_), channel_id=1, source_target_pairs={{0,16},{16,32},{32,48},{48,0},{64,80},{80,96},{96,112},{112,64},{1... | collective-permute-start | bytes 1990664 | tf_op jit(solution)/shard_map/ppermute | solution.py:130
  6.7 29.7 %collective-permute-start.4 = (bf16[648,512]{1,0:T(8,128)(2,1)S(1)}, bf16[648,512]{1,0:T(8,128)(2,1)S(1)}, u32[]{:S(2)}, u32[]{:S(2)}) collective-permute-start(bf16[648,512]{1,0:T(8,128)(2,1)S(1)} %get-tuple-element.78.refs_3_.refs_1_.refs_2_), channel_id=1, source_target_pairs={{0,48},{16,0},{32,16},{48,32},{64,112},{80,64},{96,80},{112,96},{1... | collective-permute-start | bytes 1990664 | tf_op jit(solution)/shard_map/ppermute | solution.py:131
  8.8 30.0 %collective-permute-start.1 = (bf16[648,512]{1,0:T(8,128)(2,1)}, bf16[648,512]{1,0:T(8,128)(2,1)S(1)}, u32[]{:S(2)}, u32[]{:S(2)}) collective-permute-start(bf16[648,512]{1,0:T(8,128)(2,1)} %param.9), channel_id=1, source_target_pairs={{0,0},{1,1},{2,18},{3,19},{4,36},{5,37},{6,54},{7,55},{8,64},{9,65... | collective-permute-start | bytes 1990664 | tf_op jit(solution)/shard_map/ppermute | solution.py:127
  10.5 0.7 copy-start.1
  13.4 27.3 %collective-permute-start = (bf16[648,648]{1,0:T(8,128)(2,1)S(1)}, bf16[648,648]{1,0:T(8,128)(2,1)S(1)}, u32[]{:S(2)}, u32[]{:S(2)}) collective-permute-start(bf16[648,648]{1,0:T(8,128)(2,1)S(1)} %get-tuple-element.77), channel_id=1, source_target_pairs={{0,1},{1,0},{2,3},{3,2},{4,5},{5,4},{6,7},{7,6},{8,9},{9,8},{10,11... | collective-permute-start | bytes 2519432 | tf_op jit(solution)/shard_map/ppermute | solution.py:166
  19.4 19.8 %collective-permute-start.5 = (bf16[648,512]{1,0:T(8,128)(2,1)S(1)}, bf16[648,512]{1,0:T(8,128)(2,1)S(1)}, u32[]{:S(2)}, u32[]{:S(2)}) collective-permute-start(bf16[648,512]{1,0:T(8,128)(2,1)S(1)} %get-tuple-element.78.refs_3_.refs_1_.refs_2_), channel_id=1, source_target_pairs={{0,1},{1,0},{2,3},{3,2},{4,5},{5,4},{6,7},{7,6},{8,9},{9,8},{10,11... | collective-permute-start | bytes 1990664 | tf_op jit(solution)/shard_map/ppermute | solution.py:129
  36.6 5.9 %collective-permute-start.8 = (bf16[648,512]{1,0:T(8,128)(2,1)S(1)}, bf16[648,512]{1,0:T(8,128)(2,1)S(1)}, u32[]{:S(2)}, u32[]{:S(2)}) collective-permute-start(bf16[648,512]{1,0:T(8,128)(2,1)S(1)} %get-tuple-element.84.refs_9_.refs_4_.refs_5_), channel_id=1, source_target_pairs={{0,1},{1,0},{2,3},{3,2},{4,5},{5,4},{6,7},{7,6},{8,9},{9,8},{10,11... | collective-permute-start | bytes 1990664 | tf_op jit(solution)/shard_map/ppermute | solution.py:312
  38.7 3.8 %collective-permute-start.6 = (bf16[648,512]{1,0:T(8,128)(2,1)S(1)}, bf16[648,512]{1,0:T(8,128)(2,1)S(1)}, u32[]{:S(2)}, u32[]{:S(2)}) collective-permute-start(bf16[648,512]{1,0:T(8,128)(2,1)S(1)} %get-tuple-element.82.refs_5_.refs_2_.refs_3_), channel_id=1, source_target_pairs={{0,1},{1,0},{2,3},{3,2},{4,5},{5,4},{6,7},{7,6},{8,9},{9,8},{10,11... | collective-permute-start | bytes 1990664 | tf_op jit(solution)/shard_map/ppermute | solution.py:312
  38.8 3.7 %collective-permute-start.7 = (bf16[648,512]{1,0:T(8,128)(2,1)S(1)}, bf16[648,512]{1,0:T(8,128)(2,1)S(1)}, u32[]{:S(2)}, u32[]{:S(2)}) collective-permute-start(bf16[648,512]{1,0:T(8,128)(2,1)S(1)} %get-tuple-element.83.refs_7_.refs_3_.refs_4_), channel_id=1, source_target_pairs={{0,1},{1,0},{2,3},{3,2},{4,5},{5,4},{6,7},{7,6},{8,9},{9,8},{10,11... | collective-permute-start | bytes 1990664 | tf_op jit(solution)/shard_map/ppermute | solution.py:312
  39.2 18.4 %collective-permute-start.10 = (bf16[648,512]{1,0:T(8,128)(2,1)S(1)}, bf16[648,512]{1,0:T(8,128)(2,1)S(1)}, u32[]{:S(2)}, u32[]{:S(2)}) collective-permute-start(bf16[648,512]{1,0:T(8,128)(2,1)S(1)} %get-tuple-element.84.refs_9_.refs_4_.refs_5_), channel_id=1, source_target_pairs={{0,16},{16,32},{32,48},{48,0},{64,80},{80,96},{96,112},{112,64},{1... | collective-permute-start | bytes 1990664 | tf_op jit(solution)/shard_map/ppermute | solution.py:313
  40.7 16.9 %collective-permute-start.11 = (bf16[648,512]{1,0:T(8,128)(2,1)S(1)}, bf16[648,512]{1,0:T(8,128)(2,1)S(1)}, u32[]{:S(2)}, u32[]{:S(2)}) collective-permute-start(bf16[648,512]{1,0:T(8,128)(2,1)S(1)} %get-tuple-element.84.refs_9_.refs_4_.refs_5_), channel_id=1, source_target_pairs={{0,48},{16,0},{32,16},{48,32},{64,112},{80,64},{96,80},{112,96},{1... | collective-permute-start | bytes 1990664 | tf_op jit(solution)/shard_map/ppermute | solution.py:314
  46.9 18.4 %collective-permute-start.9 = (bf16[648,1024]{1,0:T(8,128)(2,1)S(1)}, bf16[648,1024]{1,0:T(8,128)(2,1)S(1)}, u32[]{:S(2)}, u32[]{:S(2)}) collective-permute-start(bf16[648,1024]{1,0:T(8,128)(2,1)S(1)} %get-tuple-element.87), channel_id=1, source_target_pairs={{0,2},{1,7},{2,0},{3,5},{4,6},{5,3},{6,4},{7,1},{8,10},{9,15},{10,... | collective-permute-start | bytes 3981320 | tf_op jit(solution)/shard_map/ppermute | solution.py:282
  57.8 3.8 %collective-permute-start.12 = (bf16[648,512]{1,0:T(8,128)(2,1)S(1)}, bf16[648,512]{1,0:T(8,128)(2,1)S(1)}, u32[]{:S(2)}, u32[]{:S(2)}) collective-permute-start(bf16[648,512]{1,0:T(8,128)(2,1)S(1)} %get-tuple-element.90.refs_3_.refs_6_.refs_2_), channel_id=1, source_target_pairs={{0,1},{1,0},{2,3},{3,2},{4,5},{5,4},{6,7},{7,6},{8,9},{9,8},{10,11... | collective-permute-start | bytes 1990664 | tf_op jit(solution)/shard_map/ppermute | solution.py:321
  58.6 3.0 %collective-permute-start.13 = (bf16[648,512]{1,0:T(8,128)(2,1)S(1)}, bf16[648,512]{1,0:T(8,128)(2,1)S(1)}, u32[]{:S(2)}, u32[]{:S(2)}) collective-permute-start(bf16[648,512]{1,0:T(8,128)(2,1)S(1)} %get-tuple-element.91.refs_5_.refs_7_.refs_3_), channel_id=1, source_target_pairs={{0,1},{1,0},{2,3},{3,2},{4,5},{5,4},{6,7},{7,6},{8,9},{9,8},{10,11... | collective-permute-start | bytes 1990664 | tf_op jit(solution)/shard_map/ppermute | solution.py:321
  58.7 10.4 %collective-permute-start.15 = (bf16[648,512]{1,0:T(8,128)(2,1)S(1)}, bf16[648,512]{1,0:T(8,128)(2,1)S(1)}, u32[]{:S(2)}, u32[]{:S(2)}) collective-permute-start(bf16[648,512]{1,0:T(8,128)(2,1)S(1)} %get-tuple-element.95), channel_id=1, source_target_pairs={{0,16},{1,49},{2,18},{3,51},{4,20},{5,53},{6,22},{7,55},{8,24},{9,... | collective-permute-start | bytes 1990664 | tf_op jit(solution)/shard_map/ppermute | solution.py:315
  61.4 14.7 %collective-permute-start.16 = (bf16[648,512]{1,0:T(8,128)(2,1)S(1)}, bf16[648,512]{1,0:T(8,128)(2,1)S(1)}, u32[]{:S(2)}, u32[]{:S(2)}) collective-permute-start(bf16[648,512]{1,0:T(8,128)(2,1)S(1)} %get-tuple-element.96), channel_id=1, source_target_pairs={{0,16},{1,49},{2,18},{3,51},{4,20},{5,53},{6,22},{7,55},{8,24},{9,... | collective-permute-start | bytes 1990664 | tf_op jit(solution)/shard_map/ppermute | solution.py:322
  65.4 15.2 %collective-permute-start.14 = (bf16[648,512]{1,0:T(8,128)(2,1)S(1)}, bf16[648,512]{1,0:T(8,128)(2,1)S(1)}, u32[]{:S(2)}, u32[]{:S(2)}) collective-permute-start(bf16[648,512]{1,0:T(8,128)(2,1)S(1)} %get-tuple-element.94), channel_id=1, source_target_pairs={{0,6},{1,3},{2,4},{3,1},{4,2},{5,7},{6,0},{7,5},{8,14},{9,11},{10,... | collective-permute-start | bytes 1990664 | tf_op jit(solution)/shard_map/ppermute | solution.py:285
  76.2 5.3 %collective-permute-start.19 = (bf16[648,512]{1,0:T(8,128)(2,1)S(1)}, bf16[648,512]{1,0:T(8,128)(2,1)S(1)}, u32[]{:S(2)}, u32[]{:S(2)}) collective-permute-start(bf16[648,512]{1,0:T(8,128)(2,1)S(1)} %get-tuple-element.103.refs_3_.refs_9_.refs_2_), channel_id=1, source_target_pairs={{0,1},{1,0},{2,3},{3,2},{4,5},{5,4},{6,7},{7,6},{8,9},{9,8},{10,11... | collective-permute-start | bytes 1990664 | tf_op jit(solution)/shard_map/ppermute | solution.py:329
  78.1 3.4 %collective-permute-start.20 = (bf16[648,512]{1,0:T(8,128)(2,1)S(1)}, bf16[648,512]{1,0:T(8,128)(2,1)S(1)}, u32[]{:S(2)}, u32[]{:S(2)}) collective-permute-start(bf16[648,512]{1,0:T(8,128)(2,1)S(1)} %get-tuple-element.104.refs_5_.refs_10_.refs_3_), channel_id=1, source_target_pairs={{0,1},{1,0},{2,3},{3,2},{4,5},{5,4},{6,7},{7,6},{8,9},{9,8},{10,11... | collective-permute-start | bytes 1990664 | tf_op jit(solution)/shard_map/ppermute | solution.py:329
  78.1 10.7 %collective-permute-start.18 = (bf16[648,512]{1,0:T(8,128)(2,1)S(1)}, bf16[648,512]{1,0:T(8,128)(2,1)S(1)}, u32[]{:S(2)}, u32[]{:S(2)}) collective-permute-start(bf16[648,512]{1,0:T(8,128)(2,1)S(1)} %get-tuple-element.101), channel_id=1, source_target_pairs={{0,2},{1,7},{2,0},{3,5},{4,6},{5,3},{6,4},{7,1},{8,10},{9,15},{10,... | collective-permute-start | bytes 1990664 | tf_op jit(solution)/shard_map/ppermute | solution.py:282
  80.8 16.8 %collective-permute-start.17 = (bf16[648,512]{1,0:T(8,128)(2,1)S(1)}, bf16[648,512]{1,0:T(8,128)(2,1)S(1)}, u32[]{:S(2)}, u32[]{:S(2)}) collective-permute-start(bf16[648,512]{1,0:T(8,128)(2,1)S(1)} %get-tuple-element.99.refs_0_), channel_id=1, source_target_pairs={{0,8},{1,9},{2,10},{3,11},{4,12},{5,13},{6,14},{7,15},{8,0},{9,1},... | collective-permute-start | bytes 1990664 | tf_op jit(solution)/shard_map/ppermute | solution.py:288
  88.9 6.3 %collective-permute-start.21 = (bf16[648,256]{1,0:T(8,128)(2,1)S(1)}, bf16[648,256]{1,0:T(8,128)(2,1)S(1)}, u32[]{:S(2)}, u32[]{:S(2)}) collective-permute-start(bf16[648,256]{1,0:T(8,128)(2,1)S(1)} %get-tuple-element.107), channel_id=1, source_target_pairs={{0,6},{1,3},{2,4},{3,1},{4,2},{5,7},{6,0},{7,5},{8,14},{9,11},{10,... | collective-permute-start | bytes 995336 | tf_op jit(solution)/shard_map/ppermute | solution.py:285
  89.0 14.3 %collective-permute-start.24 = (bf16[648,512]{1,0:T(8,128)(2,1)S(1)}, bf16[648,512]{1,0:T(8,128)(2,1)S(1)}, u32[]{:S(2)}, u32[]{:S(2)}) collective-permute-start(bf16[648,512]{1,0:T(8,128)(2,1)S(1)} %get-tuple-element.113), channel_id=1, source_target_pairs={{0,2},{1,7},{2,0},{3,5},{4,6},{5,3},{6,4},{7,1},{8,10},{9,15},{10,... | collective-permute-start | bytes 1990664 | tf_op jit(solution)/shard_map/ppermute | solution.py:282
  97.8 11.8 %collective-permute-start.22 = (bf16[648,512]{1,0:T(8,128)(2,1)S(1)}, bf16[648,512]{1,0:T(8,128)(2,1)S(1)}, u32[]{:S(2)}, u32[]{:S(2)}) collective-permute-start(bf16[648,512]{1,0:T(8,128)(2,1)S(1)} %get-tuple-element.110.refs_0_), channel_id=1, source_target_pairs={{0,6},{1,3},{2,4},{3,1},{4,2},{5,7},{6,0},{7,5},{8,14},{9,11},{10,... | collective-permute-start | bytes 1990664 | tf_op jit(solution)/shard_map/ppermute | solution.py:291
  97.9 6.4 %collective-permute-start.23 = (bf16[648,256]{1,0:T(8,128)(2,1)S(1)}, bf16[648,256]{1,0:T(8,128)(2,1)S(1)}, u32[]{:S(2)}, u32[]{:S(2)}) collective-permute-start(bf16[648,256]{1,0:T(8,128)(2,1)S(1)} %get-tuple-element.111.refs_0_), channel_id=1, source_target_pairs={{0,8},{1,9},{2,10},{3,11},{4,12},{5,13},{6,14},{7,15},{8,0},{9,1},... | collective-permute-start | bytes 995336 | tf_op jit(solution)/shard_map/ppermute | solution.py:288
  103.4 9.7 %collective-permute-start.26 = (bf16[648,256]{1,0:T(8,128)(2,1)S(1)}, bf16[648,256]{1,0:T(8,128)(2,1)S(1)}, u32[]{:S(2)}, u32[]{:S(2)}) collective-permute-start(bf16[648,256]{1,0:T(8,128)(2,1)S(1)} %get-tuple-element.120), channel_id=1, source_target_pairs={{0,6},{1,3},{2,4},{3,1},{4,2},{5,7},{6,0},{7,5},{8,14},{9,11},{10,... | collective-permute-start | bytes 995336 | tf_op jit(solution)/shard_map/ppermute | solution.py:285
  109.7 27.6 %collective-permute-start.29 = (bf16[648,1024]{1,0:T(8,128)(2,1)S(1)}, bf16[648,1024]{1,0:T(8,128)(2,1)S(1)}, u32[]{:S(2)}, u32[]{:S(2)}) collective-permute-start(bf16[648,1024]{1,0:T(8,128)(2,1)S(1)} %get-tuple-element.117.refs_0_), channel_id=1, source_target_pairs={{0,2},{1,7},{2,0},{3,5},{4,6},{5,3},{6,4},{7,1},{8,10},{9,15},{10,... | collective-permute-start | bytes 3981320 | tf_op jit(solution)/shard_map/ppermute | solution.py:294
  113.3 6.3 %collective-permute-start.27 = (bf16[648,256]{1,0:T(8,128)(2,1)S(1)}, bf16[648,256]{1,0:T(8,128)(2,1)S(1)}, u32[]{:S(2)}, u32[]{:S(2)}) collective-permute-start(bf16[648,256]{1,0:T(8,128)(2,1)S(1)} %get-tuple-element.122.refs_0_), channel_id=1, source_target_pairs={{0,8},{1,9},{2,10},{3,11},{4,12},{5,13},{6,14},{7,15},{8,0},{9,1},... | collective-permute-start | bytes 995336 | tf_op jit(solution)/shard_map/ppermute | solution.py:288
  113.7 9.5 %collective-permute-start.25 = (bf16[648,256]{1,0:T(8,128)(2,1)S(1)}, bf16[648,256]{1,0:T(8,128)(2,1)S(1)}, u32[]{:S(2)}, u32[]{:S(2)}) collective-permute-start(bf16[648,256]{1,0:T(8,128)(2,1)S(1)} %get-tuple-element.118.refs_0_), channel_id=1, source_target_pairs={{0,6},{1,3},{2,4},{3,1},{4,2},{5,7},{6,0},{7,5},{8,14},{9,11},{10,... | collective-permute-start | bytes 995336 | tf_op jit(solution)/shard_map/ppermute | solution.py:291
  119.7 10.6 %collective-permute-start.28 = (bf16[648,256]{1,0:T(8,128)(2,1)S(1)}, bf16[648,256]{1,0:T(8,128)(2,1)S(1)}, u32[]{:S(2)}, u32[]{:S(2)}) collective-permute-start(bf16[648,256]{1,0:T(8,128)(2,1)S(1)} %get-tuple-element.126.refs_0_), channel_id=1, source_target_pairs={{0,6},{1,3},{2,4},{3,1},{4,2},{5,7},{6,0},{7,5},{8,14},{9,11},{10,... | collective-permute-start | bytes 995336 | tf_op jit(solution)/shard_map/ppermute | solution.py:291
  123.2 21.6 %collective-permute-start.30 = (bf16[648,512]{1,0:T(8,128)(2,1)S(1)}, bf16[648,512]{1,0:T(8,128)(2,1)S(1)}, u32[]{:S(2)}, u32[]{:S(2)}) collective-permute-start(bf16[648,512]{1,0:T(8,128)(2,1)S(1)} %get-tuple-element.125.refs_5_), channel_id=1, source_target_pairs={{0,2},{1,7},{2,0},{3,5},{4,6},{5,3},{6,4},{7,1},{8,10},{9,15},{10,... | collective-permute-start | bytes 1990664 | tf_op jit(solution)/shard_map/ppermute | solution.py:294
  130.3 21.6 %collective-permute-start.31 = (bf16[648,512]{1,0:T(8,128)(2,1)S(1)}, bf16[648,512]{1,0:T(8,128)(2,1)S(1)}, u32[]{:S(2)}, u32[]{:S(2)}) collective-permute-start(bf16[648,512]{1,0:T(8,128)(2,1)S(1)} %get-tuple-element.128.refs_8_), channel_id=1, source_target_pairs={{0,2},{1,7},{2,0},{3,5},{4,6},{5,3},{6,4},{7,1},{8,10},{9,15},{10,... | collective-permute-start | bytes 1990664 | tf_op jit(solution)/shard_map/ppermute | solution.py:294
  152.0 1.2 copy-start.2
  152.7 2.7 %collective-permute-start.32 = (bf16[648,648]{1,0:T(8,128)(2,1)S(1)}, bf16[648,648]{1,0:T(8,128)(2,1)S(1)}, u32[]{:S(2)}, u32[]{:S(2)}) collective-permute-start(bf16[648,648]{1,0:T(8,128)(2,1)S(1)} %get-tuple-element.144), channel_id=1, source_target_pairs={{0,1},{1,0},{2,3},{3,2},{4,5},{5,4},{6,7},{7,6},{8,9},{9,8},{10,11... | collective-permute-start | bytes 2519432 | tf_op jit(solution)/shard_map/ppermute | solution.py:305

commit v5 on v4

--- a/solution.py
+++ b/solution.py
@@ -12,11 +12,12 @@
 X, Z = 4, 4
 Q = 128
 CHUNKS = (((0, 0), (0, 3), (0, 1), (1, 0)), ((1, 3), (1, 1)), ((0, 2), (1, 2)))
+SHARED = (0,)
 FINISH = 3
 STEPS = (
     "G0", "G3", "M0", "G1", "M1", "S0", "G2", "Y0", "M2",
-    "S1", "Y1", "R0", "S2", "R1", "F0", "Y2", "R2", "F1",
-    "F2", "N2", "T0", "T1", "T2",
+    "S1", "Y1", "R0", "S2", "R1", "F0", "Y2", "R2", "W0",
+    "F1", "F2", "N2", "T1", "T0", "T2",
 )
 
 
@@ -243,6 +244,37 @@
 
         return run("join", body, [jax.ShapeDtypeStruct((rows, 2 * w), BF16)], [a, b], [VM] * 2)[0]
 
+    def is_low():
+        return place()[1] // X == 0
+
+    def join_and_pick(a, b):
+        w = a.shape[1]
+
+        def body(ins, outs, _):
+            outs[0][:, :w] = ins[0][...]
+            outs[0][:, w:] = ins[1][...]
+            for side in range(2):
+
+                @pl.when(is_low() == (side == 0))
+                def _():
+                    outs[1][...] = ins[side][...]
+
+        shapes = [jax.ShapeDtypeStruct((rows, 2 * w), BF16), like(a)]
+        return run("join", body, shapes, [a, b], [VM] * 2, mib=6)
+
+    def merge(mine, across):
+        w = mine.shape[1]
+
+        def body(ins, outs, _):
+            for side in range(2):
+
+                @pl.when(is_low() == (side == 0))
+                def _():
+                    outs[0][:, :w] = ins[side][...]
+                    outs[0][:, w:] = ins[1 - side][...]
+
+        return run("merge", body, [jax.ShapeDtypeStruct((rows, 2 * w), BF16)], [mine, across], [VM] * 2, mib=6)[0]
+
     def matmul2(groups, acc, names, swap, dtype, far):
         begins = acc is None
         args = [] if begins else [acc]
@@ -269,8 +301,9 @@
     last = len(CHUNKS) - 1
     products = [[] for _ in CHUNKS]
     got2, part3, got3, r0, r1, near_half, far_half = ({} for _ in range(7))
+    share, across = {}, {}
     own_sum = oth_sum = back = None
-    begun = done = 0
+    begun = 0
     for step in STEPS:
         run.step = step.lower() + "_"
         stage, c = step[0], int(step[1])
@@ -290,16 +323,24 @@
             r0[c] = add2(part3[c], got3[c])
             r1[c] = lax.ppermute(r0[c], "mode", SECOND)
         elif stage == "F":
-            near_half[c] = join(r0[c], r1[c])
-            far_half[c] = lax.ppermute(near_half[c], "mode", FIRST)
+            if c in SHARED:
+                near_half[c], chosen = join_and_pick(r0[c], r1[c])
+                share[c] = lax.ppermute(chosen, "mode", FIRST)
+            else:
+                near_half[c] = join(r0[c], r1[c])
+                far_half[c] = lax.ppermute(near_half[c], "mode", FIRST)
+        elif stage == "W":
+            (share[c],) = gate([share[c]])
+            across[c] = lax.ppermute(share[c], "mode", YSWAP)
         elif stage == "N":
             group = [(CHUNKS[d], near_half[d]) for d in range(begun, c + 1)]
             begun = c + 1
             oth_sum = matmul2(group, oth_sum, other, True, F32, False)
             own_sum = matmul2(group, own_sum, unit, False, F32, False)
         elif stage == "T":
-            group = [(CHUNKS[d], far_half[d]) for d in range(done, c + 1)]
-            done = c + 1
+            if c in SHARED:
+                far_half[c] = merge(share[c], across[c])
+            group = [(chunk, far_half[c])]
             oth_sum = matmul2(group, oth_sum, other, True, BF16 if c == last else F32, True)
             if c == last:
                 back = lax.ppermute(oth_sum, "mode", KSWAP)

time: 159 us -> 157 us (0.987)
  waiting for transfers between devices: 87.7 us -> 80.5 us
  starting transfers between devices: 42.1 us -> 46.9 us
    ppermute x3 -> x2, waiting for transfers between devices: 10.6 us -> 4.75 us  [on_device(): far_half[c] = lax.ppermute(near_half[c], 'mode', FIRST)]
    ppermute x3, waiting for transfers between devices: 13.3 us -> 8.3 us  [on_device(): r1[c] = lax.ppermute(r0[c], 'mode', SECOND)]
    ppermute x0 -> x2, waiting for transfers between devices: none -> 3.73 us  [the longest x1 3.72 us: on_device(): share[c] = lax.ppermute(chosen, 'mode', FIRST)]
    ppermute x1, starting transfers between devices: 0.52 us -> 4.11 us  [on_device(): back = lax.ppermute(oth_sum, 'mode', KSWAP)]
    ppermute x0 -> x2, starting transfers between devices: none -> 3.44 us  [the longest x1 2.45 us: on_device(): share[c] = lax.ppermute(chosen, 'mode', FIRST)]
    ppermute x3 -> x2, starting transfers between devices: 7.19 us -> 4.88 us  [on_device(): far_half[c] = lax.ppermute(near_half[c], 'mode', FIRST)]
    pallas_call x29 -> x31, Pallas kernels: 23.5 us -> 23.9 us  [__call__(): pl.pallas_call(kernel, out_shape=list(outs) + [TOKEN], in_specs=list(spec...]
  transfers between devices with their start and end apart: 33 -> 34, of which waited for: 19 -> 19; matrix products, arithmetic and copies ran while one was open for 0% -> 0% of each run, Pallas kernels for 14% -> 15%
where the time goes in v5:
time: 157 us; the launch traced here: 156 us
  waiting for transfers between devices  80.5 us (51%)
  starting transfers between devices  46.9 us (30%)
  Pallas kernels  26.8 us (17%)
  local copies, waits for them, and re-layouts  1.92 us (1%)
    pallas_call x31, Pallas kernels, __call__(): pl.pallas_call(kernel, out_shape=list(outs) + [TOKEN], in_specs=list(spec...  23.9 us
    ppermute x1, waiting for transfers between devices, on_device(): unit[0, 1] = lax.ppermute(unit[0, 0], 'cfg', cfg_perm(0, -1))  13.3 us
    ppermute x3, waiting for transfers between devices, on_device(): products[c].append((*got, lax.ppermute(got[2], 'mode', FIRST)))  11.4 us
    ppermute x3, waiting for transfers between devices, on_device(): r1[c] = lax.ppermute(r0[c], 'mode', SECOND)  8.3 us
    ppermute x3, waiting for transfers between devices, on_device(): got3[c] = lax.ppermute(part3[c], 'mode', YSWAP)  8.15 us
    ppermute x3, starting transfers between devices, on_device(): products[c].append((*got, lax.ppermute(got[2], 'mode', FIRST)))  7.91 us
    ppermute x1, waiting for transfers between devices, on_device(): unit[1, 3] = lax.ppermute(unit[1, 0], 'cfg', cfg_perm(0, 1))  7.81 us
    ppermute x1, waiting for transfers between devices, on_device(): unit[1, 2] = lax.ppermute(pick, ('cfg', 'mode'), ONWARD)  7.11 us
  transfers between devices with their start and end apart: 34, of which 19 were waited for; matrix products, arithmetic and copies ran while one was open for 0% of the time, Pallas kernels for 15%

profile of v5, /device:TPU:1, one launch (start us, length us, event | category | flops | bytes accessed | tf_op | source)
XLA Modules:
  0.0 156.2 jit_solution(2790527436162874116)
XLA Ops:
  0.0 1.1 copy-done
  1.2 3.8 %collective-permute-start.2 = (bf16[648,512]{1,0:T(8,128)(2,1)S(1)}, bf16[648,512]{1,0:T(8,128)(2,1)S(1)}, u32[]{:S(2)}, u32[]{:S(2)}) collective-permute-start(bf16[648,512]{1,0:T(8,128)(2,1)S(1)} %get-tuple-element.83.refs_3_.refs_1_.refs_2_), channel_id=1, source_target_pairs={{0,64},{16,80},{32,96},{48,112},{64,0},{80,16},{96,32},{112,48},{1... | collective-permute-start | bytes 1990664 | tf_op jit(solution)/shard_map/ppermute | solution.py:133
  5.0 1.6 %collective-permute-start.3 = (bf16[648,512]{1,0:T(8,128)(2,1)S(1)}, bf16[648,512]{1,0:T(8,128)(2,1)S(1)}, u32[]{:S(2)}, u32[]{:S(2)}) collective-permute-start(bf16[648,512]{1,0:T(8,128)(2,1)S(1)} %get-tuple-element.83.refs_3_.refs_1_.refs_2_), channel_id=1, source_target_pairs={{0,16},{16,32},{32,48},{48,0},{64,80},{80,96},{96,112},{112,64},{1... | collective-permute-start | bytes 1990664 | tf_op jit(solution)/shard_map/ppermute | solution.py:131
  6.7 2.1 %collective-permute-start.4 = (bf16[648,512]{1,0:T(8,128)(2,1)S(1)}, bf16[648,512]{1,0:T(8,128)(2,1)S(1)}, u32[]{:S(2)}, u32[]{:S(2)}) collective-permute-start(bf16[648,512]{1,0:T(8,128)(2,1)S(1)} %get-tuple-element.83.refs_3_.refs_1_.refs_2_), channel_id=1, source_target_pairs={{0,48},{16,0},{32,16},{48,32},{64,112},{80,64},{96,80},{112,96},{1... | collective-permute-start | bytes 1990664 | tf_op jit(solution)/shard_map/ppermute | solution.py:132
  8.8 1.7 %collective-permute-start.1 = (bf16[648,512]{1,0:T(8,128)(2,1)}, bf16[648,512]{1,0:T(8,128)(2,1)S(1)}, u32[]{:S(2)}, u32[]{:S(2)}) collective-permute-start(bf16[648,512]{1,0:T(8,128)(2,1)} %param.9), channel_id=1, source_target_pairs={{0,0},{1,1},{2,18},{3,19},{4,36},{5,37},{6,54},{7,55},{8,64},{9,65... | collective-permute-start | bytes 1990664 | tf_op jit(solution)/shard_map/ppermute | solution.py:128
  11.2 2.2 %polar.1 = (bf16[648,648]{1,0:T(8,128)(2,1)S(1)}, bf16[648,648]{1,0:T(8,128)(2,1)S(1)}, f32[8,128]{1,0:T(8,128)S(1)}) custom-call(f32[648]{0:T(1024)S(1)} %copy-done.1, bf16[648,10368]{1,0:T(8,128)(2,1)} %refs_1_.1, f32[8,128]{1,0:T(8,128)S(1)} %get-tuple-element.80.refs_2_), custom_call_target="tpu_custom_call" | custom-call | flops 1000 | bytes 1000 | tf_op jit(solution)/shard_map/polar/pallas_call | solution.py:77
  13.4 1.3 collective-permute-start
  14.7 4.7 %collective-permute-done.2.refs_0_ = bf16[648,512]{1,0:T(8,128)(2,1)S(1)} collective-permute-done((bf16[648,512]{1,0:T(8,128)(2,1)S(1)}, bf16[648,512]{1,0:T(8,128)(2,1)S(1)}, u32[]{:S(2)}, u32[]{:S(2)}) %collective-permute-start.2) | collective-permute-done | bytes 663584 | tf_op jit(solution)/shard_map/ppermute | solution.py:133
  19.4 1.5 collective-permute-start.5
  20.9 2.2 %collective-permute-done.3.refs_1_ = bf16[648,512]{1,0:T(8,128)(2,1)S(1)} collective-permute-done((bf16[648,512]{1,0:T(8,128)(2,1)S(1)}, bf16[648,512]{1,0:T(8,128)(2,1)S(1)}, u32[]{:S(2)}, u32[]{:S(2)}) %collective-permute-start.3) | collective-permute-done | bytes 663584 | tf_op jit(solution)/shard_map/ppermute | solution.py:131
  23.1 13.3 %collective-permute-done.4.refs_2_ = bf16[648,512]{1,0:T(8,128)(2,1)S(1)} collective-permute-done((bf16[648,512]{1,0:T(8,128)(2,1)S(1)}, bf16[648,512]{1,0:T(8,128)(2,1)S(1)}, u32[]{:S(2)}, u32[]{:S(2)}) %collective-permute-start.4) | collective-permute-done | bytes 663584 | tf_op jit(solution)/shard_map/ppermute | solution.py:132
  36.6 2.1 %collective-permute-start.8 = (bf16[648,512]{1,0:T(8,128)(2,1)S(1)}, bf16[648,512]{1,0:T(8,128)(2,1)S(1)}, u32[]{:S(2)}, u32[]{:S(2)}) collective-permute-start(bf16[648,512]{1,0:T(8,128)(2,1)S(1)} %get-tuple-element.89.refs_9_.refs_4_.refs_5_), channel_id=1, source_target_pairs={{0,1},{1,0},{2,3},{3,2},{4,5},{5,4},{6,7},{7,6},{8,9},{9,8},{10,11... | collective-permute-start | bytes 1990664 | tf_op jit(solution)/shard_map/ppermute | solution.py:353
  39.2 1.5 collective-permute-start.10
  40.7 1.8 %collective-permute-start.11 = (bf16[648,512]{1,0:T(8,128)(2,1)S(1)}, bf16[648,512]{1,0:T(8,128)(2,1)S(1)}, u32[]{:S(2)}, u32[]{:S(2)}) collective-permute-start(bf16[648,512]{1,0:T(8,128)(2,1)S(1)} %get-tuple-element.89.refs_9_.refs_4_.refs_5_), channel_id=1, source_target_pairs={{0,48},{16,0},{32,16},{48,32},{64,112},{80,64},{96,80},{112,96},{1... | collective-permute-start | bytes 1990664 | tf_op jit(solution)/shard_map/ppermute | solution.py:355
  42.5 4.4 %m0_product1.1 = (bf16[648,512]{1,0:T(8,128)(2,1)S(1)}, bf16[648,512]{1,0:T(8,128)(2,1)S(1)}, bf16[648,1024]{1,0:T(8,128)(2,1)S(1)}, f32[8,128]{1,0:T(8,128)S(1)}) custom-call(bf16[648,648]{1,0:T(8,128)(2,1)S(1)} %get-tuple-element.81.refs_0_, bf16[648,648]{1,0:T(8,128)(2,1)S(1)} %collective-permute-done.refs_1_, ...), custom_call_target="tpu_custom_call" | custom-call | flops 1000 | bytes 1000 | tf_op jit(solution)/shard_map/m0_product1/pallas_call | solution.py:77
  46.9 2.9 %collective-permute-start.9 = (bf16[648,1024]{1,0:T(8,128)(2,1)S(1)}, bf16[648,1024]{1,0:T(8,128)(2,1)S(1)}, u32[]{:S(2)}, u32[]{:S(2)}) collective-permute-start(bf16[648,1024]{1,0:T(8,128)(2,1)S(1)} %get-tuple-element.92), channel_id=1, source_target_pairs={{0,2},{1,7},{2,0},{3,5},{4,6},{5,3},{6,4},{7,1},{8,10},{9,15},{10,... | collective-permute-start | bytes 3981320 | tf_op jit(solution)/shard_map/ppermute | solution.py:315
  49.8 7.8 %collective-permute-done.10.refs_0_ = bf16[648,512]{1,0:T(8,128)(2,1)S(1)} collective-permute-done((bf16[648,512]{1,0:T(8,128)(2,1)S(1)}, bf16[648,512]{1,0:T(8,128)(2,1)S(1)}, u32[]{:S(2)}, u32[]{:S(2)}) %collective-permute-start.10) | collective-permute-done | bytes 663584 | tf_op jit(solution)/shard_map/ppermute | solution.py:354
  58.7 2.8 %collective-permute-start.15 = (bf16[648,512]{1,0:T(8,128)(2,1)S(1)}, bf16[648,512]{1,0:T(8,128)(2,1)S(1)}, u32[]{:S(2)}, u32[]{:S(2)}) collective-permute-start(bf16[648,512]{1,0:T(8,128)(2,1)S(1)} %get-tuple-element.100), channel_id=1, source_target_pairs={{0,16},{1,49},{2,18},{3,51},{4,20},{5,53},{6,22},{7,55},{8,24},{9,... | collective-permute-start | bytes 1990664 | tf_op jit(solution)/shard_map/ppermute | solution.py:356
  61.6 2.3 %m1_product1.1 = (bf16[648,256]{1,0:T(8,128)(2,1)S(1)}, bf16[648,256]{1,0:T(8,128)(2,1)S(1)}, bf16[648,512]{1,0:T(8,128)(2,1)S(1)}, f32[8,128]{1,0:T(8,128)S(1)}) custom-call(bf16[648,648]{1,0:T(8,128)(2,1)S(1)} %get-tuple-element.81.refs_0_, bf16[648,648]{1,0:T(8,128)(2,1)S(1)} %collective-permute-done.refs_1_, ...), custom_call_target="tpu_custom_call" | custom-call | flops 1000 | bytes 1000 | tf_op jit(solution)/shard_map/m1_product1/pallas_call | solution.py:77
  63.9 1.3 collective-permute-done.9.refs_1_
  65.5 3.6 %collective-permute-done.15.refs_0_ = bf16[648,512]{1,0:T(8,128)(2,1)S(1)} collective-permute-done((bf16[648,512]{1,0:T(8,128)(2,1)S(1)}, bf16[648,512]{1,0:T(8,128)(2,1)S(1)}, u32[]{:S(2)}, u32[]{:S(2)}) %collective-permute-start.15) | collective-permute-done | bytes 663584 | tf_op jit(solution)/shard_map/ppermute | solution.py:356
  69.0 7.1 %collective-permute-done.16.refs_1_ = bf16[648,512]{1,0:T(8,128)(2,1)S(1)} collective-permute-done((bf16[648,512]{1,0:T(8,128)(2,1)S(1)}, bf16[648,512]{1,0:T(8,128)(2,1)S(1)}, u32[]{:S(2)}, u32[]{:S(2)}) %collective-permute-start.16) | collective-permute-done | bytes 663584 | tf_op jit(solution)/shard_map/ppermute | solution.py:363
  76.2 1.9 %collective-permute-start.19 = (bf16[648,512]{1,0:T(8,128)(2,1)S(1)}, bf16[648,512]{1,0:T(8,128)(2,1)S(1)}, u32[]{:S(2)}, u32[]{:S(2)}) collective-permute-start(bf16[648,512]{1,0:T(8,128)(2,1)S(1)} %get-tuple-element.108.refs_3_.refs_9_.refs_2_), channel_id=1, source_target_pairs={{0,1},{1,0},{2,3},{3,2},{4,5},{5,4},{6,7},{7,6},{8,9},{9,8},{10,11... | collective-permute-start | bytes 1990664 | tf_op jit(solution)/shard_map/ppermute | solution.py:370
  78.1 2.5 %collective-permute-start.18 = (bf16[648,512]{1,0:T(8,128)(2,1)S(1)}, bf16[648,512]{1,0:T(8,128)(2,1)S(1)}, u32[]{:S(2)}, u32[]{:S(2)}) collective-permute-start(bf16[648,512]{1,0:T(8,128)(2,1)S(1)} %get-tuple-element.106), channel_id=1, source_target_pairs={{0,2},{1,7},{2,0},{3,5},{4,6},{5,3},{6,4},{7,1},{8,10},{9,15},{10,... | collective-permute-start | bytes 1990664 | tf_op jit(solution)/shard_map/ppermute | solution.py:315
  81.5 2.3 %m2_product1.1 = (bf16[648,256]{1,0:T(8,128)(2,1)S(1)}, bf16[648,256]{1,0:T(8,128)(2,1)S(1)}, bf16[648,512]{1,0:T(8,128)(2,1)S(1)}, f32[8,128]{1,0:T(8,128)S(1)}) custom-call(bf16[648,648]{1,0:T(8,128)(2,1)S(1)} %get-tuple-element.81.refs_0_, bf16[648,648]{1,0:T(8,128)(2,1)S(1)} %collective-permute-done.refs_1_, ...), custom_call_target="tpu_custom_call" | custom-call | flops 1000 | bytes 1000 | tf_op jit(solution)/shard_map/m2_product1/pallas_call | solution.py:77
  83.7 5.1 %collective-permute-done.18.refs_1_ = bf16[648,512]{1,0:T(8,128)(2,1)S(1)} collective-permute-done((bf16[648,512]{1,0:T(8,128)(2,1)S(1)}, bf16[648,512]{1,0:T(8,128)(2,1)S(1)}, u32[]{:S(2)}, u32[]{:S(2)}) %collective-permute-start.18) | collective-permute-done | bytes 663584 | tf_op jit(solution)/shard_map/ppermute | solution.py:315
  89.0 2.5 %collective-permute-start.24 = (bf16[648,512]{1,0:T(8,128)(2,1)S(1)}, bf16[648,512]{1,0:T(8,128)(2,1)S(1)}, u32[]{:S(2)}, u32[]{:S(2)}) collective-permute-start(bf16[648,512]{1,0:T(8,128)(2,1)S(1)} %get-tuple-element.118), channel_id=1, source_target_pairs={{0,2},{1,7},{2,0},{3,5},{4,6},{5,3},{6,4},{7,1},{8,10},{9,15},{10,... | collective-permute-start | bytes 1990664 | tf_op jit(solution)/shard_map/ppermute | solution.py:315
  91.6 3.7 %collective-permute-done.21.refs_2_ = bf16[648,256]{1,0:T(8,128)(2,1)S(1)} collective-permute-done((bf16[648,256]{1,0:T(8,128)(2,1)S(1)}, bf16[648,256]{1,0:T(8,128)(2,1)S(1)}, u32[]{:S(2)}, u32[]{:S(2)}) %collective-permute-start.21) | collective-permute-done | bytes 331808 | tf_op jit(solution)/shard_map/ppermute | solution.py:318
  95.4 2.3 %collective-permute-done.17.refs_1_ = bf16[648,512]{1,0:T(8,128)(2,1)S(1)} collective-permute-done((bf16[648,512]{1,0:T(8,128)(2,1)S(1)}, bf16[648,512]{1,0:T(8,128)(2,1)S(1)}, u32[]{:S(2)}, u32[]{:S(2)}) %collective-permute-start.17) | collective-permute-done | bytes 663584 | tf_op jit(solution)/shard_map/ppermute | solution.py:321
  98.4 5.0 %collective-permute-done.24.refs_1_ = bf16[648,512]{1,0:T(8,128)(2,1)S(1)} collective-permute-done((bf16[648,512]{1,0:T(8,128)(2,1)S(1)}, bf16[648,512]{1,0:T(8,128)(2,1)S(1)}, u32[]{:S(2)}, u32[]{:S(2)}) %collective-permute-start.24) | collective-permute-done | bytes 663584 | tf_op jit(solution)/shard_map/ppermute | solution.py:315
  104.4 5.2 %collective-permute-done.22.refs_1_ = bf16[648,512]{1,0:T(8,128)(2,1)S(1)} collective-permute-done((bf16[648,512]{1,0:T(8,128)(2,1)S(1)}, bf16[648,512]{1,0:T(8,128)(2,1)S(1)}, u32[]{:S(2)}, u32[]{:S(2)}) %collective-permute-start.22) | collective-permute-done | bytes 663584 | tf_op jit(solution)/shard_map/ppermute | solution.py:324
  109.7 2.4 %collective-permute-start.26 = (bf16[648,512]{1,0:T(8,128)(2,1)S(1)}, bf16[648,512]{1,0:T(8,128)(2,1)S(1)}, u32[]{:S(2)}, u32[]{:S(2)}) collective-permute-start(bf16[648,512]{1,0:T(8,128)(2,1)S(1)} %get-tuple-element.124), channel_id=1, source_target_pairs={{0,2},{1,7},{2,0},{3,5},{4,6},{5,3},{6,4},{7,1},{8,10},{9,15},{10,... | collective-permute-start | bytes 1990664 | tf_op jit(solution)/shard_map/ppermute | solution.py:328
  112.2 0.9 collective-permute-done.27.refs_2_
  113.7 5.9 %collective-permute-done.28.refs_1_ = bf16[648,256]{1,0:T(8,128)(2,1)S(1)} collective-permute-done((bf16[648,256]{1,0:T(8,128)(2,1)S(1)}, bf16[648,256]{1,0:T(8,128)(2,1)S(1)}, u32[]{:S(2)}, u32[]{:S(2)}) %collective-permute-start.28) | collective-permute-done | bytes 331808 | tf_op jit(solution)/shard_map/ppermute | solution.py:321
  119.8 3.7 %collective-permute-done.26.refs_0_ = bf16[648,512]{1,0:T(8,128)(2,1)S(1)} collective-permute-done((bf16[648,512]{1,0:T(8,128)(2,1)S(1)}, bf16[648,512]{1,0:T(8,128)(2,1)S(1)}, u32[]{:S(2)}, u32[]{:S(2)}) %collective-permute-start.26) | collective-permute-done | bytes 663584 | tf_op jit(solution)/shard_map/ppermute | solution.py:328
  123.6 2.6 %collective-permute-start.30 = (bf16[648,512]{1,0:T(8,128)(2,1)S(1)}, bf16[648,512]{1,0:T(8,128)(2,1)S(1)}, u32[]{:S(2)}, u32[]{:S(2)}) collective-permute-start(bf16[648,512]{1,0:T(8,128)(2,1)S(1)} %get-tuple-element.132.refs_5_), channel_id=1, source_target_pairs={{0,2},{1,7},{2,0},{3,5},{4,6},{5,3},{6,4},{7,1},{8,10},{9,15},{10,... | collective-permute-start | bytes 1990664 | tf_op jit(solution)/shard_map/ppermute | solution.py:331
  126.1 1.0 collective-permute-start.31
  127.1 3.1 %collective-permute-done.29.refs_1_ = bf16[648,256]{1,0:T(8,128)(2,1)S(1)} collective-permute-done((bf16[648,256]{1,0:T(8,128)(2,1)S(1)}, bf16[648,256]{1,0:T(8,128)(2,1)S(1)}, u32[]{:S(2)}, u32[]{:S(2)}) %collective-permute-start.29) | collective-permute-done | bytes 331808 | tf_op jit(solution)/shard_map/ppermute | solution.py:324
  130.3 2.3 %collective-permute-start.32 = (bf16[648,512]{1,0:T(8,128)(2,1)S(1)}, bf16[648,512]{1,0:T(8,128)(2,1)S(1)}, u32[]{:S(2)}, u32[]{:S(2)}) collective-permute-start(bf16[648,512]{1,0:T(8,128)(2,1)S(1)} %get-tuple-element.135.refs_8_), channel_id=1, source_target_pairs={{0,2},{1,7},{2,0},{3,5},{4,6},{5,3},{6,4},{7,1},{8,10},{9,15},{10,... | collective-permute-start | bytes 1990664 | tf_op jit(solution)/shard_map/ppermute | solution.py:331
  132.6 2.3 %n2_product2.2 = (f32[648,648]{1,0:T(8,128)S(1)}, f32[8,128]{1,0:T(8,128)S(1)}) custom-call(bf16[648,1024]{1,0:T(8,128)(2,1)S(1)} %get-tuple-element.122.refs_0_, bf16[648,512]{1,0:T(8,128)(2,1)S(1)} %collective-permute-done.5.refs_4_.refs_1_.refs_2_, bf16[648,512]{1,0:T(8,128)(2,1)S(1)} %collective-permute-done.6.refs_6_.refs_2_.refs_3_, ...), custom_call_target="tpu_custom_call" | custom-call | flops 1000 | bytes 1000 | tf_op jit(solution)/shard_map/n2_product2/pallas_call | solution.py:77
  134.9 2.3 %n2_product2.3 = (f32[648,648]{1,0:T(8,128)S(1)}, f32[8,128]{1,0:T(8,128)S(1)}) custom-call(bf16[648,1024]{1,0:T(8,128)(2,1)S(1)} %get-tuple-element.122.refs_0_, bf16[648,512]{1,0:T(8,128)(2,1)S(1)} %get-tuple-element.83.refs_3_.refs_1_.refs_2_, bf16[648,512]{1,0:T(8,128)(2,1)S(1)} %get-tuple-element.87.refs_5_.refs_2_.refs_3_, ...), custom_call_target="tpu_custom_call" | custom-call | flops 1000 | bytes 1000 | tf_op jit(solution)/shard_map/n2_product2/pallas_call | solution.py:77
  137.2 2.0 %collective-permute-done.30.refs_1_ = bf16[648,512]{1,0:T(8,128)(2,1)S(1)} collective-permute-done((bf16[648,512]{1,0:T(8,128)(2,1)S(1)}, bf16[648,512]{1,0:T(8,128)(2,1)S(1)}, u32[]{:S(2)}, u32[]{:S(2)}) %collective-permute-start.30) | collective-permute-done | bytes 663584 | tf_op jit(solution)/shard_map/ppermute | solution.py:331
  141.0 1.2 t0_product2.2
  142.3 1.3 t0_product2.3
  143.6 2.7 %collective-permute-done.32.refs_1_ = bf16[648,512]{1,0:T(8,128)(2,1)S(1)} collective-permute-done((bf16[648,512]{1,0:T(8,128)(2,1)S(1)}, bf16[648,512]{1,0:T(8,128)(2,1)S(1)}, u32[]{:S(2)}, u32[]{:S(2)}) %collective-permute-start.32) | collective-permute-done | bytes 663584 | tf_op jit(solution)/shard_map/ppermute | solution.py:331
  147.0 4.1 %collective-permute-start.33 = (bf16[648,648]{1,0:T(8,128)(2,1)S(1)}, bf16[648,648]{1,0:T(8,128)(2,1)S(1)}, u32[]{:S(2)}, u32[]{:S(2)}) collective-permute-start(bf16[648,648]{1,0:T(8,128)(2,1)S(1)} %get-tuple-element.154), channel_id=1, source_target_pairs={{0,1},{1,0},{2,3},{3,2},{4,5},{5,4},{6,7},{7,6},{8,9},{9,8},{10,11... | collective-permute-start | bytes 2519432 | tf_op jit(solution)/shard_map/ppermute | solution.py:346
  151.3 1.2 t2_product2.3
  153.4 2.9 %finish.1 = f32[648,1296]{1,0:T(8,128)} custom-call(f32[648,1]{1,0:T(8,128)S(1)} %mul.11.refs_0_, f32[648,648]{1,0:T(8,128)S(1)} %get-tuple-element.153.refs_1_, bf16[648,648]{1,0:T(8,128)(2,1)S(1)} %collective-permute-done.33.refs_2_), custom_call_target="tpu_custom_call" | custom-call | tf_op jit(solution)/shard_map/finish/pallas_call | solution.py:385
  (60 shorter events, 10.5 us)
Async XLA Ops:
  0.0 1.1 copy-start
  1.2 18.2 %collective-permute-start.2 = (bf16[648,512]{1,0:T(8,128)(2,1)S(1)}, bf16[648,512]{1,0:T(8,128)(2,1)S(1)}, u32[]{:S(2)}, u32[]{:S(2)}) collective-permute-start(bf16[648,512]{1,0:T(8,128)(2,1)S(1)} %get-tuple-element.83.refs_3_.refs_1_.refs_2_), channel_id=1, source_target_pairs={{0,64},{16,80},{32,96},{48,112},{64,0},{80,16},{96,32},{112,48},{1... | collective-permute-start | bytes 1990664 | tf_op jit(solution)/shard_map/ppermute | solution.py:133
  5.0 18.1 %collective-permute-start.3 = (bf16[648,512]{1,0:T(8,128)(2,1)S(1)}, bf16[648,512]{1,0:T(8,128)(2,1)S(1)}, u32[]{:S(2)}, u32[]{:S(2)}) collective-permute-start(bf16[648,512]{1,0:T(8,128)(2,1)S(1)} %get-tuple-element.83.refs_3_.refs_1_.refs_2_), channel_id=1, source_target_pairs={{0,16},{16,32},{32,48},{48,0},{64,80},{80,96},{96,112},{112,64},{1... | collective-permute-start | bytes 1990664 | tf_op jit(solution)/shard_map/ppermute | solution.py:131
  6.7 29.7 %collective-permute-start.4 = (bf16[648,512]{1,0:T(8,128)(2,1)S(1)}, bf16[648,512]{1,0:T(8,128)(2,1)S(1)}, u32[]{:S(2)}, u32[]{:S(2)}) collective-permute-start(bf16[648,512]{1,0:T(8,128)(2,1)S(1)} %get-tuple-element.83.refs_3_.refs_1_.refs_2_), channel_id=1, source_target_pairs={{0,48},{16,0},{32,16},{48,32},{64,112},{80,64},{96,80},{112,96},{1... | collective-permute-start | bytes 1990664 | tf_op jit(solution)/shard_map/ppermute | solution.py:132
  8.8 30.0 %collective-permute-start.1 = (bf16[648,512]{1,0:T(8,128)(2,1)}, bf16[648,512]{1,0:T(8,128)(2,1)S(1)}, u32[]{:S(2)}, u32[]{:S(2)}) collective-permute-start(bf16[648,512]{1,0:T(8,128)(2,1)} %param.9), channel_id=1, source_target_pairs={{0,0},{1,1},{2,18},{3,19},{4,36},{5,37},{6,54},{7,55},{8,64},{9,65... | collective-permute-start | bytes 1990664 | tf_op jit(solution)/shard_map/ppermute | solution.py:128
  10.5 0.7 copy-start.1
  13.4 27.3 %collective-permute-start = (bf16[648,648]{1,0:T(8,128)(2,1)S(1)}, bf16[648,648]{1,0:T(8,128)(2,1)S(1)}, u32[]{:S(2)}, u32[]{:S(2)}) collective-permute-start(bf16[648,648]{1,0:T(8,128)(2,1)S(1)} %get-tuple-element.82), channel_id=1, source_target_pairs={{0,1},{1,0},{2,3},{3,2},{4,5},{5,4},{6,7},{7,6},{8,9},{9,8},{10,11... | collective-permute-start | bytes 2519432 | tf_op jit(solution)/shard_map/ppermute | solution.py:167
  19.4 19.8 %collective-permute-start.5 = (bf16[648,512]{1,0:T(8,128)(2,1)S(1)}, bf16[648,512]{1,0:T(8,128)(2,1)S(1)}, u32[]{:S(2)}, u32[]{:S(2)}) collective-permute-start(bf16[648,512]{1,0:T(8,128)(2,1)S(1)} %get-tuple-element.83.refs_3_.refs_1_.refs_2_), channel_id=1, source_target_pairs={{0,1},{1,0},{2,3},{3,2},{4,5},{5,4},{6,7},{7,6},{8,9},{9,8},{10,11... | collective-permute-start | bytes 1990664 | tf_op jit(solution)/shard_map/ppermute | solution.py:130
  36.6 5.9 %collective-permute-start.8 = (bf16[648,512]{1,0:T(8,128)(2,1)S(1)}, bf16[648,512]{1,0:T(8,128)(2,1)S(1)}, u32[]{:S(2)}, u32[]{:S(2)}) collective-permute-start(bf16[648,512]{1,0:T(8,128)(2,1)S(1)} %get-tuple-element.89.refs_9_.refs_4_.refs_5_), channel_id=1, source_target_pairs={{0,1},{1,0},{2,3},{3,2},{4,5},{5,4},{6,7},{7,6},{8,9},{9,8},{10,11... | collective-permute-start | bytes 1990664 | tf_op jit(solution)/shard_map/ppermute | solution.py:353
  38.7 3.8 %collective-permute-start.6 = (bf16[648,512]{1,0:T(8,128)(2,1)S(1)}, bf16[648,512]{1,0:T(8,128)(2,1)S(1)}, u32[]{:S(2)}, u32[]{:S(2)}) collective-permute-start(bf16[648,512]{1,0:T(8,128)(2,1)S(1)} %get-tuple-element.87.refs_5_.refs_2_.refs_3_), channel_id=1, source_target_pairs={{0,1},{1,0},{2,3},{3,2},{4,5},{5,4},{6,7},{7,6},{8,9},{9,8},{10,11... | collective-permute-start | bytes 1990664 | tf_op jit(solution)/shard_map/ppermute | solution.py:353
  38.8 3.7 %collective-permute-start.7 = (bf16[648,512]{1,0:T(8,128)(2,1)S(1)}, bf16[648,512]{1,0:T(8,128)(2,1)S(1)}, u32[]{:S(2)}, u32[]{:S(2)}) collective-permute-start(bf16[648,512]{1,0:T(8,128)(2,1)S(1)} %get-tuple-element.88.refs_7_.refs_3_.refs_4_), channel_id=1, source_target_pairs={{0,1},{1,0},{2,3},{3,2},{4,5},{5,4},{6,7},{7,6},{8,9},{9,8},{10,11... | collective-permute-start | bytes 1990664 | tf_op jit(solution)/shard_map/ppermute | solution.py:353
  39.2 18.4 %collective-permute-start.10 = (bf16[648,512]{1,0:T(8,128)(2,1)S(1)}, bf16[648,512]{1,0:T(8,128)(2,1)S(1)}, u32[]{:S(2)}, u32[]{:S(2)}) collective-permute-start(bf16[648,512]{1,0:T(8,128)(2,1)S(1)} %get-tuple-element.89.refs_9_.refs_4_.refs_5_), channel_id=1, source_target_pairs={{0,16},{16,32},{32,48},{48,0},{64,80},{80,96},{96,112},{112,64},{1... | collective-permute-start | bytes 1990664 | tf_op jit(solution)/shard_map/ppermute | solution.py:354
  40.7 16.9 %collective-permute-start.11 = (bf16[648,512]{1,0:T(8,128)(2,1)S(1)}, bf16[648,512]{1,0:T(8,128)(2,1)S(1)}, u32[]{:S(2)}, u32[]{:S(2)}) collective-permute-start(bf16[648,512]{1,0:T(8,128)(2,1)S(1)} %get-tuple-element.89.refs_9_.refs_4_.refs_5_), channel_id=1, source_target_pairs={{0,48},{16,0},{32,16},{48,32},{64,112},{80,64},{96,80},{112,96},{1... | collective-permute-start | bytes 1990664 | tf_op jit(solution)/shard_map/ppermute | solution.py:355
  46.9 18.4 %collective-permute-start.9 = (bf16[648,1024]{1,0:T(8,128)(2,1)S(1)}, bf16[648,1024]{1,0:T(8,128)(2,1)S(1)}, u32[]{:S(2)}, u32[]{:S(2)}) collective-permute-start(bf16[648,1024]{1,0:T(8,128)(2,1)S(1)} %get-tuple-element.92), channel_id=1, source_target_pairs={{0,2},{1,7},{2,0},{3,5},{4,6},{5,3},{6,4},{7,1},{8,10},{9,15},{10,... | collective-permute-start | bytes 3981320 | tf_op jit(solution)/shard_map/ppermute | solution.py:315
  57.8 3.8 %collective-permute-start.12 = (bf16[648,512]{1,0:T(8,128)(2,1)S(1)}, bf16[648,512]{1,0:T(8,128)(2,1)S(1)}, u32[]{:S(2)}, u32[]{:S(2)}) collective-permute-start(bf16[648,512]{1,0:T(8,128)(2,1)S(1)} %get-tuple-element.95.refs_3_.refs_6_.refs_2_), channel_id=1, source_target_pairs={{0,1},{1,0},{2,3},{3,2},{4,5},{5,4},{6,7},{7,6},{8,9},{9,8},{10,11... | collective-permute-start | bytes 1990664 | tf_op jit(solution)/shard_map/ppermute | solution.py:362
  58.6 3.0 %collective-permute-start.13 = (bf16[648,512]{1,0:T(8,128)(2,1)S(1)}, bf16[648,512]{1,0:T(8,128)(2,1)S(1)}, u32[]{:S(2)}, u32[]{:S(2)}) collective-permute-start(bf16[648,512]{1,0:T(8,128)(2,1)S(1)} %get-tuple-element.96.refs_5_.refs_7_.refs_3_), channel_id=1, source_target_pairs={{0,1},{1,0},{2,3},{3,2},{4,5},{5,4},{6,7},{7,6},{8,9},{9,8},{10,11... | collective-permute-start | bytes 1990664 | tf_op jit(solution)/shard_map/ppermute | solution.py:362
  58.7 10.4 %collective-permute-start.15 = (bf16[648,512]{1,0:T(8,128)(2,1)S(1)}, bf16[648,512]{1,0:T(8,128)(2,1)S(1)}, u32[]{:S(2)}, u32[]{:S(2)}) collective-permute-start(bf16[648,512]{1,0:T(8,128)(2,1)S(1)} %get-tuple-element.100), channel_id=1, source_target_pairs={{0,16},{1,49},{2,18},{3,51},{4,20},{5,53},{6,22},{7,55},{8,24},{9,... | collective-permute-start | bytes 1990664 | tf_op jit(solution)/shard_map/ppermute | solution.py:356
  61.4 14.7 %collective-permute-start.16 = (bf16[648,512]{1,0:T(8,128)(2,1)S(1)}, bf16[648,512]{1,0:T(8,128)(2,1)S(1)}, u32[]{:S(2)}, u32[]{:S(2)}) collective-permute-start(bf16[648,512]{1,0:T(8,128)(2,1)S(1)} %get-tuple-element.101), channel_id=1, source_target_pairs={{0,16},{1,49},{2,18},{3,51},{4,20},{5,53},{6,22},{7,55},{8,24},{9,... | collective-permute-start | bytes 1990664 | tf_op jit(solution)/shard_map/ppermute | solution.py:363
  65.4 15.2 %collective-permute-start.14 = (bf16[648,512]{1,0:T(8,128)(2,1)S(1)}, bf16[648,512]{1,0:T(8,128)(2,1)S(1)}, u32[]{:S(2)}, u32[]{:S(2)}) collective-permute-start(bf16[648,512]{1,0:T(8,128)(2,1)S(1)} %get-tuple-element.99), channel_id=1, source_target_pairs={{0,6},{1,3},{2,4},{3,1},{4,2},{5,7},{6,0},{7,5},{8,14},{9,11},{10,... | collective-permute-start | bytes 1990664 | tf_op jit(solution)/shard_map/ppermute | solution.py:318
  76.2 5.3 %collective-permute-start.19 = (bf16[648,512]{1,0:T(8,128)(2,1)S(1)}, bf16[648,512]{1,0:T(8,128)(2,1)S(1)}, u32[]{:S(2)}, u32[]{:S(2)}) collective-permute-start(bf16[648,512]{1,0:T(8,128)(2,1)S(1)} %get-tuple-element.108.refs_3_.refs_9_.refs_2_), channel_id=1, source_target_pairs={{0,1},{1,0},{2,3},{3,2},{4,5},{5,4},{6,7},{7,6},{8,9},{9,8},{10,11... | collective-permute-start | bytes 1990664 | tf_op jit(solution)/shard_map/ppermute | solution.py:370
  78.1 3.4 %collective-permute-start.20 = (bf16[648,512]{1,0:T(8,128)(2,1)S(1)}, bf16[648,512]{1,0:T(8,128)(2,1)S(1)}, u32[]{:S(2)}, u32[]{:S(2)}) collective-permute-start(bf16[648,512]{1,0:T(8,128)(2,1)S(1)} %get-tuple-element.109.refs_5_.refs_10_.refs_3_), channel_id=1, source_target_pairs={{0,1},{1,0},{2,3},{3,2},{4,5},{5,4},{6,7},{7,6},{8,9},{9,8},{10,11... | collective-permute-start | bytes 1990664 | tf_op jit(solution)/shard_map/ppermute | solution.py:370
  78.1 10.7 %collective-permute-start.18 = (bf16[648,512]{1,0:T(8,128)(2,1)S(1)}, bf16[648,512]{1,0:T(8,128)(2,1)S(1)}, u32[]{:S(2)}, u32[]{:S(2)}) collective-permute-start(bf16[648,512]{1,0:T(8,128)(2,1)S(1)} %get-tuple-element.106), channel_id=1, source_target_pairs={{0,2},{1,7},{2,0},{3,5},{4,6},{5,3},{6,4},{7,1},{8,10},{9,15},{10,... | collective-permute-start | bytes 1990664 | tf_op jit(solution)/shard_map/ppermute | solution.py:315
  80.8 16.8 %collective-permute-start.17 = (bf16[648,512]{1,0:T(8,128)(2,1)S(1)}, bf16[648,512]{1,0:T(8,128)(2,1)S(1)}, u32[]{:S(2)}, u32[]{:S(2)}) collective-permute-start(bf16[648,512]{1,0:T(8,128)(2,1)S(1)} %get-tuple-element.104.refs_0_), channel_id=1, source_target_pairs={{0,8},{1,9},{2,10},{3,11},{4,12},{5,13},{6,14},{7,15},{8,0},{9,1},... | collective-permute-start | bytes 1990664 | tf_op jit(solution)/shard_map/ppermute | solution.py:321
  88.9 6.3 %collective-permute-start.21 = (bf16[648,256]{1,0:T(8,128)(2,1)S(1)}, bf16[648,256]{1,0:T(8,128)(2,1)S(1)}, u32[]{:S(2)}, u32[]{:S(2)}) collective-permute-start(bf16[648,256]{1,0:T(8,128)(2,1)S(1)} %get-tuple-element.112), channel_id=1, source_target_pairs={{0,6},{1,3},{2,4},{3,1},{4,2},{5,7},{6,0},{7,5},{8,14},{9,11},{10,... | collective-permute-start | bytes 995336 | tf_op jit(solution)/shard_map/ppermute | solution.py:318
  89.0 14.3 %collective-permute-start.24 = (bf16[648,512]{1,0:T(8,128)(2,1)S(1)}, bf16[648,512]{1,0:T(8,128)(2,1)S(1)}, u32[]{:S(2)}, u32[]{:S(2)}) collective-permute-start(bf16[648,512]{1,0:T(8,128)(2,1)S(1)} %get-tuple-element.118), channel_id=1, source_target_pairs={{0,2},{1,7},{2,0},{3,5},{4,6},{5,3},{6,4},{7,1},{8,10},{9,15},{10,... | collective-permute-start | bytes 1990664 | tf_op jit(solution)/shard_map/ppermute | solution.py:315
  97.8 11.8 %collective-permute-start.22 = (bf16[648,512]{1,0:T(8,128)(2,1)S(1)}, bf16[648,512]{1,0:T(8,128)(2,1)S(1)}, u32[]{:S(2)}, u32[]{:S(2)}) collective-permute-start(bf16[648,512]{1,0:T(8,128)(2,1)S(1)} %get-tuple-element.115.refs_0_), channel_id=1, source_target_pairs={{0,6},{1,3},{2,4},{3,1},{4,2},{5,7},{6,0},{7,5},{8,14},{9,11},{10,... | collective-permute-start | bytes 1990664 | tf_op jit(solution)/shard_map/ppermute | solution.py:324
  97.9 6.4 %collective-permute-start.23 = (bf16[648,256]{1,0:T(8,128)(2,1)S(1)}, bf16[648,256]{1,0:T(8,128)(2,1)S(1)}, u32[]{:S(2)}, u32[]{:S(2)}) collective-permute-start(bf16[648,256]{1,0:T(8,128)(2,1)S(1)} %get-tuple-element.116.refs_0_), channel_id=1, source_target_pairs={{0,8},{1,9},{2,10},{3,11},{4,12},{5,13},{6,14},{7,15},{8,0},{9,1},... | collective-permute-start | bytes 995336 | tf_op jit(solution)/shard_map/ppermute | solution.py:321
  103.4 9.7 %collective-permute-start.27 = (bf16[648,256]{1,0:T(8,128)(2,1)S(1)}, bf16[648,256]{1,0:T(8,128)(2,1)S(1)}, u32[]{:S(2)}, u32[]{:S(2)}) collective-permute-start(bf16[648,256]{1,0:T(8,128)(2,1)S(1)} %get-tuple-element.126), channel_id=1, source_target_pairs={{0,6},{1,3},{2,4},{3,1},{4,2},{5,7},{6,0},{7,5},{8,14},{9,11},{10,... | collective-permute-start | bytes 995336 | tf_op jit(solution)/shard_map/ppermute | solution.py:318
  109.7 13.8 %collective-permute-start.26 = (bf16[648,512]{1,0:T(8,128)(2,1)S(1)}, bf16[648,512]{1,0:T(8,128)(2,1)S(1)}, u32[]{:S(2)}, u32[]{:S(2)}) collective-permute-start(bf16[648,512]{1,0:T(8,128)(2,1)S(1)} %get-tuple-element.124), channel_id=1, source_target_pairs={{0,2},{1,7},{2,0},{3,5},{4,6},{5,3},{6,4},{7,1},{8,10},{9,15},{10,... | collective-permute-start | bytes 1990664 | tf_op jit(solution)/shard_map/ppermute | solution.py:328
  113.3 6.3 %collective-permute-start.28 = (bf16[648,256]{1,0:T(8,128)(2,1)S(1)}, bf16[648,256]{1,0:T(8,128)(2,1)S(1)}, u32[]{:S(2)}, u32[]{:S(2)}) collective-permute-start(bf16[648,256]{1,0:T(8,128)(2,1)S(1)} %get-tuple-element.128.refs_0_), channel_id=1, source_target_pairs={{0,8},{1,9},{2,10},{3,11},{4,12},{5,13},{6,14},{7,15},{8,0},{9,1},... | collective-permute-start | bytes 995336 | tf_op jit(solution)/shard_map/ppermute | solution.py:321
  113.7 9.8 %collective-permute-start.25 = (bf16[648,256]{1,0:T(8,128)(2,1)S(1)}, bf16[648,256]{1,0:T(8,128)(2,1)S(1)}, u32[]{:S(2)}, u32[]{:S(2)}) collective-permute-start(bf16[648,256]{1,0:T(8,128)(2,1)S(1)} %get-tuple-element.123.refs_0_), channel_id=1, source_target_pairs={{0,6},{1,3},{2,4},{3,1},{4,2},{5,7},{6,0},{7,5},{8,14},{9,11},{10,... | collective-permute-start | bytes 995336 | tf_op jit(solution)/shard_map/ppermute | solution.py:324
  119.7 10.5 %collective-permute-start.29 = (bf16[648,256]{1,0:T(8,128)(2,1)S(1)}, bf16[648,256]{1,0:T(8,128)(2,1)S(1)}, u32[]{:S(2)}, u32[]{:S(2)}) collective-permute-start(bf16[648,256]{1,0:T(8,128)(2,1)S(1)} %get-tuple-element.133.refs_0_), channel_id=1, source_target_pairs={{0,6},{1,3},{2,4},{3,1},{4,2},{5,7},{6,0},{7,5},{8,14},{9,11},{10,... | collective-permute-start | bytes 995336 | tf_op jit(solution)/shard_map/ppermute | solution.py:324
  123.6 15.6 %collective-permute-start.30 = (bf16[648,512]{1,0:T(8,128)(2,1)S(1)}, bf16[648,512]{1,0:T(8,128)(2,1)S(1)}, u32[]{:S(2)}, u32[]{:S(2)}) collective-permute-start(bf16[648,512]{1,0:T(8,128)(2,1)S(1)} %get-tuple-element.132.refs_5_), channel_id=1, source_target_pairs={{0,2},{1,7},{2,0},{3,5},{4,6},{5,3},{6,4},{7,1},{8,10},{9,15},{10,... | collective-permute-start | bytes 1990664 | tf_op jit(solution)/shard_map/ppermute | solution.py:331
  126.1 14.5 %collective-permute-start.31 = (bf16[648,512]{1,0:T(8,128)(2,1)S(1)}, bf16[648,512]{1,0:T(8,128)(2,1)S(1)}, u32[]{:S(2)}, u32[]{:S(2)}) collective-permute-start(bf16[648,512]{1,0:T(8,128)(2,1)S(1)} %get-tuple-element.143.refs_0_), channel_id=1, source_target_pairs={{0,8},{1,9},{2,10},{3,11},{4,12},{5,13},{6,14},{7,15},{8,0},{9,1},... | collective-permute-start | bytes 1990664 | tf_op jit(solution)/shard_map/ppermute | solution.py:334
  130.3 16.0 %collective-permute-start.32 = (bf16[648,512]{1,0:T(8,128)(2,1)S(1)}, bf16[648,512]{1,0:T(8,128)(2,1)S(1)}, u32[]{:S(2)}, u32[]{:S(2)}) collective-permute-start(bf16[648,512]{1,0:T(8,128)(2,1)S(1)} %get-tuple-element.135.refs_8_), channel_id=1, source_target_pairs={{0,2},{1,7},{2,0},{3,5},{4,6},{5,3},{6,4},{7,1},{8,10},{9,15},{10,... | collective-permute-start | bytes 1990664 | tf_op jit(solution)/shard_map/ppermute | solution.py:331
  146.3 4.8 %copy-start.2 = (f32[648]{0:T(1024)S(1)}, f32[648]{0:T(1024)}, u32[]{:S(2)}) copy-start(f32[648]{0:T(1024)} %param.7) | copy-start | bytes 7780
  147.0 6.3 %collective-permute-start.33 = (bf16[648,648]{1,0:T(8,128)(2,1)S(1)}, bf16[648,648]{1,0:T(8,128)(2,1)S(1)}, u32[]{:S(2)}, u32[]{:S(2)}) collective-permute-start(bf16[648,648]{1,0:T(8,128)(2,1)S(1)} %get-tuple-element.154), channel_id=1, source_target_pairs={{0,1},{1,0},{2,3},{3,2},{4,5},{5,4},{6,7},{7,6},{8,9},{9,8},{10,11... | collective-permute-start | bytes 2519432 | tf_op jit(solution)/shard_map/ppermute | solution.py:346

commit v6 on v5

--- a/solution.py
+++ b/solution.py
@@ -16,7 +16,7 @@
 FINISH = 3
 STEPS = (
     "G0", "G3", "M0", "G1", "M1", "S0", "G2", "Y0", "M2",
-    "S1", "Y1", "R0", "S2", "R1", "F0", "Y2", "R2", "W0",
+    "S1", "Y1", "S2", "R0", "R1", "F0", "Y2", "R2", "W0",
     "F1", "F2", "N2", "T1", "T0", "T2",
 )
 

time: 157 us -> 155 us (0.987)
  starting transfers between devices: 46.9 us -> 40.4 us
  waiting for transfers between devices: 80.5 us -> 85.7 us
    ppermute x3, waiting for transfers between devices: 4.63 us -> 13.1 us  [on_device(): got2[c] = lax.ppermute(v, 'mode', SECOND)]
    ppermute x3, waiting for transfers between devices: 11.4 us -> 4.18 us  [on_device(): products[c].append((*got, lax.ppermute(got[2], 'mode', FIRST)))]
    ppermute x3, waiting for transfers between devices: 8.15 us -> 15.1 us  [on_device(): got3[c] = lax.ppermute(part3[c], 'mode', YSWAP)]
    ppermute x2, starting transfers between devices: 4.88 us -> 1.05 us  [on_device(): far_half[c] = lax.ppermute(near_half[c], 'mode', FIRST)]
    ppermute x1, waiting for transfers between devices: 3.72 us -> 1.27 us  [on_device(): share[c] = lax.ppermute(chosen, 'mode', FIRST)]
    ppermute x1, starting transfers between devices: 2.45 us -> 0.09 us  [on_device(): share[c] = lax.ppermute(chosen, 'mode', FIRST)]
    ppermute x1, starting transfers between devices: 4.11 us -> 1.85 us  [on_device(): back = lax.ppermute(oth_sum, 'mode', KSWAP)]
    ppermute x3, starting transfers between devices: 0.2 us -> 2.28 us  [on_device(): r1[c] = lax.ppermute(r0[c], 'mode', SECOND)]
  transfers between devices with their start and end apart: 34 -> 34, of which waited for: 19 -> 20; matrix products, arithmetic and copies ran while one was open for 0% -> 0% of each run, Pallas kernels for 15% -> 15%
where the time goes in v6:
time: 155 us
  waiting for transfers between devices  85.7 us (55%)
  starting transfers between devices  40.4 us (26%)
  Pallas kernels  26.8 us (17%)
  local copies, waits for them, and re-layouts  1.92 us (1%)
    pallas_call x31, Pallas kernels, __call__(): pl.pallas_call(kernel, out_shape=list(outs) + [TOKEN], in_specs=list(spec...  23.9 us
    ppermute x3, waiting for transfers between devices, on_device(): got3[c] = lax.ppermute(part3[c], 'mode', YSWAP)  15.1 us
    ppermute x1, waiting for transfers between devices, on_device(): unit[0, 1] = lax.ppermute(unit[0, 0], 'cfg', cfg_perm(0, -1))  13.3 us
    ppermute x3, waiting for transfers between devices, on_device(): got2[c] = lax.ppermute(v, 'mode', SECOND)  13.1 us
    ppermute x3, starting transfers between devices, on_device(): products[c].append((*got, lax.ppermute(got[2], 'mode', FIRST)))  7.87 us
    ppermute x1, waiting for transfers between devices, on_device(): unit[1, 3] = lax.ppermute(unit[1, 0], 'cfg', cfg_perm(0, 1))  7.81 us
    ppermute x1, waiting for transfers between devices, on_device(): unit[1, 2] = lax.ppermute(pick, ('cfg', 'mode'), ONWARD)  7.11 us
    ppermute x3, waiting for transfers between devices, on_device(): r1[c] = lax.ppermute(r0[c], 'mode', SECOND)  6.9 us
  transfers between devices with their start and end apart: 34, of which 20 were waited for; matrix products, arithmetic and copies ran while one was open for 0% of the time, Pallas kernels for 15%

profile of v6, /device:TPU:1, one launch (start us, length us, event | category | flops | bytes accessed | tf_op | source)
XLA Modules:
  0.0 155.0 jit_solution(9604045110050502440)
XLA Ops:
  0.0 1.1 copy-done
  1.2 3.8 %collective-permute-start.2 = (bf16[648,512]{1,0:T(8,128)(2,1)S(1)}, bf16[648,512]{1,0:T(8,128)(2,1)S(1)}, u32[]{:S(2)}, u32[]{:S(2)}) collective-permute-start(bf16[648,512]{1,0:T(8,128)(2,1)S(1)} %get-tuple-element.83.refs_3_.refs_1_.refs_2_), channel_id=1, source_target_pairs={{0,64},{16,80},{32,96},{48,112},{64,0},{80,16},{96,32},{112,48},{1... | collective-permute-start | bytes 1990664 | tf_op jit(solution)/shard_map/ppermute | solution.py:133
  5.0 1.6 %collective-permute-start.3 = (bf16[648,512]{1,0:T(8,128)(2,1)S(1)}, bf16[648,512]{1,0:T(8,128)(2,1)S(1)}, u32[]{:S(2)}, u32[]{:S(2)}) collective-permute-start(bf16[648,512]{1,0:T(8,128)(2,1)S(1)} %get-tuple-element.83.refs_3_.refs_1_.refs_2_), channel_id=1, source_target_pairs={{0,16},{16,32},{32,48},{48,0},{64,80},{80,96},{96,112},{112,64},{1... | collective-permute-start | bytes 1990664 | tf_op jit(solution)/shard_map/ppermute | solution.py:131
  6.7 2.1 %collective-permute-start.4 = (bf16[648,512]{1,0:T(8,128)(2,1)S(1)}, bf16[648,512]{1,0:T(8,128)(2,1)S(1)}, u32[]{:S(2)}, u32[]{:S(2)}) collective-permute-start(bf16[648,512]{1,0:T(8,128)(2,1)S(1)} %get-tuple-element.83.refs_3_.refs_1_.refs_2_), channel_id=1, source_target_pairs={{0,48},{16,0},{32,16},{48,32},{64,112},{80,64},{96,80},{112,96},{1... | collective-permute-start | bytes 1990664 | tf_op jit(solution)/shard_map/ppermute | solution.py:132
  8.8 1.7 %collective-permute-start.1 = (bf16[648,512]{1,0:T(8,128)(2,1)}, bf16[648,512]{1,0:T(8,128)(2,1)S(1)}, u32[]{:S(2)}, u32[]{:S(2)}) collective-permute-start(bf16[648,512]{1,0:T(8,128)(2,1)} %param.9), channel_id=1, source_target_pairs={{0,0},{1,1},{2,18},{3,19},{4,36},{5,37},{6,54},{7,55},{8,64},{9,65... | collective-permute-start | bytes 1990664 | tf_op jit(solution)/shard_map/ppermute | solution.py:128
  11.2 2.2 %polar.1 = (bf16[648,648]{1,0:T(8,128)(2,1)S(1)}, bf16[648,648]{1,0:T(8,128)(2,1)S(1)}, f32[8,128]{1,0:T(8,128)S(1)}) custom-call(f32[648]{0:T(1024)S(1)} %copy-done.1, bf16[648,10368]{1,0:T(8,128)(2,1)} %refs_1_.1, f32[8,128]{1,0:T(8,128)S(1)} %get-tuple-element.80.refs_2_), custom_call_target="tpu_custom_call" | custom-call | flops 1000 | bytes 1000 | tf_op jit(solution)/shard_map/polar/pallas_call | solution.py:77
  13.4 1.3 collective-permute-start
  14.7 4.7 %collective-permute-done.2.refs_0_ = bf16[648,512]{1,0:T(8,128)(2,1)S(1)} collective-permute-done((bf16[648,512]{1,0:T(8,128)(2,1)S(1)}, bf16[648,512]{1,0:T(8,128)(2,1)S(1)}, u32[]{:S(2)}, u32[]{:S(2)}) %collective-permute-start.2) | collective-permute-done | bytes 663584 | tf_op jit(solution)/shard_map/ppermute | solution.py:133
  19.4 1.5 collective-permute-start.5
  20.9 2.2 %collective-permute-done.3.refs_1_ = bf16[648,512]{1,0:T(8,128)(2,1)S(1)} collective-permute-done((bf16[648,512]{1,0:T(8,128)(2,1)S(1)}, bf16[648,512]{1,0:T(8,128)(2,1)S(1)}, u32[]{:S(2)}, u32[]{:S(2)}) %collective-permute-start.3) | collective-permute-done | bytes 663584 | tf_op jit(solution)/shard_map/ppermute | solution.py:131
  23.1 13.3 %collective-permute-done.4.refs_2_ = bf16[648,512]{1,0:T(8,128)(2,1)S(1)} collective-permute-done((bf16[648,512]{1,0:T(8,128)(2,1)S(1)}, bf16[648,512]{1,0:T(8,128)(2,1)S(1)}, u32[]{:S(2)}, u32[]{:S(2)}) %collective-permute-start.4) | collective-permute-done | bytes 663584 | tf_op jit(solution)/shard_map/ppermute | solution.py:132
  36.6 2.1 %collective-permute-start.8 = (bf16[648,512]{1,0:T(8,128)(2,1)S(1)}, bf16[648,512]{1,0:T(8,128)(2,1)S(1)}, u32[]{:S(2)}, u32[]{:S(2)}) collective-permute-start(bf16[648,512]{1,0:T(8,128)(2,1)S(1)} %get-tuple-element.89.refs_9_.refs_4_.refs_5_), channel_id=1, source_target_pairs={{0,1},{1,0},{2,3},{3,2},{4,5},{5,4},{6,7},{7,6},{8,9},{9,8},{10,11... | collective-permute-start | bytes 1990664 | tf_op jit(solution)/shard_map/ppermute | solution.py:353
  39.2 1.5 collective-permute-start.10
  40.7 1.8 %collective-permute-start.11 = (bf16[648,512]{1,0:T(8,128)(2,1)S(1)}, bf16[648,512]{1,0:T(8,128)(2,1)S(1)}, u32[]{:S(2)}, u32[]{:S(2)}) collective-permute-start(bf16[648,512]{1,0:T(8,128)(2,1)S(1)} %get-tuple-element.89.refs_9_.refs_4_.refs_5_), channel_id=1, source_target_pairs={{0,48},{16,0},{32,16},{48,32},{64,112},{80,64},{96,80},{112,96},{1... | collective-permute-start | bytes 1990664 | tf_op jit(solution)/shard_map/ppermute | solution.py:355
  42.5 4.4 %m0_product1.1 = (bf16[648,512]{1,0:T(8,128)(2,1)S(1)}, bf16[648,512]{1,0:T(8,128)(2,1)S(1)}, bf16[648,1024]{1,0:T(8,128)(2,1)S(1)}, f32[8,128]{1,0:T(8,128)S(1)}) custom-call(bf16[648,648]{1,0:T(8,128)(2,1)S(1)} %get-tuple-element.81.refs_0_, bf16[648,648]{1,0:T(8,128)(2,1)S(1)} %collective-permute-done.refs_1_, ...), custom_call_target="tpu_custom_call" | custom-call | flops 1000 | bytes 1000 | tf_op jit(solution)/shard_map/m0_product1/pallas_call | solution.py:77
  46.9 2.9 %collective-permute-start.9 = (bf16[648,1024]{1,0:T(8,128)(2,1)S(1)}, bf16[648,1024]{1,0:T(8,128)(2,1)S(1)}, u32[]{:S(2)}, u32[]{:S(2)}) collective-permute-start(bf16[648,1024]{1,0:T(8,128)(2,1)S(1)} %get-tuple-element.92), channel_id=1, source_target_pairs={{0,2},{1,7},{2,0},{3,5},{4,6},{5,3},{6,4},{7,1},{8,10},{9,15},{10,... | collective-permute-start | bytes 3981320 | tf_op jit(solution)/shard_map/ppermute | solution.py:315
  49.8 7.8 %collective-permute-done.10.refs_0_ = bf16[648,512]{1,0:T(8,128)(2,1)S(1)} collective-permute-done((bf16[648,512]{1,0:T(8,128)(2,1)S(1)}, bf16[648,512]{1,0:T(8,128)(2,1)S(1)}, u32[]{:S(2)}, u32[]{:S(2)}) %collective-permute-start.10) | collective-permute-done | bytes 663584 | tf_op jit(solution)/shard_map/ppermute | solution.py:354
  58.7 2.8 %collective-permute-start.15 = (bf16[648,512]{1,0:T(8,128)(2,1)S(1)}, bf16[648,512]{1,0:T(8,128)(2,1)S(1)}, u32[]{:S(2)}, u32[]{:S(2)}) collective-permute-start(bf16[648,512]{1,0:T(8,128)(2,1)S(1)} %get-tuple-element.100), channel_id=1, source_target_pairs={{0,16},{1,49},{2,18},{3,51},{4,20},{5,53},{6,22},{7,55},{8,24},{9,... | collective-permute-start | bytes 1990664 | tf_op jit(solution)/shard_map/ppermute | solution.py:356
  61.6 2.3 %m1_product1.1 = (bf16[648,256]{1,0:T(8,128)(2,1)S(1)}, bf16[648,256]{1,0:T(8,128)(2,1)S(1)}, bf16[648,512]{1,0:T(8,128)(2,1)S(1)}, f32[8,128]{1,0:T(8,128)S(1)}) custom-call(bf16[648,648]{1,0:T(8,128)(2,1)S(1)} %get-tuple-element.81.refs_0_, bf16[648,648]{1,0:T(8,128)(2,1)S(1)} %collective-permute-done.refs_1_, ...), custom_call_target="tpu_custom_call" | custom-call | flops 1000 | bytes 1000 | tf_op jit(solution)/shard_map/m1_product1/pallas_call | solution.py:77
  63.9 1.3 collective-permute-done.9.refs_1_
  65.5 3.6 %collective-permute-done.15.refs_0_ = bf16[648,512]{1,0:T(8,128)(2,1)S(1)} collective-permute-done((bf16[648,512]{1,0:T(8,128)(2,1)S(1)}, bf16[648,512]{1,0:T(8,128)(2,1)S(1)}, u32[]{:S(2)}, u32[]{:S(2)}) %collective-permute-start.15) | collective-permute-done | bytes 663584 | tf_op jit(solution)/shard_map/ppermute | solution.py:356
  69.0 7.1 %collective-permute-done.16.refs_1_ = bf16[648,512]{1,0:T(8,128)(2,1)S(1)} collective-permute-done((bf16[648,512]{1,0:T(8,128)(2,1)S(1)}, bf16[648,512]{1,0:T(8,128)(2,1)S(1)}, u32[]{:S(2)}, u32[]{:S(2)}) %collective-permute-start.16) | collective-permute-done | bytes 663584 | tf_op jit(solution)/shard_map/ppermute | solution.py:363
  76.2 1.9 %collective-permute-start.18 = (bf16[648,512]{1,0:T(8,128)(2,1)S(1)}, bf16[648,512]{1,0:T(8,128)(2,1)S(1)}, u32[]{:S(2)}, u32[]{:S(2)}) collective-permute-start(bf16[648,512]{1,0:T(8,128)(2,1)S(1)} %get-tuple-element.105.refs_3_.refs_9_.refs_2_), channel_id=1, source_target_pairs={{0,1},{1,0},{2,3},{3,2},{4,5},{5,4},{6,7},{7,6},{8,9},{9,8},{10,11... | collective-permute-start | bytes 1990664 | tf_op jit(solution)/shard_map/ppermute | solution.py:370
  78.1 2.5 %collective-permute-start.21 = (bf16[648,512]{1,0:T(8,128)(2,1)S(1)}, bf16[648,512]{1,0:T(8,128)(2,1)S(1)}, u32[]{:S(2)}, u32[]{:S(2)}) collective-permute-start(bf16[648,512]{1,0:T(8,128)(2,1)S(1)} %get-tuple-element.111), channel_id=1, source_target_pairs={{0,2},{1,7},{2,0},{3,5},{4,6},{5,3},{6,4},{7,1},{8,10},{9,15},{10,... | collective-permute-start | bytes 1990664 | tf_op jit(solution)/shard_map/ppermute | solution.py:315
  80.8 2.3 %m2_product1.1 = (bf16[648,256]{1,0:T(8,128)(2,1)S(1)}, bf16[648,256]{1,0:T(8,128)(2,1)S(1)}, bf16[648,512]{1,0:T(8,128)(2,1)S(1)}, f32[8,128]{1,0:T(8,128)S(1)}) custom-call(bf16[648,648]{1,0:T(8,128)(2,1)S(1)} %get-tuple-element.81.refs_0_, bf16[648,648]{1,0:T(8,128)(2,1)S(1)} %collective-permute-done.refs_1_, ...), custom_call_target="tpu_custom_call" | custom-call | flops 1000 | bytes 1000 | tf_op jit(solution)/shard_map/m2_product1/pallas_call | solution.py:77
  83.1 2.5 %collective-permute-start.20 = (bf16[648,512]{1,0:T(8,128)(2,1)S(1)}, bf16[648,512]{1,0:T(8,128)(2,1)S(1)}, u32[]{:S(2)}, u32[]{:S(2)}) collective-permute-start(bf16[648,512]{1,0:T(8,128)(2,1)S(1)} %get-tuple-element.109), channel_id=1, source_target_pairs={{0,2},{1,7},{2,0},{3,5},{4,6},{5,3},{6,4},{7,1},{8,10},{9,15},{10,... | collective-permute-start | bytes 1990664 | tf_op jit(solution)/shard_map/ppermute | solution.py:315
  86.0 2.8 %collective-permute-done.21.refs_1_ = bf16[648,512]{1,0:T(8,128)(2,1)S(1)} collective-permute-done((bf16[648,512]{1,0:T(8,128)(2,1)S(1)}, bf16[648,512]{1,0:T(8,128)(2,1)S(1)}, u32[]{:S(2)}, u32[]{:S(2)}) %collective-permute-start.21) | collective-permute-done | bytes 663584 | tf_op jit(solution)/shard_map/ppermute | solution.py:315
  89.0 9.8 %collective-permute-done.22.refs_2_ = bf16[648,256]{1,0:T(8,128)(2,1)S(1)} collective-permute-done((bf16[648,256]{1,0:T(8,128)(2,1)S(1)}, bf16[648,256]{1,0:T(8,128)(2,1)S(1)}, u32[]{:S(2)}, u32[]{:S(2)}) %collective-permute-start.22) | collective-permute-done | bytes 331808 | tf_op jit(solution)/shard_map/ppermute | solution.py:318
  99.1 2.7 %collective-permute-done.17.refs_1_ = bf16[648,512]{1,0:T(8,128)(2,1)S(1)} collective-permute-done((bf16[648,512]{1,0:T(8,128)(2,1)S(1)}, bf16[648,512]{1,0:T(8,128)(2,1)S(1)}, u32[]{:S(2)}, u32[]{:S(2)}) %collective-permute-start.17) | collective-permute-done | bytes 663584 | tf_op jit(solution)/shard_map/ppermute | solution.py:321
  102.6 1.3 collective-permute-start.27
  103.8 6.9 %collective-permute-done.24.refs_1_ = bf16[648,256]{1,0:T(8,128)(2,1)S(1)} collective-permute-done((bf16[648,256]{1,0:T(8,128)(2,1)S(1)}, bf16[648,256]{1,0:T(8,128)(2,1)S(1)}, u32[]{:S(2)}, u32[]{:S(2)}) %collective-permute-start.24) | collective-permute-done | bytes 331808 | tf_op jit(solution)/shard_map/ppermute | solution.py:321
  110.8 1.0 collective-permute-done.23.refs_1_
  112.0 3.3 %collective-permute-done.27.refs_2_ = bf16[648,256]{1,0:T(8,128)(2,1)S(1)} collective-permute-done((bf16[648,256]{1,0:T(8,128)(2,1)S(1)}, bf16[648,256]{1,0:T(8,128)(2,1)S(1)}, u32[]{:S(2)}, u32[]{:S(2)}) %collective-permute-start.27) | collective-permute-done | bytes 331808 | tf_op jit(solution)/shard_map/ppermute | solution.py:318
  116.2 5.6 %collective-permute-done.28.refs_1_ = bf16[648,256]{1,0:T(8,128)(2,1)S(1)} collective-permute-done((bf16[648,256]{1,0:T(8,128)(2,1)S(1)}, bf16[648,256]{1,0:T(8,128)(2,1)S(1)}, u32[]{:S(2)}, u32[]{:S(2)}) %collective-permute-start.28) | collective-permute-done | bytes 331808 | tf_op jit(solution)/shard_map/ppermute | solution.py:321
  121.9 1.3 collective-permute-start.29
  123.2 1.3 collective-permute-done.26.refs_0_
  124.5 1.3 collective-permute-done.25.refs_1_
  125.9 1.2 collective-permute-start.31
  127.1 4.6 %collective-permute-done.29.refs_1_ = bf16[648,256]{1,0:T(8,128)(2,1)S(1)} collective-permute-done((bf16[648,256]{1,0:T(8,128)(2,1)S(1)}, bf16[648,256]{1,0:T(8,128)(2,1)S(1)}, u32[]{:S(2)}, u32[]{:S(2)}) %collective-permute-start.29) | collective-permute-done | bytes 331808 | tf_op jit(solution)/shard_map/ppermute | solution.py:324
  132.7 2.3 %n2_product2.2 = (f32[648,648]{1,0:T(8,128)S(1)}, f32[8,128]{1,0:T(8,128)S(1)}) custom-call(bf16[648,1024]{1,0:T(8,128)(2,1)S(1)} %get-tuple-element.122.refs_0_, bf16[648,512]{1,0:T(8,128)(2,1)S(1)} %collective-permute-done.5.refs_4_.refs_1_.refs_2_, bf16[648,512]{1,0:T(8,128)(2,1)S(1)} %collective-permute-done.6.refs_6_.refs_2_.refs_3_, ...), custom_call_target="tpu_custom_call" | custom-call | flops 1000 | bytes 1000 | tf_op jit(solution)/shard_map/n2_product2/pallas_call | solution.py:77
  135.0 2.3 %n2_product2.3 = (f32[648,648]{1,0:T(8,128)S(1)}, f32[8,128]{1,0:T(8,128)S(1)}) custom-call(bf16[648,1024]{1,0:T(8,128)(2,1)S(1)} %get-tuple-element.122.refs_0_, bf16[648,512]{1,0:T(8,128)(2,1)S(1)} %get-tuple-element.83.refs_3_.refs_1_.refs_2_, bf16[648,512]{1,0:T(8,128)(2,1)S(1)} %get-tuple-element.87.refs_5_.refs_2_.refs_3_, ...), custom_call_target="tpu_custom_call" | custom-call | flops 1000 | bytes 1000 | tf_op jit(solution)/shard_map/n2_product2/pallas_call | solution.py:77
  137.3 2.9 %collective-permute-done.30.refs_1_ = bf16[648,512]{1,0:T(8,128)(2,1)S(1)} collective-permute-done((bf16[648,512]{1,0:T(8,128)(2,1)S(1)}, bf16[648,512]{1,0:T(8,128)(2,1)S(1)}, u32[]{:S(2)}, u32[]{:S(2)}) %collective-permute-start.30) | collective-permute-done | bytes 663584 | tf_op jit(solution)/shard_map/ppermute | solution.py:331
  142.0 1.2 t0_product2.2
  143.3 1.3 t0_product2.3
  144.6 2.7 %collective-permute-done.32.refs_1_ = bf16[648,512]{1,0:T(8,128)(2,1)S(1)} collective-permute-done((bf16[648,512]{1,0:T(8,128)(2,1)S(1)}, bf16[648,512]{1,0:T(8,128)(2,1)S(1)}, u32[]{:S(2)}, u32[]{:S(2)}) %collective-permute-start.32) | collective-permute-done | bytes 663584 | tf_op jit(solution)/shard_map/ppermute | solution.py:331
  148.0 1.8 %collective-permute-start.33 = (bf16[648,648]{1,0:T(8,128)(2,1)S(1)}, bf16[648,648]{1,0:T(8,128)(2,1)S(1)}, u32[]{:S(2)}, u32[]{:S(2)}) collective-permute-start(bf16[648,648]{1,0:T(8,128)(2,1)S(1)} %get-tuple-element.154), channel_id=1, source_target_pairs={{0,1},{1,0},{2,3},{3,2},{4,5},{5,4},{6,7},{7,6},{8,9},{9,8},{10,11... | collective-permute-start | bytes 2519432 | tf_op jit(solution)/shard_map/ppermute | solution.py:346
  150.0 1.2 t2_product2.3
  152.1 2.9 %finish.1 = f32[648,1296]{1,0:T(8,128)} custom-call(f32[648,1]{1,0:T(8,128)S(1)} %mul.11.refs_0_, f32[648,648]{1,0:T(8,128)S(1)} %get-tuple-element.153.refs_1_, bf16[648,648]{1,0:T(8,128)(2,1)S(1)} %collective-permute-done.33.refs_2_), custom_call_target="tpu_custom_call" | custom-call | tf_op jit(solution)/shard_map/finish/pallas_call | solution.py:385
  (60 shorter events, 10.8 us)
Async XLA Ops:
  0.0 1.1 copy-start
  1.2 18.2 %collective-permute-start.2 = (bf16[648,512]{1,0:T(8,128)(2,1)S(1)}, bf16[648,512]{1,0:T(8,128)(2,1)S(1)}, u32[]{:S(2)}, u32[]{:S(2)}) collective-permute-start(bf16[648,512]{1,0:T(8,128)(2,1)S(1)} %get-tuple-element.83.refs_3_.refs_1_.refs_2_), channel_id=1, source_target_pairs={{0,64},{16,80},{32,96},{48,112},{64,0},{80,16},{96,32},{112,48},{1... | collective-permute-start | bytes 1990664 | tf_op jit(solution)/shard_map/ppermute | solution.py:133
  5.0 18.1 %collective-permute-start.3 = (bf16[648,512]{1,0:T(8,128)(2,1)S(1)}, bf16[648,512]{1,0:T(8,128)(2,1)S(1)}, u32[]{:S(2)}, u32[]{:S(2)}) collective-permute-start(bf16[648,512]{1,0:T(8,128)(2,1)S(1)} %get-tuple-element.83.refs_3_.refs_1_.refs_2_), channel_id=1, source_target_pairs={{0,16},{16,32},{32,48},{48,0},{64,80},{80,96},{96,112},{112,64},{1... | collective-permute-start | bytes 1990664 | tf_op jit(solution)/shard_map/ppermute | solution.py:131
  6.7 29.7 %collective-permute-start.4 = (bf16[648,512]{1,0:T(8,128)(2,1)S(1)}, bf16[648,512]{1,0:T(8,128)(2,1)S(1)}, u32[]{:S(2)}, u32[]{:S(2)}) collective-permute-start(bf16[648,512]{1,0:T(8,128)(2,1)S(1)} %get-tuple-element.83.refs_3_.refs_1_.refs_2_), channel_id=1, source_target_pairs={{0,48},{16,0},{32,16},{48,32},{64,112},{80,64},{96,80},{112,96},{1... | collective-permute-start | bytes 1990664 | tf_op jit(solution)/shard_map/ppermute | solution.py:132
  8.8 30.0 %collective-permute-start.1 = (bf16[648,512]{1,0:T(8,128)(2,1)}, bf16[648,512]{1,0:T(8,128)(2,1)S(1)}, u32[]{:S(2)}, u32[]{:S(2)}) collective-permute-start(bf16[648,512]{1,0:T(8,128)(2,1)} %param.9), channel_id=1, source_target_pairs={{0,0},{1,1},{2,18},{3,19},{4,36},{5,37},{6,54},{7,55},{8,64},{9,65... | collective-permute-start | bytes 1990664 | tf_op jit(solution)/shard_map/ppermute | solution.py:128
  10.5 0.7 copy-start.1
  13.4 27.3 %collective-permute-start = (bf16[648,648]{1,0:T(8,128)(2,1)S(1)}, bf16[648,648]{1,0:T(8,128)(2,1)S(1)}, u32[]{:S(2)}, u32[]{:S(2)}) collective-permute-start(bf16[648,648]{1,0:T(8,128)(2,1)S(1)} %get-tuple-element.82), channel_id=1, source_target_pairs={{0,1},{1,0},{2,3},{3,2},{4,5},{5,4},{6,7},{7,6},{8,9},{9,8},{10,11... | collective-permute-start | bytes 2519432 | tf_op jit(solution)/shard_map/ppermute | solution.py:167
  19.4 19.8 %collective-permute-start.5 = (bf16[648,512]{1,0:T(8,128)(2,1)S(1)}, bf16[648,512]{1,0:T(8,128)(2,1)S(1)}, u32[]{:S(2)}, u32[]{:S(2)}) collective-permute-start(bf16[648,512]{1,0:T(8,128)(2,1)S(1)} %get-tuple-element.83.refs_3_.refs_1_.refs_2_), channel_id=1, source_target_pairs={{0,1},{1,0},{2,3},{3,2},{4,5},{5,4},{6,7},{7,6},{8,9},{9,8},{10,11... | collective-permute-start | bytes 1990664 | tf_op jit(solution)/shard_map/ppermute | solution.py:130
  36.6 5.9 %collective-permute-start.8 = (bf16[648,512]{1,0:T(8,128)(2,1)S(1)}, bf16[648,512]{1,0:T(8,128)(2,1)S(1)}, u32[]{:S(2)}, u32[]{:S(2)}) collective-permute-start(bf16[648,512]{1,0:T(8,128)(2,1)S(1)} %get-tuple-element.89.refs_9_.refs_4_.refs_5_), channel_id=1, source_target_pairs={{0,1},{1,0},{2,3},{3,2},{4,5},{5,4},{6,7},{7,6},{8,9},{9,8},{10,11... | collective-permute-start | bytes 1990664 | tf_op jit(solution)/shard_map/ppermute | solution.py:353
  38.7 3.8 %collective-permute-start.6 = (bf16[648,512]{1,0:T(8,128)(2,1)S(1)}, bf16[648,512]{1,0:T(8,128)(2,1)S(1)}, u32[]{:S(2)}, u32[]{:S(2)}) collective-permute-start(bf16[648,512]{1,0:T(8,128)(2,1)S(1)} %get-tuple-element.87.refs_5_.refs_2_.refs_3_), channel_id=1, source_target_pairs={{0,1},{1,0},{2,3},{3,2},{4,5},{5,4},{6,7},{7,6},{8,9},{9,8},{10,11... | collective-permute-start | bytes 1990664 | tf_op jit(solution)/shard_map/ppermute | solution.py:353
  38.8 3.7 %collective-permute-start.7 = (bf16[648,512]{1,0:T(8,128)(2,1)S(1)}, bf16[648,512]{1,0:T(8,128)(2,1)S(1)}, u32[]{:S(2)}, u32[]{:S(2)}) collective-permute-start(bf16[648,512]{1,0:T(8,128)(2,1)S(1)} %get-tuple-element.88.refs_7_.refs_3_.refs_4_), channel_id=1, source_target_pairs={{0,1},{1,0},{2,3},{3,2},{4,5},{5,4},{6,7},{7,6},{8,9},{9,8},{10,11... | collective-permute-start | bytes 1990664 | tf_op jit(solution)/shard_map/ppermute | solution.py:353
  39.2 18.4 %collective-permute-start.10 = (bf16[648,512]{1,0:T(8,128)(2,1)S(1)}, bf16[648,512]{1,0:T(8,128)(2,1)S(1)}, u32[]{:S(2)}, u32[]{:S(2)}) collective-permute-start(bf16[648,512]{1,0:T(8,128)(2,1)S(1)} %get-tuple-element.89.refs_9_.refs_4_.refs_5_), channel_id=1, source_target_pairs={{0,16},{16,32},{32,48},{48,0},{64,80},{80,96},{96,112},{112,64},{1... | collective-permute-start | bytes 1990664 | tf_op jit(solution)/shard_map/ppermute | solution.py:354
  40.7 16.9 %collective-permute-start.11 = (bf16[648,512]{1,0:T(8,128)(2,1)S(1)}, bf16[648,512]{1,0:T(8,128)(2,1)S(1)}, u32[]{:S(2)}, u32[]{:S(2)}) collective-permute-start(bf16[648,512]{1,0:T(8,128)(2,1)S(1)} %get-tuple-element.89.refs_9_.refs_4_.refs_5_), channel_id=1, source_target_pairs={{0,48},{16,0},{32,16},{48,32},{64,112},{80,64},{96,80},{112,96},{1... | collective-permute-start | bytes 1990664 | tf_op jit(solution)/shard_map/ppermute | solution.py:355
  46.9 18.4 %collective-permute-start.9 = (bf16[648,1024]{1,0:T(8,128)(2,1)S(1)}, bf16[648,1024]{1,0:T(8,128)(2,1)S(1)}, u32[]{:S(2)}, u32[]{:S(2)}) collective-permute-start(bf16[648,1024]{1,0:T(8,128)(2,1)S(1)} %get-tuple-element.92), channel_id=1, source_target_pairs={{0,2},{1,7},{2,0},{3,5},{4,6},{5,3},{6,4},{7,1},{8,10},{9,15},{10,... | collective-permute-start | bytes 3981320 | tf_op jit(solution)/shard_map/ppermute | solution.py:315
  57.8 3.8 %collective-permute-start.12 = (bf16[648,512]{1,0:T(8,128)(2,1)S(1)}, bf16[648,512]{1,0:T(8,128)(2,1)S(1)}, u32[]{:S(2)}, u32[]{:S(2)}) collective-permute-start(bf16[648,512]{1,0:T(8,128)(2,1)S(1)} %get-tuple-element.95.refs_3_.refs_6_.refs_2_), channel_id=1, source_target_pairs={{0,1},{1,0},{2,3},{3,2},{4,5},{5,4},{6,7},{7,6},{8,9},{9,8},{10,11... | collective-permute-start | bytes 1990664 | tf_op jit(solution)/shard_map/ppermute | solution.py:362
  58.6 3.0 %collective-permute-start.13 = (bf16[648,512]{1,0:T(8,128)(2,1)S(1)}, bf16[648,512]{1,0:T(8,128)(2,1)S(1)}, u32[]{:S(2)}, u32[]{:S(2)}) collective-permute-start(bf16[648,512]{1,0:T(8,128)(2,1)S(1)} %get-tuple-element.96.refs_5_.refs_7_.refs_3_), channel_id=1, source_target_pairs={{0,1},{1,0},{2,3},{3,2},{4,5},{5,4},{6,7},{7,6},{8,9},{9,8},{10,11... | collective-permute-start | bytes 1990664 | tf_op jit(solution)/shard_map/ppermute | solution.py:362
  58.7 10.4 %collective-permute-start.15 = (bf16[648,512]{1,0:T(8,128)(2,1)S(1)}, bf16[648,512]{1,0:T(8,128)(2,1)S(1)}, u32[]{:S(2)}, u32[]{:S(2)}) collective-permute-start(bf16[648,512]{1,0:T(8,128)(2,1)S(1)} %get-tuple-element.100), channel_id=1, source_target_pairs={{0,16},{1,49},{2,18},{3,51},{4,20},{5,53},{6,22},{7,55},{8,24},{9,... | collective-permute-start | bytes 1990664 | tf_op jit(solution)/shard_map/ppermute | solution.py:356
  61.4 14.7 %collective-permute-start.16 = (bf16[648,512]{1,0:T(8,128)(2,1)S(1)}, bf16[648,512]{1,0:T(8,128)(2,1)S(1)}, u32[]{:S(2)}, u32[]{:S(2)}) collective-permute-start(bf16[648,512]{1,0:T(8,128)(2,1)S(1)} %get-tuple-element.101), channel_id=1, source_target_pairs={{0,16},{1,49},{2,18},{3,51},{4,20},{5,53},{6,22},{7,55},{8,24},{9,... | collective-permute-start | bytes 1990664 | tf_op jit(solution)/shard_map/ppermute | solution.py:363
  65.4 15.2 %collective-permute-start.14 = (bf16[648,512]{1,0:T(8,128)(2,1)S(1)}, bf16[648,512]{1,0:T(8,128)(2,1)S(1)}, u32[]{:S(2)}, u32[]{:S(2)}) collective-permute-start(bf16[648,512]{1,0:T(8,128)(2,1)S(1)} %get-tuple-element.99), channel_id=1, source_target_pairs={{0,6},{1,3},{2,4},{3,1},{4,2},{5,7},{6,0},{7,5},{8,14},{9,11},{10,... | collective-permute-start | bytes 1990664 | tf_op jit(solution)/shard_map/ppermute | solution.py:318
  76.2 4.7 %collective-permute-start.18 = (bf16[648,512]{1,0:T(8,128)(2,1)S(1)}, bf16[648,512]{1,0:T(8,128)(2,1)S(1)}, u32[]{:S(2)}, u32[]{:S(2)}) collective-permute-start(bf16[648,512]{1,0:T(8,128)(2,1)S(1)} %get-tuple-element.105.refs_3_.refs_9_.refs_2_), channel_id=1, source_target_pairs={{0,1},{1,0},{2,3},{3,2},{4,5},{5,4},{6,7},{7,6},{8,9},{9,8},{10,11... | collective-permute-start | bytes 1990664 | tf_op jit(solution)/shard_map/ppermute | solution.py:370
  78.1 2.8 %collective-permute-start.19 = (bf16[648,512]{1,0:T(8,128)(2,1)S(1)}, bf16[648,512]{1,0:T(8,128)(2,1)S(1)}, u32[]{:S(2)}, u32[]{:S(2)}) collective-permute-start(bf16[648,512]{1,0:T(8,128)(2,1)S(1)} %get-tuple-element.106.refs_5_.refs_10_.refs_3_), channel_id=1, source_target_pairs={{0,1},{1,0},{2,3},{3,2},{4,5},{5,4},{6,7},{7,6},{8,9},{9,8},{10,11... | collective-permute-start | bytes 1990664 | tf_op jit(solution)/shard_map/ppermute | solution.py:370
  78.1 10.7 %collective-permute-start.21 = (bf16[648,512]{1,0:T(8,128)(2,1)S(1)}, bf16[648,512]{1,0:T(8,128)(2,1)S(1)}, u32[]{:S(2)}, u32[]{:S(2)}) collective-permute-start(bf16[648,512]{1,0:T(8,128)(2,1)S(1)} %get-tuple-element.111), channel_id=1, source_target_pairs={{0,2},{1,7},{2,0},{3,5},{4,6},{5,3},{6,4},{7,1},{8,10},{9,15},{10,... | collective-permute-start | bytes 1990664 | tf_op jit(solution)/shard_map/ppermute | solution.py:315
  83.1 15.9 %collective-permute-start.20 = (bf16[648,512]{1,0:T(8,128)(2,1)S(1)}, bf16[648,512]{1,0:T(8,128)(2,1)S(1)}, u32[]{:S(2)}, u32[]{:S(2)}) collective-permute-start(bf16[648,512]{1,0:T(8,128)(2,1)S(1)} %get-tuple-element.109), channel_id=1, source_target_pairs={{0,2},{1,7},{2,0},{3,5},{4,6},{5,3},{6,4},{7,1},{8,10},{9,15},{10,... | collective-permute-start | bytes 1990664 | tf_op jit(solution)/shard_map/ppermute | solution.py:315
  85.6 16.1 %collective-permute-start.17 = (bf16[648,512]{1,0:T(8,128)(2,1)S(1)}, bf16[648,512]{1,0:T(8,128)(2,1)S(1)}, u32[]{:S(2)}, u32[]{:S(2)}) collective-permute-start(bf16[648,512]{1,0:T(8,128)(2,1)S(1)} %get-tuple-element.104.refs_0_), channel_id=1, source_target_pairs={{0,8},{1,9},{2,10},{3,11},{4,12},{5,13},{6,14},{7,15},{8,0},{9,1},... | collective-permute-start | bytes 1990664 | tf_op jit(solution)/shard_map/ppermute | solution.py:321
  88.9 10.0 %collective-permute-start.22 = (bf16[648,256]{1,0:T(8,128)(2,1)S(1)}, bf16[648,256]{1,0:T(8,128)(2,1)S(1)}, u32[]{:S(2)}, u32[]{:S(2)}) collective-permute-start(bf16[648,256]{1,0:T(8,128)(2,1)S(1)} %get-tuple-element.114), channel_id=1, source_target_pairs={{0,6},{1,3},{2,4},{3,1},{4,2},{5,7},{6,0},{7,5},{8,14},{9,11},{10,... | collective-permute-start | bytes 995336 | tf_op jit(solution)/shard_map/ppermute | solution.py:318
  101.9 9.9 %collective-permute-start.23 = (bf16[648,512]{1,0:T(8,128)(2,1)S(1)}, bf16[648,512]{1,0:T(8,128)(2,1)S(1)}, u32[]{:S(2)}, u32[]{:S(2)}) collective-permute-start(bf16[648,512]{1,0:T(8,128)(2,1)S(1)} %get-tuple-element.118.refs_0_), channel_id=1, source_target_pairs={{0,6},{1,3},{2,4},{3,1},{4,2},{5,7},{6,0},{7,5},{8,14},{9,11},{10,... | collective-permute-start | bytes 1990664 | tf_op jit(solution)/shard_map/ppermute | solution.py:324
  102.6 8.2 %collective-permute-start.24 = (bf16[648,256]{1,0:T(8,128)(2,1)S(1)}, bf16[648,256]{1,0:T(8,128)(2,1)S(1)}, u32[]{:S(2)}, u32[]{:S(2)}) collective-permute-start(bf16[648,256]{1,0:T(8,128)(2,1)S(1)} %get-tuple-element.119.refs_0_), channel_id=1, source_target_pairs={{0,8},{1,9},{2,10},{3,11},{4,12},{5,13},{6,14},{7,15},{8,0},{9,1},... | collective-permute-start | bytes 995336 | tf_op jit(solution)/shard_map/ppermute | solution.py:321
  102.6 12.8 %collective-permute-start.27 = (bf16[648,256]{1,0:T(8,128)(2,1)S(1)}, bf16[648,256]{1,0:T(8,128)(2,1)S(1)}, u32[]{:S(2)}, u32[]{:S(2)}) collective-permute-start(bf16[648,256]{1,0:T(8,128)(2,1)S(1)} %get-tuple-element.126), channel_id=1, source_target_pairs={{0,6},{1,3},{2,4},{3,1},{4,2},{5,7},{6,0},{7,5},{8,14},{9,11},{10,... | collective-permute-start | bytes 995336 | tf_op jit(solution)/shard_map/ppermute | solution.py:318
  111.9 12.5 %collective-permute-start.26 = (bf16[648,512]{1,0:T(8,128)(2,1)S(1)}, bf16[648,512]{1,0:T(8,128)(2,1)S(1)}, u32[]{:S(2)}, u32[]{:S(2)}) collective-permute-start(bf16[648,512]{1,0:T(8,128)(2,1)S(1)} %get-tuple-element.124), channel_id=1, source_target_pairs={{0,2},{1,7},{2,0},{3,5},{4,6},{5,3},{6,4},{7,1},{8,10},{9,15},{10,... | collective-permute-start | bytes 1990664 | tf_op jit(solution)/shard_map/ppermute | solution.py:328
  115.5 6.3 %collective-permute-start.28 = (bf16[648,256]{1,0:T(8,128)(2,1)S(1)}, bf16[648,256]{1,0:T(8,128)(2,1)S(1)}, u32[]{:S(2)}, u32[]{:S(2)}) collective-permute-start(bf16[648,256]{1,0:T(8,128)(2,1)S(1)} %get-tuple-element.128.refs_0_), channel_id=1, source_target_pairs={{0,8},{1,9},{2,10},{3,11},{4,12},{5,13},{6,14},{7,15},{8,0},{9,1},... | collective-permute-start | bytes 995336 | tf_op jit(solution)/shard_map/ppermute | solution.py:321
  115.9 9.8 %collective-permute-start.25 = (bf16[648,256]{1,0:T(8,128)(2,1)S(1)}, bf16[648,256]{1,0:T(8,128)(2,1)S(1)}, u32[]{:S(2)}, u32[]{:S(2)}) collective-permute-start(bf16[648,256]{1,0:T(8,128)(2,1)S(1)} %get-tuple-element.123.refs_0_), channel_id=1, source_target_pairs={{0,6},{1,3},{2,4},{3,1},{4,2},{5,7},{6,0},{7,5},{8,14},{9,11},{10,... | collective-permute-start | bytes 995336 | tf_op jit(solution)/shard_map/ppermute | solution.py:324
  121.9 9.8 %collective-permute-start.29 = (bf16[648,256]{1,0:T(8,128)(2,1)S(1)}, bf16[648,256]{1,0:T(8,128)(2,1)S(1)}, u32[]{:S(2)}, u32[]{:S(2)}) collective-permute-start(bf16[648,256]{1,0:T(8,128)(2,1)S(1)} %get-tuple-element.133.refs_0_), channel_id=1, source_target_pairs={{0,6},{1,3},{2,4},{3,1},{4,2},{5,7},{6,0},{7,5},{8,14},{9,11},{10,... | collective-permute-start | bytes 995336 | tf_op jit(solution)/shard_map/ppermute | solution.py:324
  125.8 14.4 %collective-permute-start.30 = (bf16[648,512]{1,0:T(8,128)(2,1)S(1)}, bf16[648,512]{1,0:T(8,128)(2,1)S(1)}, u32[]{:S(2)}, u32[]{:S(2)}) collective-permute-start(bf16[648,512]{1,0:T(8,128)(2,1)S(1)} %get-tuple-element.132.refs_5_), channel_id=1, source_target_pairs={{0,2},{1,7},{2,0},{3,5},{4,6},{5,3},{6,4},{7,1},{8,10},{9,15},{10,... | collective-permute-start | bytes 1990664 | tf_op jit(solution)/shard_map/ppermute | solution.py:331
  125.9 15.7 %collective-permute-start.31 = (bf16[648,512]{1,0:T(8,128)(2,1)S(1)}, bf16[648,512]{1,0:T(8,128)(2,1)S(1)}, u32[]{:S(2)}, u32[]{:S(2)}) collective-permute-start(bf16[648,512]{1,0:T(8,128)(2,1)S(1)} %get-tuple-element.143.refs_0_), channel_id=1, source_target_pairs={{0,8},{1,9},{2,10},{3,11},{4,12},{5,13},{6,14},{7,15},{8,0},{9,1},... | collective-permute-start | bytes 1990664 | tf_op jit(solution)/shard_map/ppermute | solution.py:334
  131.8 15.5 %collective-permute-start.32 = (bf16[648,512]{1,0:T(8,128)(2,1)S(1)}, bf16[648,512]{1,0:T(8,128)(2,1)S(1)}, u32[]{:S(2)}, u32[]{:S(2)}) collective-permute-start(bf16[648,512]{1,0:T(8,128)(2,1)S(1)} %get-tuple-element.135.refs_8_), channel_id=1, source_target_pairs={{0,2},{1,7},{2,0},{3,5},{4,6},{5,3},{6,4},{7,1},{8,10},{9,15},{10,... | collective-permute-start | bytes 1990664 | tf_op jit(solution)/shard_map/ppermute | solution.py:331
  147.3 2.6 %copy-start.2 = (f32[648]{0:T(1024)S(1)}, f32[648]{0:T(1024)}, u32[]{:S(2)}) copy-start(f32[648]{0:T(1024)} %param.7) | copy-start | bytes 7780
  148.0 4.1 %collective-permute-start.33 = (bf16[648,648]{1,0:T(8,128)(2,1)S(1)}, bf16[648,648]{1,0:T(8,128)(2,1)S(1)}, u32[]{:S(2)}, u32[]{:S(2)}) collective-permute-start(bf16[648,648]{1,0:T(8,128)(2,1)S(1)} %get-tuple-element.154), channel_id=1, source_target_pairs={{0,1},{1,0},{2,3},{3,2},{4,5},{5,4},{6,7},{7,6},{8,9},{9,8},{10,11... | collective-permute-start | bytes 2519432 | tf_op jit(solution)/shard_map/ppermute | solution.py:346

commit v7 on v6

--- a/solution.py
+++ b/solution.py
@@ -16,7 +16,7 @@
 FINISH = 3
 STEPS = (
     "G0", "G3", "M0", "G1", "M1", "S0", "G2", "Y0", "M2",
-    "S1", "Y1", "S2", "R0", "R1", "F0", "Y2", "R2", "W0",
+    "S1", "Y1", "S2", "R0", "R1", "F0", "Y2", "W0", "R2",
     "F1", "F2", "N2", "T1", "T0", "T2",
 )
 

time: 155 us -> 158 us (1.019)
  starting transfers between devices: 40.4 us -> 42.7 us
    ppermute x1, waiting for transfers between devices: 1.27 us -> 8.23 us  [on_device(): share[c] = lax.ppermute(chosen, 'mode', FIRST)]
    ppermute x3, waiting for transfers between devices: 15.1 us -> 9.54 us  [on_device(): got3[c] = lax.ppermute(part3[c], 'mode', YSWAP)]
    ppermute x1, starting transfers between devices: 1.85 us -> 4.1 us  [on_device(): back = lax.ppermute(oth_sum, 'mode', KSWAP)]
    ppermute x3, waiting for transfers between devices: 6.9 us -> 5.3 us  [on_device(): r1[c] = lax.ppermute(r0[c], 'mode', SECOND)]
  transfers between devices with their start and end apart: 34 -> 34, of which waited for: 20 -> 18; matrix products, arithmetic and copies ran while one was open for 0% -> 0% of each run, Pallas kernels for 15% -> 14%
where the time goes in v7:
time: 158 us
  waiting for transfers between devices  86.2 us (55%)
  starting transfers between devices  42.7 us (27%)
  Pallas kernels  26.8 us (17%)
  local copies, waits for them, and re-layouts  1.92 us (1%)
    pallas_call x31, Pallas kernels, __call__(): pl.pallas_call(kernel, out_shape=list(outs) + [TOKEN], in_specs=list(spec...  23.9 us
    ppermute x1, waiting for transfers between devices, on_device(): unit[0, 1] = lax.ppermute(unit[0, 0], 'cfg', cfg_perm(0, -1))  13.3 us
    ppermute x3, waiting for transfers between devices, on_device(): got2[c] = lax.ppermute(v, 'mode', SECOND)  13.1 us
    ppermute x3, waiting for transfers between devices, on_device(): got3[c] = lax.ppermute(part3[c], 'mode', YSWAP)  9.54 us
    ppermute x1, waiting for transfers between devices, on_device(): share[c] = lax.ppermute(chosen, 'mode', FIRST)  8.23 us
    ppermute x3, starting transfers between devices, on_device(): products[c].append((*got, lax.ppermute(got[2], 'mode', FIRST)))  7.87 us
    ppermute x1, waiting for transfers between devices, on_device(): unit[1, 3] = lax.ppermute(unit[1, 0], 'cfg', cfg_perm(0, 1))  7.81 us
    ppermute x1, waiting for transfers between devices, on_device(): unit[1, 2] = lax.ppermute(pick, ('cfg', 'mode'), ONWARD)  7.11 us
  transfers between devices with their start and end apart: 34, of which 18 were waited for; matrix products, arithmetic and copies ran while one was open for 0% of the time, Pallas kernels for 14%

profile of v7, /device:TPU:1, one launch (start us, length us, event | category | flops | bytes accessed | tf_op | source)
XLA Modules:
  0.0 157.9 jit_solution(14012687389990695561)
XLA Ops:
  0.0 1.1 copy-done
  1.2 3.8 %collective-permute-start.2 = (bf16[648,512]{1,0:T(8,128)(2,1)S(1)}, bf16[648,512]{1,0:T(8,128)(2,1)S(1)}, u32[]{:S(2)}, u32[]{:S(2)}) collective-permute-start(bf16[648,512]{1,0:T(8,128)(2,1)S(1)} %get-tuple-element.83.refs_3_.refs_1_.refs_2_), channel_id=1, source_target_pairs={{0,64},{16,80},{32,96},{48,112},{64,0},{80,16},{96,32},{112,48},{1... | collective-permute-start | bytes 1990664 | tf_op jit(solution)/shard_map/ppermute | solution.py:133
  5.0 1.6 %collective-permute-start.3 = (bf16[648,512]{1,0:T(8,128)(2,1)S(1)}, bf16[648,512]{1,0:T(8,128)(2,1)S(1)}, u32[]{:S(2)}, u32[]{:S(2)}) collective-permute-start(bf16[648,512]{1,0:T(8,128)(2,1)S(1)} %get-tuple-element.83.refs_3_.refs_1_.refs_2_), channel_id=1, source_target_pairs={{0,16},{16,32},{32,48},{48,0},{64,80},{80,96},{96,112},{112,64},{1... | collective-permute-start | bytes 1990664 | tf_op jit(solution)/shard_map/ppermute | solution.py:131
  6.7 2.1 %collective-permute-start.4 = (bf16[648,512]{1,0:T(8,128)(2,1)S(1)}, bf16[648,512]{1,0:T(8,128)(2,1)S(1)}, u32[]{:S(2)}, u32[]{:S(2)}) collective-permute-start(bf16[648,512]{1,0:T(8,128)(2,1)S(1)} %get-tuple-element.83.refs_3_.refs_1_.refs_2_), channel_id=1, source_target_pairs={{0,48},{16,0},{32,16},{48,32},{64,112},{80,64},{96,80},{112,96},{1... | collective-permute-start | bytes 1990664 | tf_op jit(solution)/shard_map/ppermute | solution.py:132
  8.8 1.7 %collective-permute-start.1 = (bf16[648,512]{1,0:T(8,128)(2,1)}, bf16[648,512]{1,0:T(8,128)(2,1)S(1)}, u32[]{:S(2)}, u32[]{:S(2)}) collective-permute-start(bf16[648,512]{1,0:T(8,128)(2,1)} %param.9), channel_id=1, source_target_pairs={{0,0},{1,1},{2,18},{3,19},{4,36},{5,37},{6,54},{7,55},{8,64},{9,65... | collective-permute-start | bytes 1990664 | tf_op jit(solution)/shard_map/ppermute | solution.py:128
  11.2 2.2 %polar.1 = (bf16[648,648]{1,0:T(8,128)(2,1)S(1)}, bf16[648,648]{1,0:T(8,128)(2,1)S(1)}, f32[8,128]{1,0:T(8,128)S(1)}) custom-call(f32[648]{0:T(1024)S(1)} %copy-done.1, bf16[648,10368]{1,0:T(8,128)(2,1)} %refs_1_.1, f32[8,128]{1,0:T(8,128)S(1)} %get-tuple-element.80.refs_2_), custom_call_target="tpu_custom_call" | custom-call | flops 1000 | bytes 1000 | tf_op jit(solution)/shard_map/polar/pallas_call | solution.py:77
  13.4 1.3 collective-permute-start
  14.7 4.7 %collective-permute-done.2.refs_0_ = bf16[648,512]{1,0:T(8,128)(2,1)S(1)} collective-permute-done((bf16[648,512]{1,0:T(8,128)(2,1)S(1)}, bf16[648,512]{1,0:T(8,128)(2,1)S(1)}, u32[]{:S(2)}, u32[]{:S(2)}) %collective-permute-start.2) | collective-permute-done | bytes 663584 | tf_op jit(solution)/shard_map/ppermute | solution.py:133
  19.4 1.5 collective-permute-start.5
  20.9 2.2 %collective-permute-done.3.refs_1_ = bf16[648,512]{1,0:T(8,128)(2,1)S(1)} collective-permute-done((bf16[648,512]{1,0:T(8,128)(2,1)S(1)}, bf16[648,512]{1,0:T(8,128)(2,1)S(1)}, u32[]{:S(2)}, u32[]{:S(2)}) %collective-permute-start.3) | collective-permute-done | bytes 663584 | tf_op jit(solution)/shard_map/ppermute | solution.py:131
  23.1 13.3 %collective-permute-done.4.refs_2_ = bf16[648,512]{1,0:T(8,128)(2,1)S(1)} collective-permute-done((bf16[648,512]{1,0:T(8,128)(2,1)S(1)}, bf16[648,512]{1,0:T(8,128)(2,1)S(1)}, u32[]{:S(2)}, u32[]{:S(2)}) %collective-permute-start.4) | collective-permute-done | bytes 663584 | tf_op jit(solution)/shard_map/ppermute | solution.py:132
  36.6 2.1 %collective-permute-start.8 = (bf16[648,512]{1,0:T(8,128)(2,1)S(1)}, bf16[648,512]{1,0:T(8,128)(2,1)S(1)}, u32[]{:S(2)}, u32[]{:S(2)}) collective-permute-start(bf16[648,512]{1,0:T(8,128)(2,1)S(1)} %get-tuple-element.89.refs_9_.refs_4_.refs_5_), channel_id=1, source_target_pairs={{0,1},{1,0},{2,3},{3,2},{4,5},{5,4},{6,7},{7,6},{8,9},{9,8},{10,11... | collective-permute-start | bytes 1990664 | tf_op jit(solution)/shard_map/ppermute | solution.py:353
  39.2 1.5 collective-permute-start.10
  40.7 1.8 %collective-permute-start.11 = (bf16[648,512]{1,0:T(8,128)(2,1)S(1)}, bf16[648,512]{1,0:T(8,128)(2,1)S(1)}, u32[]{:S(2)}, u32[]{:S(2)}) collective-permute-start(bf16[648,512]{1,0:T(8,128)(2,1)S(1)} %get-tuple-element.89.refs_9_.refs_4_.refs_5_), channel_id=1, source_target_pairs={{0,48},{16,0},{32,16},{48,32},{64,112},{80,64},{96,80},{112,96},{1... | collective-permute-start | bytes 1990664 | tf_op jit(solution)/shard_map/ppermute | solution.py:355
  42.5 4.4 %m0_product1.1 = (bf16[648,512]{1,0:T(8,128)(2,1)S(1)}, bf16[648,512]{1,0:T(8,128)(2,1)S(1)}, bf16[648,1024]{1,0:T(8,128)(2,1)S(1)}, f32[8,128]{1,0:T(8,128)S(1)}) custom-call(bf16[648,648]{1,0:T(8,128)(2,1)S(1)} %get-tuple-element.81.refs_0_, bf16[648,648]{1,0:T(8,128)(2,1)S(1)} %collective-permute-done.refs_1_, ...), custom_call_target="tpu_custom_call" | custom-call | flops 1000 | bytes 1000 | tf_op jit(solution)/shard_map/m0_product1/pallas_call | solution.py:77
  46.9 2.9 %collective-permute-start.9 = (bf16[648,1024]{1,0:T(8,128)(2,1)S(1)}, bf16[648,1024]{1,0:T(8,128)(2,1)S(1)}, u32[]{:S(2)}, u32[]{:S(2)}) collective-permute-start(bf16[648,1024]{1,0:T(8,128)(2,1)S(1)} %get-tuple-element.92), channel_id=1, source_target_pairs={{0,2},{1,7},{2,0},{3,5},{4,6},{5,3},{6,4},{7,1},{8,10},{9,15},{10,... | collective-permute-start | bytes 3981320 | tf_op jit(solution)/shard_map/ppermute | solution.py:315
  49.8 7.8 %collective-permute-done.10.refs_0_ = bf16[648,512]{1,0:T(8,128)(2,1)S(1)} collective-permute-done((bf16[648,512]{1,0:T(8,128)(2,1)S(1)}, bf16[648,512]{1,0:T(8,128)(2,1)S(1)}, u32[]{:S(2)}, u32[]{:S(2)}) %collective-permute-start.10) | collective-permute-done | bytes 663584 | tf_op jit(solution)/shard_map/ppermute | solution.py:354
  57.8 0.8 collective-permute-start.12
  58.7 2.8 %collective-permute-start.15 = (bf16[648,512]{1,0:T(8,128)(2,1)S(1)}, bf16[648,512]{1,0:T(8,128)(2,1)S(1)}, u32[]{:S(2)}, u32[]{:S(2)}) collective-permute-start(bf16[648,512]{1,0:T(8,128)(2,1)S(1)} %get-tuple-element.100), channel_id=1, source_target_pairs={{0,16},{1,49},{2,18},{3,51},{4,20},{5,53},{6,22},{7,55},{8,24},{9,... | collective-permute-start | bytes 1990664 | tf_op jit(solution)/shard_map/ppermute | solution.py:356
  61.6 2.3 %m1_product1.1 = (bf16[648,256]{1,0:T(8,128)(2,1)S(1)}, bf16[648,256]{1,0:T(8,128)(2,1)S(1)}, bf16[648,512]{1,0:T(8,128)(2,1)S(1)}, f32[8,128]{1,0:T(8,128)S(1)}) custom-call(bf16[648,648]{1,0:T(8,128)(2,1)S(1)} %get-tuple-element.81.refs_0_, bf16[648,648]{1,0:T(8,128)(2,1)S(1)} %collective-permute-done.refs_1_, ...), custom_call_target="tpu_custom_call" | custom-call | flops 1000 | bytes 1000 | tf_op jit(solution)/shard_map/m1_product1/pallas_call | solution.py:77
  63.9 1.3 collective-permute-done.9.refs_1_
  65.5 3.6 %collective-permute-done.15.refs_0_ = bf16[648,512]{1,0:T(8,128)(2,1)S(1)} collective-permute-done((bf16[648,512]{1,0:T(8,128)(2,1)S(1)}, bf16[648,512]{1,0:T(8,128)(2,1)S(1)}, u32[]{:S(2)}, u32[]{:S(2)}) %collective-permute-start.15) | collective-permute-done | bytes 663584 | tf_op jit(solution)/shard_map/ppermute | solution.py:356
  69.0 7.1 %collective-permute-done.16.refs_1_ = bf16[648,512]{1,0:T(8,128)(2,1)S(1)} collective-permute-done((bf16[648,512]{1,0:T(8,128)(2,1)S(1)}, bf16[648,512]{1,0:T(8,128)(2,1)S(1)}, u32[]{:S(2)}, u32[]{:S(2)}) %collective-permute-start.16) | collective-permute-done | bytes 663584 | tf_op jit(solution)/shard_map/ppermute | solution.py:363
  76.2 1.9 %collective-permute-start.18 = (bf16[648,512]{1,0:T(8,128)(2,1)S(1)}, bf16[648,512]{1,0:T(8,128)(2,1)S(1)}, u32[]{:S(2)}, u32[]{:S(2)}) collective-permute-start(bf16[648,512]{1,0:T(8,128)(2,1)S(1)} %get-tuple-element.105.refs_3_.refs_9_.refs_2_), channel_id=1, source_target_pairs={{0,1},{1,0},{2,3},{3,2},{4,5},{5,4},{6,7},{7,6},{8,9},{9,8},{10,11... | collective-permute-start | bytes 1990664 | tf_op jit(solution)/shard_map/ppermute | solution.py:370
  78.1 2.5 %collective-permute-start.21 = (bf16[648,512]{1,0:T(8,128)(2,1)S(1)}, bf16[648,512]{1,0:T(8,128)(2,1)S(1)}, u32[]{:S(2)}, u32[]{:S(2)}) collective-permute-start(bf16[648,512]{1,0:T(8,128)(2,1)S(1)} %get-tuple-element.111), channel_id=1, source_target_pairs={{0,2},{1,7},{2,0},{3,5},{4,6},{5,3},{6,4},{7,1},{8,10},{9,15},{10,... | collective-permute-start | bytes 1990664 | tf_op jit(solution)/shard_map/ppermute | solution.py:315
  80.8 2.3 %m2_product1.1 = (bf16[648,256]{1,0:T(8,128)(2,1)S(1)}, bf16[648,256]{1,0:T(8,128)(2,1)S(1)}, bf16[648,512]{1,0:T(8,128)(2,1)S(1)}, f32[8,128]{1,0:T(8,128)S(1)}) custom-call(bf16[648,648]{1,0:T(8,128)(2,1)S(1)} %get-tuple-element.81.refs_0_, bf16[648,648]{1,0:T(8,128)(2,1)S(1)} %collective-permute-done.refs_1_, ...), custom_call_target="tpu_custom_call" | custom-call | flops 1000 | bytes 1000 | tf_op jit(solution)/shard_map/m2_product1/pallas_call | solution.py:77
  83.1 2.5 %collective-permute-start.20 = (bf16[648,512]{1,0:T(8,128)(2,1)S(1)}, bf16[648,512]{1,0:T(8,128)(2,1)S(1)}, u32[]{:S(2)}, u32[]{:S(2)}) collective-permute-start(bf16[648,512]{1,0:T(8,128)(2,1)S(1)} %get-tuple-element.109), channel_id=1, source_target_pairs={{0,2},{1,7},{2,0},{3,5},{4,6},{5,3},{6,4},{7,1},{8,10},{9,15},{10,... | collective-permute-start | bytes 1990664 | tf_op jit(solution)/shard_map/ppermute | solution.py:315
  86.0 2.8 %collective-permute-done.21.refs_1_ = bf16[648,512]{1,0:T(8,128)(2,1)S(1)} collective-permute-done((bf16[648,512]{1,0:T(8,128)(2,1)S(1)}, bf16[648,512]{1,0:T(8,128)(2,1)S(1)}, u32[]{:S(2)}, u32[]{:S(2)}) %collective-permute-start.21) | collective-permute-done | bytes 663584 | tf_op jit(solution)/shard_map/ppermute | solution.py:315
  89.0 9.8 %collective-permute-done.22.refs_2_ = bf16[648,256]{1,0:T(8,128)(2,1)S(1)} collective-permute-done((bf16[648,256]{1,0:T(8,128)(2,1)S(1)}, bf16[648,256]{1,0:T(8,128)(2,1)S(1)}, u32[]{:S(2)}, u32[]{:S(2)}) %collective-permute-start.22) | collective-permute-done | bytes 331808 | tf_op jit(solution)/shard_map/ppermute | solution.py:318
  99.1 2.7 %collective-permute-done.17.refs_1_ = bf16[648,512]{1,0:T(8,128)(2,1)S(1)} collective-permute-done((bf16[648,512]{1,0:T(8,128)(2,1)S(1)}, bf16[648,512]{1,0:T(8,128)(2,1)S(1)}, u32[]{:S(2)}, u32[]{:S(2)}) %collective-permute-start.17) | collective-permute-done | bytes 663584 | tf_op jit(solution)/shard_map/ppermute | solution.py:321
  102.6 1.3 collective-permute-start.26
  103.8 6.9 %collective-permute-done.24.refs_1_ = bf16[648,256]{1,0:T(8,128)(2,1)S(1)} collective-permute-done((bf16[648,256]{1,0:T(8,128)(2,1)S(1)}, bf16[648,256]{1,0:T(8,128)(2,1)S(1)}, u32[]{:S(2)}, u32[]{:S(2)}) %collective-permute-start.24) | collective-permute-done | bytes 331808 | tf_op jit(solution)/shard_map/ppermute | solution.py:321
  110.8 1.0 collective-permute-done.23.refs_1_
  112.0 3.3 %collective-permute-done.26.refs_2_ = bf16[648,256]{1,0:T(8,128)(2,1)S(1)} collective-permute-done((bf16[648,256]{1,0:T(8,128)(2,1)S(1)}, bf16[648,256]{1,0:T(8,128)(2,1)S(1)}, u32[]{:S(2)}, u32[]{:S(2)}) %collective-permute-start.26) | collective-permute-done | bytes 331808 | tf_op jit(solution)/shard_map/ppermute | solution.py:318
  116.2 8.2 %collective-permute-done.28.refs_0_ = bf16[648,512]{1,0:T(8,128)(2,1)S(1)} collective-permute-done((bf16[648,512]{1,0:T(8,128)(2,1)S(1)}, bf16[648,512]{1,0:T(8,128)(2,1)S(1)}, u32[]{:S(2)}, u32[]{:S(2)}) %collective-permute-start.28) | collective-permute-done | bytes 663584 | tf_op jit(solution)/shard_map/ppermute | solution.py:328
  124.6 1.8 %collective-permute-start.29 = (bf16[648,256]{1,0:T(8,128)(2,1)S(1)}, bf16[648,256]{1,0:T(8,128)(2,1)S(1)}, u32[]{:S(2)}, u32[]{:S(2)}) collective-permute-start(bf16[648,256]{1,0:T(8,128)(2,1)S(1)} %get-tuple-element.133.refs_0_), channel_id=1, source_target_pairs={{0,6},{1,3},{2,4},{3,1},{4,2},{5,7},{6,0},{7,5},{8,14},{9,11},{10,... | collective-permute-start | bytes 995336 | tf_op jit(solution)/shard_map/ppermute | solution.py:324
  127.1 4.3 %collective-permute-done.29.refs_1_ = bf16[648,256]{1,0:T(8,128)(2,1)S(1)} collective-permute-done((bf16[648,256]{1,0:T(8,128)(2,1)S(1)}, bf16[648,256]{1,0:T(8,128)(2,1)S(1)}, u32[]{:S(2)}, u32[]{:S(2)}) %collective-permute-start.29) | collective-permute-done | bytes 331808 | tf_op jit(solution)/shard_map/ppermute | solution.py:324
  131.5 1.1 collective-permute-start.32
  132.6 2.3 %n2_product2.2 = (f32[648,648]{1,0:T(8,128)S(1)}, f32[8,128]{1,0:T(8,128)S(1)}) custom-call(bf16[648,1024]{1,0:T(8,128)(2,1)S(1)} %get-tuple-element.122.refs_0_, bf16[648,512]{1,0:T(8,128)(2,1)S(1)} %collective-permute-done.5.refs_4_.refs_1_.refs_2_, bf16[648,512]{1,0:T(8,128)(2,1)S(1)} %collective-permute-done.6.refs_6_.refs_2_.refs_3_, ...), custom_call_target="tpu_custom_call" | custom-call | flops 1000 | bytes 1000 | tf_op jit(solution)/shard_map/n2_product2/pallas_call | solution.py:77
  134.9 2.3 %n2_product2.3 = (f32[648,648]{1,0:T(8,128)S(1)}, f32[8,128]{1,0:T(8,128)S(1)}) custom-call(bf16[648,1024]{1,0:T(8,128)(2,1)S(1)} %get-tuple-element.122.refs_0_, bf16[648,512]{1,0:T(8,128)(2,1)S(1)} %get-tuple-element.83.refs_3_.refs_1_.refs_2_, bf16[648,512]{1,0:T(8,128)(2,1)S(1)} %get-tuple-element.87.refs_5_.refs_2_.refs_3_, ...), custom_call_target="tpu_custom_call" | custom-call | flops 1000 | bytes 1000 | tf_op jit(solution)/shard_map/n2_product2/pallas_call | solution.py:77
  137.2 3.6 %collective-permute-done.30.refs_1_ = bf16[648,512]{1,0:T(8,128)(2,1)S(1)} collective-permute-done((bf16[648,512]{1,0:T(8,128)(2,1)S(1)}, bf16[648,512]{1,0:T(8,128)(2,1)S(1)}, u32[]{:S(2)}, u32[]{:S(2)}) %collective-permute-start.30) | collective-permute-done | bytes 663584 | tf_op jit(solution)/shard_map/ppermute | solution.py:331
  142.6 1.2 t0_product2.2
  143.9 1.3 t0_product2.3
  145.2 2.7 %collective-permute-done.32.refs_1_ = bf16[648,512]{1,0:T(8,128)(2,1)S(1)} collective-permute-done((bf16[648,512]{1,0:T(8,128)(2,1)S(1)}, bf16[648,512]{1,0:T(8,128)(2,1)S(1)}, u32[]{:S(2)}, u32[]{:S(2)}) %collective-permute-start.32) | collective-permute-done | bytes 663584 | tf_op jit(solution)/shard_map/ppermute | solution.py:331
  148.7 4.1 %collective-permute-start.33 = (bf16[648,648]{1,0:T(8,128)(2,1)S(1)}, bf16[648,648]{1,0:T(8,128)(2,1)S(1)}, u32[]{:S(2)}, u32[]{:S(2)}) collective-permute-start(bf16[648,648]{1,0:T(8,128)(2,1)S(1)} %get-tuple-element.154), channel_id=1, source_target_pairs={{0,1},{1,0},{2,3},{3,2},{4,5},{5,4},{6,7},{7,6},{8,9},{9,8},{10,11... | collective-permute-start | bytes 2519432 | tf_op jit(solution)/shard_map/ppermute | solution.py:346
  152.9 1.2 t2_product2.3
  154.2 0.8 collective-permute-done.33.refs_2_
  155.0 2.9 %finish.1 = f32[648,1296]{1,0:T(8,128)} custom-call(f32[648,1]{1,0:T(8,128)S(1)} %mul.11.refs_0_, f32[648,648]{1,0:T(8,128)S(1)} %get-tuple-element.153.refs_1_, bf16[648,648]{1,0:T(8,128)(2,1)S(1)} %collective-permute-done.33.refs_2_), custom_call_target="tpu_custom_call" | custom-call | tf_op jit(solution)/shard_map/finish/pallas_call | solution.py:385
  (60 shorter events, 8.9 us)
Async XLA Ops:
  0.0 1.1 copy-start
  1.2 18.2 %collective-permute-start.2 = (bf16[648,512]{1,0:T(8,128)(2,1)S(1)}, bf16[648,512]{1,0:T(8,128)(2,1)S(1)}, u32[]{:S(2)}, u32[]{:S(2)}) collective-permute-start(bf16[648,512]{1,0:T(8,128)(2,1)S(1)} %get-tuple-element.83.refs_3_.refs_1_.refs_2_), channel_id=1, source_target_pairs={{0,64},{16,80},{32,96},{48,112},{64,0},{80,16},{96,32},{112,48},{1... | collective-permute-start | bytes 1990664 | tf_op jit(solution)/shard_map/ppermute | solution.py:133
  5.0 18.1 %collective-permute-start.3 = (bf16[648,512]{1,0:T(8,128)(2,1)S(1)}, bf16[648,512]{1,0:T(8,128)(2,1)S(1)}, u32[]{:S(2)}, u32[]{:S(2)}) collective-permute-start(bf16[648,512]{1,0:T(8,128)(2,1)S(1)} %get-tuple-element.83.refs_3_.refs_1_.refs_2_), channel_id=1, source_target_pairs={{0,16},{16,32},{32,48},{48,0},{64,80},{80,96},{96,112},{112,64},{1... | collective-permute-start | bytes 1990664 | tf_op jit(solution)/shard_map/ppermute | solution.py:131
  6.7 29.7 %collective-permute-start.4 = (bf16[648,512]{1,0:T(8,128)(2,1)S(1)}, bf16[648,512]{1,0:T(8,128)(2,1)S(1)}, u32[]{:S(2)}, u32[]{:S(2)}) collective-permute-start(bf16[648,512]{1,0:T(8,128)(2,1)S(1)} %get-tuple-element.83.refs_3_.refs_1_.refs_2_), channel_id=1, source_target_pairs={{0,48},{16,0},{32,16},{48,32},{64,112},{80,64},{96,80},{112,96},{1... | collective-permute-start | bytes 1990664 | tf_op jit(solution)/shard_map/ppermute | solution.py:132
  8.8 30.0 %collective-permute-start.1 = (bf16[648,512]{1,0:T(8,128)(2,1)}, bf16[648,512]{1,0:T(8,128)(2,1)S(1)}, u32[]{:S(2)}, u32[]{:S(2)}) collective-permute-start(bf16[648,512]{1,0:T(8,128)(2,1)} %param.9), channel_id=1, source_target_pairs={{0,0},{1,1},{2,18},{3,19},{4,36},{5,37},{6,54},{7,55},{8,64},{9,65... | collective-permute-start | bytes 1990664 | tf_op jit(solution)/shard_map/ppermute | solution.py:128
  10.5 0.7 copy-start.1
  13.4 27.3 %collective-permute-start = (bf16[648,648]{1,0:T(8,128)(2,1)S(1)}, bf16[648,648]{1,0:T(8,128)(2,1)S(1)}, u32[]{:S(2)}, u32[]{:S(2)}) collective-permute-start(bf16[648,648]{1,0:T(8,128)(2,1)S(1)} %get-tuple-element.82), channel_id=1, source_target_pairs={{0,1},{1,0},{2,3},{3,2},{4,5},{5,4},{6,7},{7,6},{8,9},{9,8},{10,11... | collective-permute-start | bytes 2519432 | tf_op jit(solution)/shard_map/ppermute | solution.py:167
  19.4 19.8 %collective-permute-start.5 = (bf16[648,512]{1,0:T(8,128)(2,1)S(1)}, bf16[648,512]{1,0:T(8,128)(2,1)S(1)}, u32[]{:S(2)}, u32[]{:S(2)}) collective-permute-start(bf16[648,512]{1,0:T(8,128)(2,1)S(1)} %get-tuple-element.83.refs_3_.refs_1_.refs_2_), channel_id=1, source_target_pairs={{0,1},{1,0},{2,3},{3,2},{4,5},{5,4},{6,7},{7,6},{8,9},{9,8},{10,11... | collective-permute-start | bytes 1990664 | tf_op jit(solution)/shard_map/ppermute | solution.py:130
  36.6 5.9 %collective-permute-start.8 = (bf16[648,512]{1,0:T(8,128)(2,1)S(1)}, bf16[648,512]{1,0:T(8,128)(2,1)S(1)}, u32[]{:S(2)}, u32[]{:S(2)}) collective-permute-start(bf16[648,512]{1,0:T(8,128)(2,1)S(1)} %get-tuple-element.89.refs_9_.refs_4_.refs_5_), channel_id=1, source_target_pairs={{0,1},{1,0},{2,3},{3,2},{4,5},{5,4},{6,7},{7,6},{8,9},{9,8},{10,11... | collective-permute-start | bytes 1990664 | tf_op jit(solution)/shard_map/ppermute | solution.py:353
  38.7 3.8 %collective-permute-start.6 = (bf16[648,512]{1,0:T(8,128)(2,1)S(1)}, bf16[648,512]{1,0:T(8,128)(2,1)S(1)}, u32[]{:S(2)}, u32[]{:S(2)}) collective-permute-start(bf16[648,512]{1,0:T(8,128)(2,1)S(1)} %get-tuple-element.87.refs_5_.refs_2_.refs_3_), channel_id=1, source_target_pairs={{0,1},{1,0},{2,3},{3,2},{4,5},{5,4},{6,7},{7,6},{8,9},{9,8},{10,11... | collective-permute-start | bytes 1990664 | tf_op jit(solution)/shard_map/ppermute | solution.py:353
  38.8 3.7 %collective-permute-start.7 = (bf16[648,512]{1,0:T(8,128)(2,1)S(1)}, bf16[648,512]{1,0:T(8,128)(2,1)S(1)}, u32[]{:S(2)}, u32[]{:S(2)}) collective-permute-start(bf16[648,512]{1,0:T(8,128)(2,1)S(1)} %get-tuple-element.88.refs_7_.refs_3_.refs_4_), channel_id=1, source_target_pairs={{0,1},{1,0},{2,3},{3,2},{4,5},{5,4},{6,7},{7,6},{8,9},{9,8},{10,11... | collective-permute-start | bytes 1990664 | tf_op jit(solution)/shard_map/ppermute | solution.py:353
  39.2 18.4 %collective-permute-start.10 = (bf16[648,512]{1,0:T(8,128)(2,1)S(1)}, bf16[648,512]{1,0:T(8,128)(2,1)S(1)}, u32[]{:S(2)}, u32[]{:S(2)}) collective-permute-start(bf16[648,512]{1,0:T(8,128)(2,1)S(1)} %get-tuple-element.89.refs_9_.refs_4_.refs_5_), channel_id=1, source_target_pairs={{0,16},{16,32},{32,48},{48,0},{64,80},{80,96},{96,112},{112,64},{1... | collective-permute-start | bytes 1990664 | tf_op jit(solution)/shard_map/ppermute | solution.py:354
  40.7 16.9 %collective-permute-start.11 = (bf16[648,512]{1,0:T(8,128)(2,1)S(1)}, bf16[648,512]{1,0:T(8,128)(2,1)S(1)}, u32[]{:S(2)}, u32[]{:S(2)}) collective-permute-start(bf16[648,512]{1,0:T(8,128)(2,1)S(1)} %get-tuple-element.89.refs_9_.refs_4_.refs_5_), channel_id=1, source_target_pairs={{0,48},{16,0},{32,16},{48,32},{64,112},{80,64},{96,80},{112,96},{1... | collective-permute-start | bytes 1990664 | tf_op jit(solution)/shard_map/ppermute | solution.py:355
  46.9 18.4 %collective-permute-start.9 = (bf16[648,1024]{1,0:T(8,128)(2,1)S(1)}, bf16[648,1024]{1,0:T(8,128)(2,1)S(1)}, u32[]{:S(2)}, u32[]{:S(2)}) collective-permute-start(bf16[648,1024]{1,0:T(8,128)(2,1)S(1)} %get-tuple-element.92), channel_id=1, source_target_pairs={{0,2},{1,7},{2,0},{3,5},{4,6},{5,3},{6,4},{7,1},{8,10},{9,15},{10,... | collective-permute-start | bytes 3981320 | tf_op jit(solution)/shard_map/ppermute | solution.py:315
  57.8 3.8 %collective-permute-start.12 = (bf16[648,512]{1,0:T(8,128)(2,1)S(1)}, bf16[648,512]{1,0:T(8,128)(2,1)S(1)}, u32[]{:S(2)}, u32[]{:S(2)}) collective-permute-start(bf16[648,512]{1,0:T(8,128)(2,1)S(1)} %get-tuple-element.95.refs_3_.refs_6_.refs_2_), channel_id=1, source_target_pairs={{0,1},{1,0},{2,3},{3,2},{4,5},{5,4},{6,7},{7,6},{8,9},{9,8},{10,11... | collective-permute-start | bytes 1990664 | tf_op jit(solution)/shard_map/ppermute | solution.py:362
  58.6 3.0 %collective-permute-start.13 = (bf16[648,512]{1,0:T(8,128)(2,1)S(1)}, bf16[648,512]{1,0:T(8,128)(2,1)S(1)}, u32[]{:S(2)}, u32[]{:S(2)}) collective-permute-start(bf16[648,512]{1,0:T(8,128)(2,1)S(1)} %get-tuple-element.96.refs_5_.refs_7_.refs_3_), channel_id=1, source_target_pairs={{0,1},{1,0},{2,3},{3,2},{4,5},{5,4},{6,7},{7,6},{8,9},{9,8},{10,11... | collective-permute-start | bytes 1990664 | tf_op jit(solution)/shard_map/ppermute | solution.py:362
  58.7 10.4 %collective-permute-start.15 = (bf16[648,512]{1,0:T(8,128)(2,1)S(1)}, bf16[648,512]{1,0:T(8,128)(2,1)S(1)}, u32[]{:S(2)}, u32[]{:S(2)}) collective-permute-start(bf16[648,512]{1,0:T(8,128)(2,1)S(1)} %get-tuple-element.100), channel_id=1, source_target_pairs={{0,16},{1,49},{2,18},{3,51},{4,20},{5,53},{6,22},{7,55},{8,24},{9,... | collective-permute-start | bytes 1990664 | tf_op jit(solution)/shard_map/ppermute | solution.py:356
  61.4 14.7 %collective-permute-start.16 = (bf16[648,512]{1,0:T(8,128)(2,1)S(1)}, bf16[648,512]{1,0:T(8,128)(2,1)S(1)}, u32[]{:S(2)}, u32[]{:S(2)}) collective-permute-start(bf16[648,512]{1,0:T(8,128)(2,1)S(1)} %get-tuple-element.101), channel_id=1, source_target_pairs={{0,16},{1,49},{2,18},{3,51},{4,20},{5,53},{6,22},{7,55},{8,24},{9,... | collective-permute-start | bytes 1990664 | tf_op jit(solution)/shard_map/ppermute | solution.py:363
  65.4 15.2 %collective-permute-start.14 = (bf16[648,512]{1,0:T(8,128)(2,1)S(1)}, bf16[648,512]{1,0:T(8,128)(2,1)S(1)}, u32[]{:S(2)}, u32[]{:S(2)}) collective-permute-start(bf16[648,512]{1,0:T(8,128)(2,1)S(1)} %get-tuple-element.99), channel_id=1, source_target_pairs={{0,6},{1,3},{2,4},{3,1},{4,2},{5,7},{6,0},{7,5},{8,14},{9,11},{10,... | collective-permute-start | bytes 1990664 | tf_op jit(solution)/shard_map/ppermute | solution.py:318
  76.2 4.7 %collective-permute-start.18 = (bf16[648,512]{1,0:T(8,128)(2,1)S(1)}, bf16[648,512]{1,0:T(8,128)(2,1)S(1)}, u32[]{:S(2)}, u32[]{:S(2)}) collective-permute-start(bf16[648,512]{1,0:T(8,128)(2,1)S(1)} %get-tuple-element.105.refs_3_.refs_9_.refs_2_), channel_id=1, source_target_pairs={{0,1},{1,0},{2,3},{3,2},{4,5},{5,4},{6,7},{7,6},{8,9},{9,8},{10,11... | collective-permute-start | bytes 1990664 | tf_op jit(solution)/shard_map/ppermute | solution.py:370
  78.1 2.8 %collective-permute-start.19 = (bf16[648,512]{1,0:T(8,128)(2,1)S(1)}, bf16[648,512]{1,0:T(8,128)(2,1)S(1)}, u32[]{:S(2)}, u32[]{:S(2)}) collective-permute-start(bf16[648,512]{1,0:T(8,128)(2,1)S(1)} %get-tuple-element.106.refs_5_.refs_10_.refs_3_), channel_id=1, source_target_pairs={{0,1},{1,0},{2,3},{3,2},{4,5},{5,4},{6,7},{7,6},{8,9},{9,8},{10,11... | collective-permute-start | bytes 1990664 | tf_op jit(solution)/shard_map/ppermute | solution.py:370
  78.1 10.7 %collective-permute-start.21 = (bf16[648,512]{1,0:T(8,128)(2,1)S(1)}, bf16[648,512]{1,0:T(8,128)(2,1)S(1)}, u32[]{:S(2)}, u32[]{:S(2)}) collective-permute-start(bf16[648,512]{1,0:T(8,128)(2,1)S(1)} %get-tuple-element.111), channel_id=1, source_target_pairs={{0,2},{1,7},{2,0},{3,5},{4,6},{5,3},{6,4},{7,1},{8,10},{9,15},{10,... | collective-permute-start | bytes 1990664 | tf_op jit(solution)/shard_map/ppermute | solution.py:315
  83.1 15.9 %collective-permute-start.20 = (bf16[648,512]{1,0:T(8,128)(2,1)S(1)}, bf16[648,512]{1,0:T(8,128)(2,1)S(1)}, u32[]{:S(2)}, u32[]{:S(2)}) collective-permute-start(bf16[648,512]{1,0:T(8,128)(2,1)S(1)} %get-tuple-element.109), channel_id=1, source_target_pairs={{0,2},{1,7},{2,0},{3,5},{4,6},{5,3},{6,4},{7,1},{8,10},{9,15},{10,... | collective-permute-start | bytes 1990664 | tf_op jit(solution)/shard_map/ppermute | solution.py:315
  85.6 16.1 %collective-permute-start.17 = (bf16[648,512]{1,0:T(8,128)(2,1)S(1)}, bf16[648,512]{1,0:T(8,128)(2,1)S(1)}, u32[]{:S(2)}, u32[]{:S(2)}) collective-permute-start(bf16[648,512]{1,0:T(8,128)(2,1)S(1)} %get-tuple-element.104.refs_0_), channel_id=1, source_target_pairs={{0,8},{1,9},{2,10},{3,11},{4,12},{5,13},{6,14},{7,15},{8,0},{9,1},... | collective-permute-start | bytes 1990664 | tf_op jit(solution)/shard_map/ppermute | solution.py:321
  88.9 10.0 %collective-permute-start.22 = (bf16[648,256]{1,0:T(8,128)(2,1)S(1)}, bf16[648,256]{1,0:T(8,128)(2,1)S(1)}, u32[]{:S(2)}, u32[]{:S(2)}) collective-permute-start(bf16[648,256]{1,0:T(8,128)(2,1)S(1)} %get-tuple-element.114), channel_id=1, source_target_pairs={{0,6},{1,3},{2,4},{3,1},{4,2},{5,7},{6,0},{7,5},{8,14},{9,11},{10,... | collective-permute-start | bytes 995336 | tf_op jit(solution)/shard_map/ppermute | solution.py:318
  101.9 9.9 %collective-permute-start.23 = (bf16[648,512]{1,0:T(8,128)(2,1)S(1)}, bf16[648,512]{1,0:T(8,128)(2,1)S(1)}, u32[]{:S(2)}, u32[]{:S(2)}) collective-permute-start(bf16[648,512]{1,0:T(8,128)(2,1)S(1)} %get-tuple-element.118.refs_0_), channel_id=1, source_target_pairs={{0,6},{1,3},{2,4},{3,1},{4,2},{5,7},{6,0},{7,5},{8,14},{9,11},{10,... | collective-permute-start | bytes 1990664 | tf_op jit(solution)/shard_map/ppermute | solution.py:324
  102.6 8.2 %collective-permute-start.24 = (bf16[648,256]{1,0:T(8,128)(2,1)S(1)}, bf16[648,256]{1,0:T(8,128)(2,1)S(1)}, u32[]{:S(2)}, u32[]{:S(2)}) collective-permute-start(bf16[648,256]{1,0:T(8,128)(2,1)S(1)} %get-tuple-element.119.refs_0_), channel_id=1, source_target_pairs={{0,8},{1,9},{2,10},{3,11},{4,12},{5,13},{6,14},{7,15},{8,0},{9,1},... | collective-permute-start | bytes 995336 | tf_op jit(solution)/shard_map/ppermute | solution.py:321
  102.6 12.8 %collective-permute-start.26 = (bf16[648,256]{1,0:T(8,128)(2,1)S(1)}, bf16[648,256]{1,0:T(8,128)(2,1)S(1)}, u32[]{:S(2)}, u32[]{:S(2)}) collective-permute-start(bf16[648,256]{1,0:T(8,128)(2,1)S(1)} %get-tuple-element.125), channel_id=1, source_target_pairs={{0,6},{1,3},{2,4},{3,1},{4,2},{5,7},{6,0},{7,5},{8,14},{9,11},{10,... | collective-permute-start | bytes 995336 | tf_op jit(solution)/shard_map/ppermute | solution.py:318
  111.9 12.5 %collective-permute-start.28 = (bf16[648,512]{1,0:T(8,128)(2,1)S(1)}, bf16[648,512]{1,0:T(8,128)(2,1)S(1)}, u32[]{:S(2)}, u32[]{:S(2)}) collective-permute-start(bf16[648,512]{1,0:T(8,128)(2,1)S(1)} %get-tuple-element.128), channel_id=1, source_target_pairs={{0,2},{1,7},{2,0},{3,5},{4,6},{5,3},{6,4},{7,1},{8,10},{9,15},{10,... | collective-permute-start | bytes 1990664 | tf_op jit(solution)/shard_map/ppermute | solution.py:328
  115.5 9.0 %collective-permute-start.27 = (bf16[648,256]{1,0:T(8,128)(2,1)S(1)}, bf16[648,256]{1,0:T(8,128)(2,1)S(1)}, u32[]{:S(2)}, u32[]{:S(2)}) collective-permute-start(bf16[648,256]{1,0:T(8,128)(2,1)S(1)} %get-tuple-element.127.refs_0_), channel_id=1, source_target_pairs={{0,8},{1,9},{2,10},{3,11},{4,12},{5,13},{6,14},{7,15},{8,0},{9,1},... | collective-permute-start | bytes 995336 | tf_op jit(solution)/shard_map/ppermute | solution.py:321
  115.9 10.4 %collective-permute-start.25 = (bf16[648,256]{1,0:T(8,128)(2,1)S(1)}, bf16[648,256]{1,0:T(8,128)(2,1)S(1)}, u32[]{:S(2)}, u32[]{:S(2)}) collective-permute-start(bf16[648,256]{1,0:T(8,128)(2,1)S(1)} %get-tuple-element.123.refs_0_), channel_id=1, source_target_pairs={{0,6},{1,3},{2,4},{3,1},{4,2},{5,7},{6,0},{7,5},{8,14},{9,11},{10,... | collective-permute-start | bytes 995336 | tf_op jit(solution)/shard_map/ppermute | solution.py:324
  124.6 6.9 %collective-permute-start.29 = (bf16[648,256]{1,0:T(8,128)(2,1)S(1)}, bf16[648,256]{1,0:T(8,128)(2,1)S(1)}, u32[]{:S(2)}, u32[]{:S(2)}) collective-permute-start(bf16[648,256]{1,0:T(8,128)(2,1)S(1)} %get-tuple-element.133.refs_0_), channel_id=1, source_target_pairs={{0,6},{1,3},{2,4},{3,1},{4,2},{5,7},{6,0},{7,5},{8,14},{9,11},{10,... | collective-permute-start | bytes 995336 | tf_op jit(solution)/shard_map/ppermute | solution.py:324
  126.4 14.4 %collective-permute-start.30 = (bf16[648,512]{1,0:T(8,128)(2,1)S(1)}, bf16[648,512]{1,0:T(8,128)(2,1)S(1)}, u32[]{:S(2)}, u32[]{:S(2)}) collective-permute-start(bf16[648,512]{1,0:T(8,128)(2,1)S(1)} %get-tuple-element.132.refs_5_), channel_id=1, source_target_pairs={{0,2},{1,7},{2,0},{3,5},{4,6},{5,3},{6,4},{7,1},{8,10},{9,15},{10,... | collective-permute-start | bytes 1990664 | tf_op jit(solution)/shard_map/ppermute | solution.py:331
  127.0 15.2 %collective-permute-start.31 = (bf16[648,512]{1,0:T(8,128)(2,1)S(1)}, bf16[648,512]{1,0:T(8,128)(2,1)S(1)}, u32[]{:S(2)}, u32[]{:S(2)}) collective-permute-start(bf16[648,512]{1,0:T(8,128)(2,1)S(1)} %get-tuple-element.143.refs_0_), channel_id=1, source_target_pairs={{0,8},{1,9},{2,10},{3,11},{4,12},{5,13},{6,14},{7,15},{8,0},{9,1},... | collective-permute-start | bytes 1990664 | tf_op jit(solution)/shard_map/ppermute | solution.py:334
  131.5 16.4 %collective-permute-start.32 = (bf16[648,512]{1,0:T(8,128)(2,1)S(1)}, bf16[648,512]{1,0:T(8,128)(2,1)S(1)}, u32[]{:S(2)}, u32[]{:S(2)}) collective-permute-start(bf16[648,512]{1,0:T(8,128)(2,1)S(1)} %get-tuple-element.135.refs_8_), channel_id=1, source_target_pairs={{0,2},{1,7},{2,0},{3,5},{4,6},{5,3},{6,4},{7,1},{8,10},{9,15},{10,... | collective-permute-start | bytes 1990664 | tf_op jit(solution)/shard_map/ppermute | solution.py:331
  147.9 4.8 %copy-start.2 = (f32[648]{0:T(1024)S(1)}, f32[648]{0:T(1024)}, u32[]{:S(2)}) copy-start(f32[648]{0:T(1024)} %param.7) | copy-start | bytes 7780
  148.7 6.3 %collective-permute-start.33 = (bf16[648,648]{1,0:T(8,128)(2,1)S(1)}, bf16[648,648]{1,0:T(8,128)(2,1)S(1)}, u32[]{:S(2)}, u32[]{:S(2)}) collective-permute-start(bf16[648,648]{1,0:T(8,128)(2,1)S(1)} %get-tuple-element.154), channel_id=1, source_target_pairs={{0,1},{1,0},{2,3},{3,2},{4,5},{5,4},{6,7},{7,6},{8,9},{9,8},{10,11... | collective-permute-start | bytes 2519432 | tf_op jit(solution)/shard_map/ppermute | solution.py:346
